TPU v7x, 256 devices: a whole 4x4x8 slice. The times are simulated.
256 devices in a mesh: layer: 4 (over z_hi, core), tile: 64 (over x, z_lo, y).
Axes of the slice: x: 4, y: 4, z: 8 (z_hi: 2, z_lo: 4; z = z_hi * 4 + z_lo), core: 2. Of those that a mesh axis runs over, the one named last changes fastest.
Arguments:
- sources: bfloat16 [4, 2, 64, 32768], P('layer', None, None, 'tile'), may hold values from -6 to 6
- down_blocks: bfloat16 [4, 3, 2, 32768, 512], P('layer', None, None, 'tile'), may hold values from -0.109375 to 0.109375
- up_blocks: bfloat16 [4, 3, 2, 32768, 512], P('layer', None, None, 'tile'), may hold values from -0.109375 to 0.109375
Outputs:
- down_trace: bfloat16 [4, 2, 64, 32768], P('layer', None, None, 'tile')
- up_trace: bfloat16 [4, 2, 64, 32768], P('layer', None, None, 'tile')
All inputs are finite; a program needn't handle non-finite values.
Results may differ from a plain program's by a relative error of at most 0.011.
Values may be sent and summed in bfloat16 or wider, within the bound.
No kernel may reach another device: no remote copies, remote signals or barrier semaphores. Data moves between devices by JAX's collectives and lax.ppermute only.
A program may use at most 128 MiB of HBM per device.

v0:
```python
import jax
import jax.numpy as jnp
from jax import lax
from jax.sharding import PartitionSpec as P


def padded(cells, sides, width):
    for axis, dim in sides:
        count = lax.axis_size(axis)
        ends = count - 1
        head = lax.slice_in_dim(cells, 0, width, axis=dim)
        tail = lax.slice_in_dim(cells, cells.shape[dim] - width, cells.shape[dim], axis=dim)
        cells = jnp.concatenate(
            [
                lax.ppermute(tail, axis, [(i, (i + 1) % count) for i in range(ends)]),
                cells,
                lax.ppermute(head, axis, [((i + 1) % count, i) for i in range(ends)]),
            ],
            axis=dim,
        )
    return cells


def passed_along(x, axis, by):
    size = lax.axis_size(axis)
    pairs = [(i, i + by) for i in range(size) if 0 <= i + by < size]
    return lax.ppermute(x, axis, pairs)


def couple_tiles(extended, blocks, tile_cells):
    own_tile = extended[:, :, tile_cells : 2 * tile_cells]
    lower_tile = extended[:, :, :tile_cells]
    upper_tile = extended[:, :, 2 * tile_cells :]
    real_part = jnp.zeros(own_tile.shape[1:], jnp.float32)
    imag_part = jnp.zeros(own_tile.shape[1:], jnp.float32)
    for number, neighbour in enumerate((own_tile, lower_tile, upper_tile)):
        block_real = blocks[number, 0]
        block_imag = blocks[number, 1]
        real_part = (
            real_part
            + jnp.dot(neighbour[0], block_real, preferred_element_type=jnp.float32)
            - jnp.dot(neighbour[1], block_imag, preferred_element_type=jnp.float32)
        )
        imag_part = (
            imag_part
            + jnp.dot(neighbour[0], block_imag, preferred_element_type=jnp.float32)
            + jnp.dot(neighbour[1], block_real, preferred_element_type=jnp.float32)
        )
    return jnp.stack([real_part, imag_part])


def sweep_layers(downward, addend, blocks):
    depth_count = lax.axis_size("layer")
    layer_index = lax.axis_index("layer")
    position = layer_index if downward else depth_count - 1 - layer_index
    panels = 1
    panel_rows = addend.shape[1] // panels
    tile_cells = addend.shape[2]
    arriving = jnp.zeros((2, panel_rows, tile_cells), jnp.bfloat16)
    result = jnp.zeros_like(addend)
    rounds = depth_count + panels - 1
    for round_index in range(rounds):
        panel_index = round_index - position
        active = jnp.logical_and(panel_index >= 0, panel_index < panels)
        if downward:
            extended = padded(arriving, (("tile", 2),), tile_cells)
        else:
            extended = padded(arriving, (("tile", 2),), tile_cells)
        computed = (couple_tiles(extended, blocks, tile_cells) + addend.astype(jnp.float32)).astype(
            jnp.bfloat16
        )
        result = jnp.where(active, computed, result)
        if round_index + 1 < rounds:
            if downward:
                arriving = passed_along(computed, "layer", 1)
            else:
                arriving = passed_along(computed, "layer", -1)
    return result


def per_device(sources, down_blocks, up_blocks):
    falling = sweep_layers(True, sources[0], down_blocks[0])
    rising = sweep_layers(False, falling, up_blocks[0])
    return (falling[None], rising[None])


def solution(mesh):
    return jax.shard_map(
        per_device,
        mesh=mesh,
        in_specs=(
            P("layer", None, None, "tile"),
            P("layer", None, None, "tile", None),
            P("layer", None, None, "tile", None),
        ),
        out_specs=(P("layer", None, None, "tile"), P("layer", None, None, "tile")),
        check_vma=False,
    )
```

profile of v0, /device:TPU:7, one launch (start us, length us, event | category | flops | bytes accessed | tf_op | source)
XLA Modules:
  0.0 186.4 jit_solution(11867359681853344404)
XLA Ops:
  0.6 0.7 broadcast.24
  1.3 3.3 %collective-permute-start = (bf16[2,64,512]{2,1,0:T(8,128)(2,1)}, bf16[2,64,512]{2,1,0:T(8,128)(2,1)S(1)}, u32[]{:S(2)}, u32[]{:S(2)}) collective-permute-start(bf16[2,64,512]{2,1,0:T(8,128)(2,1)} %broadcast.24), channel_id=1, source_target_pairs={{0,1},{1,2},{2,3},{3,4},{4,5},{5,6},{6,7},{7,8},{8,9},{9,10},{10,1... | collective-permute-start | bytes 393224 | tf_op jit(solution)/shard_map/ppermute | solution.py:15
  4.6 7.7 %collective-permute-start.1 = (bf16[2,64,512]{2,1,0:T(8,128)(2,1)}, bf16[2,64,512]{2,1,0:T(8,128)(2,1)S(1)}, u32[]{:S(2)}, u32[]{:S(2)}) collective-permute-start(bf16[2,64,512]{2,1,0:T(8,128)(2,1)} %broadcast.24), channel_id=1, source_target_pairs={{1,0},{2,1},{3,2},{4,3},{5,4},{6,5},{7,6},{8,7},{9,8},{10,9},{11,1... | collective-permute-start | bytes 393224 | tf_op jit(solution)/shard_map/ppermute | solution.py:17
  12.3 1.9 %fusion.72 = f32[64,512]{1,0:T(8,128)} fusion(bf16[3,2,512,512]{3,2,1,0:T(8,128)(2,1)} %bitcast.345), kind=kOutput, calls=%fused_computation.124 | convolution fusion | flops 33554432 | bytes 655360 | tf_op jit(solution)/shard_map/dot_general | solution.py:41
  14.2 1.9 %fusion.76 = f32[64,512]{1,0:T(8,128)} fusion(bf16[3,2,512,512]{3,2,1,0:T(8,128)(2,1)} %bitcast.346), kind=kOutput, calls=%fused_computation.128 | convolution fusion | flops 33554432 | bytes 655360 | tf_op jit(solution)/shard_map/dot_general | solution.py:42
  16.1 1.9 %fusion.80 = f32[64,512]{1,0:T(8,128)} fusion(bf16[3,2,512,512]{3,2,1,0:T(8,128)(2,1)} %bitcast.391), kind=kOutput, calls=%fused_computation.132 | convolution fusion | flops 33554432 | bytes 655360 | tf_op jit(solution)/shard_map/dot_general | solution.py:41
  18.1 1.3 fusion.84
  19.4 1.3 fusion.109
  21.8 0.2 fusion.49
  22.3 9.1 %collective-permute-start.2 = (bf16[2,64,512]{2,1,0:T(8,128)(2,1)S(1)}, bf16[2,64,512]{2,1,0:T(8,128)(2,1)S(1)}, u32[]{:S(2)}, u32[]{:S(2)}) collective-permute-start(bf16[2,64,512]{2,1,0:T(8,128)(2,1)S(1)} %fusion.61), channel_id=1, source_target_pairs={{0,64},{64,128},{128,192},{1,65},{65,129},{129,193},{2,66},{66,130... | collective-permute-start | bytes 393224 | tf_op jit(solution)/shard_map/ppermute | solution.py:27
  32.3 0.2 fusion.25
  32.8 0.6 collective-permute-done.2
  33.6 1.9 %collective-permute-start.3 = (bf16[2,64,512]{2,1,0:T(8,128)(2,1)S(1)}, bf16[2,64,512]{2,1,0:T(8,128)(2,1)S(1)}, u32[]{:S(2)}, u32[]{:S(2)}) collective-permute-start(bf16[2,64,512]{2,1,0:T(8,128)(2,1)S(1)} %collective-permute-done.2), channel_id=1, source_target_pairs={{0,1},{1,2},{2,3},{3,4},{4,5},{5,6},{6,7},{7,8},{8,9},{9,10},{10,1... | collective-permute-start | bytes 393224 | tf_op jit(solution)/shard_map/ppermute | solution.py:15
  35.5 8.2 %collective-permute-start.4 = (bf16[2,64,512]{2,1,0:T(8,128)(2,1)S(1)}, bf16[2,64,512]{2,1,0:T(8,128)(2,1)S(1)}, u32[]{:S(2)}, u32[]{:S(2)}) collective-permute-start(bf16[2,64,512]{2,1,0:T(8,128)(2,1)S(1)} %collective-permute-done.2), channel_id=1, source_target_pairs={{1,0},{2,1},{3,2},{4,3},{5,4},{6,5},{7,6},{8,7},{9,8},{10,9},{11,1... | collective-permute-start | bytes 393224 | tf_op jit(solution)/shard_map/ppermute | solution.py:17
  44.3 1.3 collective-permute-done.4
  47.1 0.2 fusion.40
  47.4 9.4 %collective-permute-start.5 = (bf16[2,64,512]{2,1,0:T(8,128)(2,1)S(1)}, bf16[2,64,512]{2,1,0:T(8,128)(2,1)S(1)}, u32[]{:S(2)}, u32[]{:S(2)}) collective-permute-start(bf16[2,64,512]{2,1,0:T(8,128)(2,1)S(1)} %fusion.62), channel_id=1, source_target_pairs={{0,64},{64,128},{128,192},{1,65},{65,129},{129,193},{2,66},{66,130... | collective-permute-start | bytes 393224 | tf_op jit(solution)/shard_map/ppermute | solution.py:27
  57.0 1.7 collective-permute-done.5
  58.9 8.9 %collective-permute-start.7 = (bf16[2,64,512]{2,1,0:T(8,128)(2,1)S(1)}, bf16[2,64,512]{2,1,0:T(8,128)(2,1)S(1)}, u32[]{:S(2)}, u32[]{:S(2)}) collective-permute-start(bf16[2,64,512]{2,1,0:T(8,128)(2,1)S(1)} %collective-permute-done.5), channel_id=1, source_target_pairs={{1,0},{2,1},{3,2},{4,3},{5,4},{6,5},{7,6},{8,7},{9,8},{10,9},{11,1... | collective-permute-start | bytes 393224 | tf_op jit(solution)/shard_map/ppermute | solution.py:17
  67.8 1.9 %collective-permute-start.6 = (bf16[2,64,512]{2,1,0:T(8,128)(2,1)S(1)}, bf16[2,64,512]{2,1,0:T(8,128)(2,1)S(1)}, u32[]{:S(2)}, u32[]{:S(2)}) collective-permute-start(bf16[2,64,512]{2,1,0:T(8,128)(2,1)S(1)} %collective-permute-done.5), channel_id=1, source_target_pairs={{0,1},{1,2},{2,3},{3,4},{4,5},{5,6},{6,7},{7,8},{8,9},{9,10},{10,1... | collective-permute-start | bytes 393224 | tf_op jit(solution)/shard_map/ppermute | solution.py:15
  71.2 7.1 %collective-permute-done.6 = bf16[2,64,512]{2,1,0:T(8,128)(2,1)S(1)} collective-permute-done((bf16[2,64,512]{2,1,0:T(8,128)(2,1)S(1)}, bf16[2,64,512]{2,1,0:T(8,128)(2,1)S(1)}, u32[]{:S(2)}, u32[]{:S(2)}) %collective-permute-start.6) | collective-permute-done | bytes 131104 | tf_op jit(solution)/shard_map/ppermute | solution.py:15
  79.2 10.7 %collective-permute-start.8 = (bf16[2,64,512]{2,1,0:T(8,128)(2,1)S(1)}, bf16[2,64,512]{2,1,0:T(8,128)(2,1)S(1)}, u32[]{:S(2)}, u32[]{:S(2)}) collective-permute-start(bf16[2,64,512]{2,1,0:T(8,128)(2,1)S(1)} %fusion.63), channel_id=1, source_target_pairs={{0,64},{64,128},{128,192},{1,65},{65,129},{129,193},{2,66},{66,130... | collective-permute-start | bytes 393224 | tf_op jit(solution)/shard_map/ppermute | solution.py:27
  89.9 0.2 fusion.22
  90.2 1.7 collective-permute-done.8
  92.1 1.9 %collective-permute-start.10 = (bf16[2,64,512]{2,1,0:T(8,128)(2,1)S(1)}, bf16[2,64,512]{2,1,0:T(8,128)(2,1)S(1)}, u32[]{:S(2)}, u32[]{:S(2)}) collective-permute-start(bf16[2,64,512]{2,1,0:T(8,128)(2,1)S(1)} %collective-permute-done.8), channel_id=1, source_target_pairs={{1,0},{2,1},{3,2},{4,3},{5,4},{6,5},{7,6},{8,7},{9,8},{10,9},{11,1... | collective-permute-start | bytes 393224 | tf_op jit(solution)/shard_map/ppermute | solution.py:17
  94.0 3.4 %collective-permute-start.9 = (bf16[2,64,512]{2,1,0:T(8,128)(2,1)S(1)}, bf16[2,64,512]{2,1,0:T(8,128)(2,1)S(1)}, u32[]{:S(2)}, u32[]{:S(2)}) collective-permute-start(bf16[2,64,512]{2,1,0:T(8,128)(2,1)S(1)} %collective-permute-done.8), channel_id=1, source_target_pairs={{0,1},{1,2},{2,3},{3,4},{4,5},{5,6},{6,7},{7,8},{8,9},{9,10},{10,1... | collective-permute-start | bytes 393224 | tf_op jit(solution)/shard_map/ppermute | solution.py:15
  98.9 6.2 %collective-permute-done.9 = bf16[2,64,512]{2,1,0:T(8,128)(2,1)S(1)} collective-permute-done((bf16[2,64,512]{2,1,0:T(8,128)(2,1)S(1)}, bf16[2,64,512]{2,1,0:T(8,128)(2,1)S(1)}, u32[]{:S(2)}, u32[]{:S(2)}) %collective-permute-start.9) | collective-permute-done | bytes 131104 | tf_op jit(solution)/shard_map/ppermute | solution.py:15
  106.2 1.9 %collective-permute-start.11 = (bf16[2,64,512]{2,1,0:T(8,128)(2,1)S(1)}, bf16[2,64,512]{2,1,0:T(8,128)(2,1)S(1)}, u32[]{:S(2)}, u32[]{:S(2)}) collective-permute-start(bf16[2,64,512]{2,1,0:T(8,128)(2,1)S(1)} %get-tuple-element.4), channel_id=1, source_target_pairs={{64,0},{128,64},{192,128},{65,1},{129,65},{193,129},{66,2},{130,66... | collective-permute-start | bytes 393224 | tf_op jit(solution)/shard_map/ppermute | solution.py:27
  108.1 9.6 %collective-permute-done.11 = bf16[2,64,512]{2,1,0:T(8,128)(2,1)S(1)} collective-permute-done((bf16[2,64,512]{2,1,0:T(8,128)(2,1)S(1)}, bf16[2,64,512]{2,1,0:T(8,128)(2,1)S(1)}, u32[]{:S(2)}, u32[]{:S(2)}) %collective-permute-start.11) | collective-permute-done | bytes 131104 | tf_op jit(solution)/shard_map/ppermute | solution.py:27
  117.9 1.9 %collective-permute-start.12 = (bf16[2,64,512]{2,1,0:T(8,128)(2,1)S(1)}, bf16[2,64,512]{2,1,0:T(8,128)(2,1)S(1)}, u32[]{:S(2)}, u32[]{:S(2)}) collective-permute-start(bf16[2,64,512]{2,1,0:T(8,128)(2,1)S(1)} %collective-permute-done.11), channel_id=1, source_target_pairs={{0,1},{1,2},{2,3},{3,4},{4,5},{5,6},{6,7},{7,8},{8,9},{9,10},{10,1... | collective-permute-start | bytes 393224 | tf_op jit(solution)/shard_map/ppermute | solution.py:15
  119.8 8.2 %collective-permute-start.13 = (bf16[2,64,512]{2,1,0:T(8,128)(2,1)S(1)}, bf16[2,64,512]{2,1,0:T(8,128)(2,1)S(1)}, u32[]{:S(2)}, u32[]{:S(2)}) collective-permute-start(bf16[2,64,512]{2,1,0:T(8,128)(2,1)S(1)} %collective-permute-done.11), channel_id=1, source_target_pairs={{1,0},{2,1},{3,2},{4,3},{5,4},{6,5},{7,6},{8,7},{9,8},{10,9},{11,1... | collective-permute-start | bytes 393224 | tf_op jit(solution)/shard_map/ppermute | solution.py:17
  128.6 1.3 collective-permute-done.13
  131.7 1.9 %collective-permute-start.14 = (bf16[2,64,512]{2,1,0:T(8,128)(2,1)S(1)}, bf16[2,64,512]{2,1,0:T(8,128)(2,1)S(1)}, u32[]{:S(2)}, u32[]{:S(2)}) collective-permute-start(bf16[2,64,512]{2,1,0:T(8,128)(2,1)S(1)} %fusion.55), channel_id=1, source_target_pairs={{64,0},{128,64},{192,128},{65,1},{129,65},{193,129},{66,2},{130,66... | collective-permute-start | bytes 393224 | tf_op jit(solution)/shard_map/ppermute | solution.py:27
  133.6 8.3 %collective-permute-done.14 = bf16[2,64,512]{2,1,0:T(8,128)(2,1)S(1)} collective-permute-done((bf16[2,64,512]{2,1,0:T(8,128)(2,1)S(1)}, bf16[2,64,512]{2,1,0:T(8,128)(2,1)S(1)}, u32[]{:S(2)}, u32[]{:S(2)}) %collective-permute-start.14) | collective-permute-done | bytes 131104 | tf_op jit(solution)/shard_map/ppermute | solution.py:27
  142.1 1.9 %collective-permute-start.15 = (bf16[2,64,512]{2,1,0:T(8,128)(2,1)S(1)}, bf16[2,64,512]{2,1,0:T(8,128)(2,1)S(1)}, u32[]{:S(2)}, u32[]{:S(2)}) collective-permute-start(bf16[2,64,512]{2,1,0:T(8,128)(2,1)S(1)} %collective-permute-done.14), channel_id=1, source_target_pairs={{0,1},{1,2},{2,3},{3,4},{4,5},{5,6},{6,7},{7,8},{8,9},{9,10},{10,1... | collective-permute-start | bytes 393224 | tf_op jit(solution)/shard_map/ppermute | solution.py:15
  144.0 8.6 %collective-permute-start.16 = (bf16[2,64,512]{2,1,0:T(8,128)(2,1)S(1)}, bf16[2,64,512]{2,1,0:T(8,128)(2,1)S(1)}, u32[]{:S(2)}, u32[]{:S(2)}) collective-permute-start(bf16[2,64,512]{2,1,0:T(8,128)(2,1)S(1)} %collective-permute-done.14), channel_id=1, source_target_pairs={{1,0},{2,1},{3,2},{4,3},{5,4},{6,5},{7,6},{8,7},{9,8},{10,9},{11,1... | collective-permute-start | bytes 393224 | tf_op jit(solution)/shard_map/ppermute | solution.py:17
  153.3 1.3 collective-permute-done.16
  156.3 0.4 copy-done.20
  156.7 0.7 fusion.56
  157.4 1.9 %collective-permute-start.17 = (bf16[2,64,512]{2,1,0:T(8,128)(2,1)}, bf16[2,64,512]{2,1,0:T(8,128)(2,1)}, u32[]{:S(2)}, u32[]{:S(2)}) collective-permute-start(bf16[2,64,512]{2,1,0:T(8,128)(2,1)} %fusion.56), channel_id=1, source_target_pairs={{64,0},{128,64},{192,128},{65,1},{129,65},{193,129},{66,2},{130,66... | collective-permute-start | bytes 393224 | tf_op jit(solution)/shard_map/ppermute | solution.py:27
  159.3 8.6 %collective-permute-done.17 = bf16[2,64,512]{2,1,0:T(8,128)(2,1)} collective-permute-done((bf16[2,64,512]{2,1,0:T(8,128)(2,1)}, bf16[2,64,512]{2,1,0:T(8,128)(2,1)}, u32[]{:S(2)}, u32[]{:S(2)}) %collective-permute-start.17) | collective-permute-done | bytes 131104 | tf_op jit(solution)/shard_map/ppermute | solution.py:27
  167.9 1.0 fusion.81
  169.0 1.9 %collective-permute-start.18 = (bf16[2,64,512]{2,1,0:T(8,128)(2,1)}, bf16[2,64,512]{2,1,0:T(8,128)(2,1)S(1)}, u32[]{:S(2)}, u32[]{:S(2)}) collective-permute-start(bf16[2,64,512]{2,1,0:T(8,128)(2,1)} %collective-permute-done.17), channel_id=1, source_target_pairs={{0,1},{1,2},{2,3},{3,4},{4,5},{5,6},{6,7},{7,8},{8,9},{9,10},{10,1... | collective-permute-start | bytes 393224 | tf_op jit(solution)/shard_map/ppermute | solution.py:15
  170.9 9.5 %collective-permute-start.19 = (bf16[2,64,512]{2,1,0:T(8,128)(2,1)}, bf16[2,64,512]{2,1,0:T(8,128)(2,1)S(1)}, u32[]{:S(2)}, u32[]{:S(2)}) collective-permute-start(bf16[2,64,512]{2,1,0:T(8,128)(2,1)} %collective-permute-done.17), channel_id=1, source_target_pairs={{1,0},{2,1},{3,2},{4,3},{5,4},{6,5},{7,6},{8,7},{9,8},{10,9},{11,1... | collective-permute-start | bytes 393224 | tf_op jit(solution)/shard_map/ppermute | solution.py:17
  180.3 1.0 fusion.77
  181.4 1.0 convolution_subtract_fusion
  182.5 1.0 convolution_add_fusion.1
  185.5 1.0 fusion.93
  (162 shorter events, 16.5 us)
Async XLA Ops:
  0.6 20.0 %copy-start = (bf16[1,3,2,512,512]{4,3,2,1,0:T(8,128)(2,1)S(1)}, bf16[1,3,2,512,512]{4,3,2,1,0:T(8,128)(2,1)}, u32[]{:S(2)}) copy-start(bf16[1,3,2,512,512]{4,3,2,1,0:T(8,128)(2,1)} %param.4) | copy-start | bytes 9437188
  1.3 20.0 %collective-permute-start = (bf16[2,64,512]{2,1,0:T(8,128)(2,1)}, bf16[2,64,512]{2,1,0:T(8,128)(2,1)S(1)}, u32[]{:S(2)}, u32[]{:S(2)}) collective-permute-start(bf16[2,64,512]{2,1,0:T(8,128)(2,1)} %broadcast.24), channel_id=1, source_target_pairs={{0,1},{1,2},{2,3},{3,4},{4,5},{5,6},{6,7},{7,8},{8,9},{9,10},{10,1... | collective-permute-start | bytes 393224 | tf_op jit(solution)/shard_map/ppermute | solution.py:15
  4.6 14.7 %collective-permute-start.1 = (bf16[2,64,512]{2,1,0:T(8,128)(2,1)}, bf16[2,64,512]{2,1,0:T(8,128)(2,1)S(1)}, u32[]{:S(2)}, u32[]{:S(2)}) collective-permute-start(bf16[2,64,512]{2,1,0:T(8,128)(2,1)} %broadcast.24), channel_id=1, source_target_pairs={{1,0},{2,1},{3,2},{4,3},{5,4},{6,5},{7,6},{8,7},{9,8},{10,9},{11,1... | collective-permute-start | bytes 393224 | tf_op jit(solution)/shard_map/ppermute | solution.py:17
  18.0 3.7 %copy-start.33 = (f32[64,512]{1,0:T(8,128)S(1)}, f32[64,512]{1,0:T(8,128)}, u32[]{:S(2)}) copy-start(f32[64,512]{1,0:T(8,128)} %fusion.72) | copy-start | bytes 393220
  18.0 3.7 %copy-start.34 = (f32[64,512]{1,0:T(8,128)S(1)}, f32[64,512]{1,0:T(8,128)}, u32[]{:S(2)}) copy-start(f32[64,512]{1,0:T(8,128)} %fusion.76) | copy-start | bytes 393220
  19.4 13.2 %copy-start.12 = (bf16[2,64,512]{2,1,0:T(8,128)(2,1)}, bf16[2,64,512]{2,1,0:T(8,128)(2,1)S(1)}, u32[]{:S(2)}) copy-start(bf16[2,64,512]{2,1,0:T(8,128)(2,1)S(1)} %collective-permute-done.1) | copy-start | bytes 393220
  20.9 10.6 %copy-start.1 = (bf16[1,3,2,512,512]{4,3,2,1,0:T(8,128)(2,1)S(1)}, bf16[1,3,2,512,512]{4,3,2,1,0:T(8,128)(2,1)}, u32[]{:S(2)}) copy-start(bf16[1,3,2,512,512]{4,3,2,1,0:T(8,128)(2,1)} %param.5) | copy-start | bytes 9437188
  21.3 11.0 %copy-start.14 = (bf16[2,64,512]{2,1,0:T(8,128)(2,1)}, bf16[2,64,512]{2,1,0:T(8,128)(2,1)S(1)}, u32[]{:S(2)}) copy-start(bf16[2,64,512]{2,1,0:T(8,128)(2,1)S(1)} %collective-permute-done) | copy-start | bytes 393220
  21.8 10.5 %copy-start.32 = (f32[64,512]{1,0:T(8,128)S(1)}, f32[64,512]{1,0:T(8,128)}, u32[]{:S(2)}) copy-start(f32[64,512]{1,0:T(8,128)} %fusion.80) | copy-start | bytes 393220
  22.0 83.9 %copy-start.8 = (f32[64,512]{1,0:T(8,128)}, f32[64,512]{1,0:T(8,128)S(1)}, u32[]{:S(2)}) copy-start(f32[64,512]{1,0:T(8,128)S(1)} %fusion.49) | copy-start | bytes 393220
  22.2 83.7 %copy-start.10 = (f32[64,512]{1,0:T(8,128)}, f32[64,512]{1,0:T(8,128)S(1)}, u32[]{:S(2)}) copy-start(f32[64,512]{1,0:T(8,128)S(1)} %fusion.46) | copy-start | bytes 393220
  22.3 11.1 %collective-permute-start.2 = (bf16[2,64,512]{2,1,0:T(8,128)(2,1)S(1)}, bf16[2,64,512]{2,1,0:T(8,128)(2,1)S(1)}, u32[]{:S(2)}, u32[]{:S(2)}) collective-permute-start(bf16[2,64,512]{2,1,0:T(8,128)(2,1)S(1)} %fusion.61), channel_id=1, source_target_pairs={{0,64},{64,128},{128,192},{1,65},{65,129},{129,193},{2,66},{66,130... | collective-permute-start | bytes 393224 | tf_op jit(solution)/shard_map/ppermute | solution.py:27
  32.5 73.4 %copy-start.28 = (f32[64,512]{1,0:T(8,128)}, f32[64,512]{1,0:T(8,128)S(1)}, u32[]{:S(2)}) copy-start(f32[64,512]{1,0:T(8,128)S(1)} %fusion.25) | copy-start | bytes 393220
  33.6 12.9 %collective-permute-start.3 = (bf16[2,64,512]{2,1,0:T(8,128)(2,1)S(1)}, bf16[2,64,512]{2,1,0:T(8,128)(2,1)S(1)}, u32[]{:S(2)}, u32[]{:S(2)}) collective-permute-start(bf16[2,64,512]{2,1,0:T(8,128)(2,1)S(1)} %collective-permute-done.2), channel_id=1, source_target_pairs={{0,1},{1,2},{2,3},{3,4},{4,5},{5,6},{6,7},{7,8},{8,9},{9,10},{10,1... | collective-permute-start | bytes 393224 | tf_op jit(solution)/shard_map/ppermute | solution.py:15
  35.5 10.1 %collective-permute-start.4 = (bf16[2,64,512]{2,1,0:T(8,128)(2,1)S(1)}, bf16[2,64,512]{2,1,0:T(8,128)(2,1)S(1)}, u32[]{:S(2)}, u32[]{:S(2)}) collective-permute-start(bf16[2,64,512]{2,1,0:T(8,128)(2,1)S(1)} %collective-permute-done.2), channel_id=1, source_target_pairs={{1,0},{2,1},{3,2},{4,3},{5,4},{6,5},{7,6},{8,7},{9,8},{10,9},{11,1... | collective-permute-start | bytes 393224 | tf_op jit(solution)/shard_map/ppermute | solution.py:17
  45.8 10.9 %copy-start.13 = (bf16[2,64,512]{2,1,0:T(8,128)(2,1)S(1)}, bf16[2,64,512]{2,1,0:T(8,128)(2,1)}, u32[]{:S(2)}) copy-start(bf16[2,64,512]{2,1,0:T(8,128)(2,1)} %copy-done.12) | copy-start | bytes 393220
  47.4 11.3 %collective-permute-start.5 = (bf16[2,64,512]{2,1,0:T(8,128)(2,1)S(1)}, bf16[2,64,512]{2,1,0:T(8,128)(2,1)S(1)}, u32[]{:S(2)}, u32[]{:S(2)}) collective-permute-start(bf16[2,64,512]{2,1,0:T(8,128)(2,1)S(1)} %fusion.62), channel_id=1, source_target_pairs={{0,64},{64,128},{128,192},{1,65},{65,129},{129,193},{2,66},{66,130... | collective-permute-start | bytes 393224 | tf_op jit(solution)/shard_map/ppermute | solution.py:27
  58.9 11.5 %collective-permute-start.7 = (bf16[2,64,512]{2,1,0:T(8,128)(2,1)S(1)}, bf16[2,64,512]{2,1,0:T(8,128)(2,1)S(1)}, u32[]{:S(2)}, u32[]{:S(2)}) collective-permute-start(bf16[2,64,512]{2,1,0:T(8,128)(2,1)S(1)} %collective-permute-done.5), channel_id=1, source_target_pairs={{1,0},{2,1},{3,2},{4,3},{5,4},{6,5},{7,6},{8,7},{9,8},{10,9},{11,1... | collective-permute-start | bytes 393224 | tf_op jit(solution)/shard_map/ppermute | solution.py:17
  67.8 10.5 %collective-permute-start.6 = (bf16[2,64,512]{2,1,0:T(8,128)(2,1)S(1)}, bf16[2,64,512]{2,1,0:T(8,128)(2,1)S(1)}, u32[]{:S(2)}, u32[]{:S(2)}) collective-permute-start(bf16[2,64,512]{2,1,0:T(8,128)(2,1)S(1)} %collective-permute-done.5), channel_id=1, source_target_pairs={{0,1},{1,2},{2,3},{3,4},{4,5},{5,6},{6,7},{7,8},{8,9},{9,10},{10,1... | collective-permute-start | bytes 393224 | tf_op jit(solution)/shard_map/ppermute | solution.py:15
  70.6 19.4 %copy-start.15 = (bf16[2,64,512]{2,1,0:T(8,128)(2,1)S(1)}, bf16[2,64,512]{2,1,0:T(8,128)(2,1)}, u32[]{:S(2)}) copy-start(bf16[2,64,512]{2,1,0:T(8,128)(2,1)} %copy-done.14) | copy-start | bytes 393220
  78.9 27.0 %copy-start.4 = (f32[64,512]{1,0:T(8,128)}, f32[64,512]{1,0:T(8,128)S(1)}, u32[]{:S(2)}) copy-start(f32[64,512]{1,0:T(8,128)S(1)} %fusion.37) | copy-start | bytes 393220
  79.2 26.8 %copy-start.6 = (f32[64,512]{1,0:T(8,128)}, f32[64,512]{1,0:T(8,128)S(1)}, u32[]{:S(2)}) copy-start(f32[64,512]{1,0:T(8,128)S(1)} %fusion.34) | copy-start | bytes 393220
  79.2 12.6 %collective-permute-start.8 = (bf16[2,64,512]{2,1,0:T(8,128)(2,1)S(1)}, bf16[2,64,512]{2,1,0:T(8,128)(2,1)S(1)}, u32[]{:S(2)}, u32[]{:S(2)}) collective-permute-start(bf16[2,64,512]{2,1,0:T(8,128)(2,1)S(1)} %fusion.63), channel_id=1, source_target_pairs={{0,64},{64,128},{128,192},{1,65},{65,129},{129,193},{2,66},{66,130... | collective-permute-start | bytes 393224 | tf_op jit(solution)/shard_map/ppermute | solution.py:27
  90.2 15.8 %copy-start.30 = (f32[64,512]{1,0:T(8,128)}, f32[64,512]{1,0:T(8,128)S(1)}, u32[]{:S(2)}) copy-start(f32[64,512]{1,0:T(8,128)S(1)} %fusion.22) | copy-start | bytes 393220
  92.1 5.9 %collective-permute-start.10 = (bf16[2,64,512]{2,1,0:T(8,128)(2,1)S(1)}, bf16[2,64,512]{2,1,0:T(8,128)(2,1)S(1)}, u32[]{:S(2)}, u32[]{:S(2)}) collective-permute-start(bf16[2,64,512]{2,1,0:T(8,128)(2,1)S(1)} %collective-permute-done.8), channel_id=1, source_target_pairs={{1,0},{2,1},{3,2},{4,3},{5,4},{6,5},{7,6},{8,7},{9,8},{10,9},{11,1... | collective-permute-start | bytes 393224 | tf_op jit(solution)/shard_map/ppermute | solution.py:17
  94.0 11.0 %collective-permute-start.9 = (bf16[2,64,512]{2,1,0:T(8,128)(2,1)S(1)}, bf16[2,64,512]{2,1,0:T(8,128)(2,1)S(1)}, u32[]{:S(2)}, u32[]{:S(2)}) collective-permute-start(bf16[2,64,512]{2,1,0:T(8,128)(2,1)S(1)} %collective-permute-done.8), channel_id=1, source_target_pairs={{0,1},{1,2},{2,3},{3,4},{4,5},{5,6},{6,7},{7,8},{8,9},{9,10},{10,1... | collective-permute-start | bytes 393224 | tf_op jit(solution)/shard_map/ppermute | solution.py:15
  105.7 24.5 %copy-start.24 = (f32[64,512]{1,0:T(8,128)}, f32[64,512]{1,0:T(8,128)S(1)}, u32[]{:S(2)}) copy-start(f32[64,512]{1,0:T(8,128)S(1)} %fusion.31) | copy-start | bytes 393220
  105.9 24.4 %copy-start.26 = (f32[64,512]{1,0:T(8,128)}, f32[64,512]{1,0:T(8,128)S(1)}, u32[]{:S(2)}) copy-start(f32[64,512]{1,0:T(8,128)S(1)} %fusion.28) | copy-start | bytes 393220
  106.2 11.5 %collective-permute-start.11 = (bf16[2,64,512]{2,1,0:T(8,128)(2,1)S(1)}, bf16[2,64,512]{2,1,0:T(8,128)(2,1)S(1)}, u32[]{:S(2)}, u32[]{:S(2)}) collective-permute-start(bf16[2,64,512]{2,1,0:T(8,128)(2,1)S(1)} %get-tuple-element.4), channel_id=1, source_target_pairs={{64,0},{128,64},{192,128},{65,1},{129,65},{193,129},{66,2},{130,66... | collective-permute-start | bytes 393224 | tf_op jit(solution)/shard_map/ppermute | solution.py:27
  117.9 12.5 %collective-permute-start.12 = (bf16[2,64,512]{2,1,0:T(8,128)(2,1)S(1)}, bf16[2,64,512]{2,1,0:T(8,128)(2,1)S(1)}, u32[]{:S(2)}, u32[]{:S(2)}) collective-permute-start(bf16[2,64,512]{2,1,0:T(8,128)(2,1)S(1)} %collective-permute-done.11), channel_id=1, source_target_pairs={{0,1},{1,2},{2,3},{3,4},{4,5},{5,6},{6,7},{7,8},{8,9},{9,10},{10,1... | collective-permute-start | bytes 393224 | tf_op jit(solution)/shard_map/ppermute | solution.py:15
  119.8 10.1 %collective-permute-start.13 = (bf16[2,64,512]{2,1,0:T(8,128)(2,1)S(1)}, bf16[2,64,512]{2,1,0:T(8,128)(2,1)S(1)}, u32[]{:S(2)}, u32[]{:S(2)}) collective-permute-start(bf16[2,64,512]{2,1,0:T(8,128)(2,1)S(1)} %collective-permute-done.11), channel_id=1, source_target_pairs={{1,0},{2,1},{3,2},{4,3},{5,4},{6,5},{7,6},{8,7},{9,8},{10,9},{11,1... | collective-permute-start | bytes 393224 | tf_op jit(solution)/shard_map/ppermute | solution.py:17
  131.4 23.5 %copy-start.16 = (f32[64,512]{1,0:T(8,128)}, f32[64,512]{1,0:T(8,128)S(1)}, u32[]{:S(2)}) copy-start(f32[64,512]{1,0:T(8,128)S(1)} %fusion.19) | copy-start | bytes 393220
  131.7 23.8 %copy-start.18 = (f32[64,512]{1,0:T(8,128)}, f32[64,512]{1,0:T(8,128)S(1)}, u32[]{:S(2)}) copy-start(f32[64,512]{1,0:T(8,128)S(1)} %fusion.16) | copy-start | bytes 393220
  131.7 10.2 %collective-permute-start.14 = (bf16[2,64,512]{2,1,0:T(8,128)(2,1)S(1)}, bf16[2,64,512]{2,1,0:T(8,128)(2,1)S(1)}, u32[]{:S(2)}, u32[]{:S(2)}) collective-permute-start(bf16[2,64,512]{2,1,0:T(8,128)(2,1)S(1)} %fusion.55), channel_id=1, source_target_pairs={{64,0},{128,64},{192,128},{65,1},{129,65},{193,129},{66,2},{130,66... | collective-permute-start | bytes 393224 | tf_op jit(solution)/shard_map/ppermute | solution.py:27
  142.1 12.9 %collective-permute-start.15 = (bf16[2,64,512]{2,1,0:T(8,128)(2,1)S(1)}, bf16[2,64,512]{2,1,0:T(8,128)(2,1)S(1)}, u32[]{:S(2)}, u32[]{:S(2)}) collective-permute-start(bf16[2,64,512]{2,1,0:T(8,128)(2,1)S(1)} %collective-permute-done.14), channel_id=1, source_target_pairs={{0,1},{1,2},{2,3},{3,4},{4,5},{5,6},{6,7},{7,8},{8,9},{9,10},{10,1... | collective-permute-start | bytes 393224 | tf_op jit(solution)/shard_map/ppermute | solution.py:15
  144.0 10.5 %collective-permute-start.16 = (bf16[2,64,512]{2,1,0:T(8,128)(2,1)S(1)}, bf16[2,64,512]{2,1,0:T(8,128)(2,1)S(1)}, u32[]{:S(2)}, u32[]{:S(2)}) collective-permute-start(bf16[2,64,512]{2,1,0:T(8,128)(2,1)S(1)} %collective-permute-done.14), channel_id=1, source_target_pairs={{1,0},{2,1},{3,2},{4,3},{5,4},{6,5},{7,6},{8,7},{9,8},{10,9},{11,1... | collective-permute-start | bytes 393224 | tf_op jit(solution)/shard_map/ppermute | solution.py:17
  155.0 12.9 %copy-start.2 = (bf16[1,3,2,512,512]{4,3,2,1,0:T(8,128)(2,1)S(1)}, bf16[1,3,2,512,512]{4,3,2,1,0:T(8,128)(2,1)}, u32[]{:S(2)}) copy-start(bf16[1,3,2,512,512]{4,3,2,1,0:T(8,128)(2,1)} %param.5) | copy-start | bytes 9437188
  157.4 10.5 %collective-permute-start.17 = (bf16[2,64,512]{2,1,0:T(8,128)(2,1)}, bf16[2,64,512]{2,1,0:T(8,128)(2,1)}, u32[]{:S(2)}, u32[]{:S(2)}) collective-permute-start(bf16[2,64,512]{2,1,0:T(8,128)(2,1)} %fusion.56), channel_id=1, source_target_pairs={{64,0},{128,64},{192,128},{65,1},{129,65},{193,129},{66,2},{130,66... | collective-permute-start | bytes 393224 | tf_op jit(solution)/shard_map/ppermute | solution.py:27
  169.0 15.1 %collective-permute-start.18 = (bf16[2,64,512]{2,1,0:T(8,128)(2,1)}, bf16[2,64,512]{2,1,0:T(8,128)(2,1)S(1)}, u32[]{:S(2)}, u32[]{:S(2)}) collective-permute-start(bf16[2,64,512]{2,1,0:T(8,128)(2,1)} %collective-permute-done.17), channel_id=1, source_target_pairs={{0,1},{1,2},{2,3},{3,4},{4,5},{5,6},{6,7},{7,8},{8,9},{9,10},{10,1... | collective-permute-start | bytes 393224 | tf_op jit(solution)/shard_map/ppermute | solution.py:15
  170.9 12.6 %collective-permute-start.19 = (bf16[2,64,512]{2,1,0:T(8,128)(2,1)}, bf16[2,64,512]{2,1,0:T(8,128)(2,1)S(1)}, u32[]{:S(2)}, u32[]{:S(2)}) collective-permute-start(bf16[2,64,512]{2,1,0:T(8,128)(2,1)} %collective-permute-done.17), channel_id=1, source_target_pairs={{1,0},{2,1},{3,2},{4,3},{5,4},{6,5},{7,6},{8,7},{9,8},{10,9},{11,1... | collective-permute-start | bytes 393224 | tf_op jit(solution)/shard_map/ppermute | solution.py:17
  183.7 1.6 copy-start.5
  183.7 1.6 copy-start.7
  183.7 1.6 copy-start.9
  183.8 1.6 copy-start.11
  183.8 1.6 copy-start.17
  183.8 1.6 copy-start.19
  183.8 1.6 copy-start.21
  183.8 1.6 copy-start.23
  (7 other events, 9.8 us)
where the time goes:
time: 187 us; the launch traced here: 186 us
  starting transfers between devices  104 us (56%)
  waiting for transfers between devices  47.6 us (25%)
  matrix products  29.4 us (16%)
  between operations  2.13 us (1%)
  other arithmetic  1.94 us (1%)
    ppermute x7, starting transfers between devices, padded(): lax.ppermute(head, axis, [((i + 1) % count, i) for i in range(ends)])  52.9 us
    ppermute x6, starting transfers between devices, passed_along(): return lax.ppermute(x, axis, pairs)  35 us
    ppermute x6, waiting for transfers between devices, passed_along(): return lax.ppermute(x, axis, pairs)  30.4 us
    ppermute x7, starting transfers between devices, padded(): lax.ppermute(tail, axis, [(i, (i + 1) % count) for i in range(ends)])  16.3 us
    ppermute x7, waiting for transfers between devices, padded(): lax.ppermute(tail, axis, [(i, (i + 1) % count) for i in range(ends)])  13.3 us
    dot_general x24, matrix products, couple_tiles(): jnp.dot(neighbour[0], block_real, preferred_element_type=jnp.float32)  10.3 us
    dot_general x24, matrix products, couple_tiles(): jnp.dot(neighbour[1], block_imag, preferred_element_type=jnp.float32)  8.41 us
    dot_general x22, matrix products, couple_tiles(): jnp.dot(neighbour[0], block_imag, preferred_element_type=jnp.float32)  5.39 us
  transfers between devices with their start and end apart: 20, of which 11 were waited for; matrix products, arithmetic and copies ran while one was open for 11% of the time, Pallas kernels for 0%

commit v1 on v0

v1 whole, which is shorter than its diff:
```python
import functools

import jax
import jax.numpy as jnp
from jax import lax
from jax.experimental import pallas as pl
from jax.experimental.pallas import tpu as pltpu
from jax.sharding import PartitionSpec as P

AXES = ("layer", "tile")
VMEM_LIMIT = 32 * 1024 * 1024


def far_mate(tile, tiles):
    return (tile + 1) % tiles if tile % 2 else (tile - 1) % tiles


def near_mate(tile, tiles):
    return tile - 1 if tile % 2 else tile + 1


def same(tile, tiles):
    return tile


def hop_pairs(route, mate, tiles):
    pairs = []
    for number, (source, target) in enumerate(route):
        for tile in range(tiles):
            there = mate(tile, tiles) if number == 0 else tile
            pairs.append((source * tiles + tile, target * tiles + there))
    return pairs


def step_kernel(own_ref, near_ref, far_ref, blocks_ref, addend_ref, out_ref):
    tiles = lax.axis_size("tile")
    tile = lax.axis_index("tile")
    odd = lax.rem(tile, 2)
    rows, cells = own_ref.shape[1:]
    edge = jnp.logical_or(tile == 0, tile == tiles - 1)

    def product(values, number):
        by_real = jnp.dot(values, blocks_ref[number, 0], preferred_element_type=jnp.float32)
        by_imag = jnp.dot(values, blocks_ref[number, 1], preferred_element_type=jnp.float32)
        return by_real, by_imag

    def stacked(ref):
        return ref[...].reshape(2 * rows, cells)

    far = stacked(far_ref)
    far = jnp.where(edge, jnp.zeros_like(far), far)
    own_real, own_imag = product(stacked(own_ref), 0)
    near_real, near_imag = product(stacked(near_ref), 2 - odd)
    far_real, far_imag = product(far, 1 + odd)
    by_real = own_real + near_real + far_real
    by_imag = own_imag + near_imag + far_imag
    out_ref[0] = (by_real[:rows] - by_imag[rows:] + addend_ref[0].astype(jnp.float32)).astype(out_ref.dtype)
    out_ref[1] = (by_imag[:rows] + by_real[rows:] + addend_ref[1].astype(jnp.float32)).astype(out_ref.dtype)


def step(own, near, far, blocks, addend):
    vmem = pl.BlockSpec(memory_space=pltpu.VMEM)
    return pl.pallas_call(
        step_kernel,
        out_shape=jax.ShapeDtypeStruct(own.shape, own.dtype),
        in_specs=[vmem] * 5,
        out_specs=vmem,
        compiler_params=pltpu.CompilerParams(vmem_limit_bytes=VMEM_LIMIT),
        cost_estimate=pl.CostEstimate(
            flops=24 * own.shape[1] * own.shape[2] * own.shape[2],
            bytes_accessed=blocks.size * 2 + own.size * 10,
            transcendentals=0,
        ),
    )(own, near, far, blocks, addend)


ROUTES = {
    (0, 1): ((0, 1), (1, 0), (2, 3), (3, 2)),
    (1, 0): ((1, 0), (0, 1), (2, 3), (3, 2)),
    (1, 2): ((1, 2), (2, 3), (3, 0), (0, 1)),
    (2, 1): ((2, 1), (1, 0), (0, 3), (3, 2)),
    (2, 3): ((2, 3), (3, 2), (0, 1), (1, 0)),
    (3, 2): ((3, 2), (2, 3), (0, 1), (1, 0)),
}


def hop(values, source, target, blocks, addend):
    tiles = lax.axis_size("tile")
    route = ROUTES[source, target]
    far = lax.ppermute(values, AXES, hop_pairs(route, far_mate, tiles))
    near = lax.ppermute(values, AXES, hop_pairs(route, near_mate, tiles))
    own = lax.ppermute(values, AXES, hop_pairs(route, same, tiles))
    return step(own, near, far, blocks, addend)


def per_device(sources, down_blocks, up_blocks):
    layer = lax.axis_index("layer")
    source = sources[0]
    down = pltpu.with_memory_space_constraint(down_blocks[0], pltpu.VMEM)
    up = pltpu.with_memory_space_constraint(up_blocks[0], pltpu.VMEM)
    values = source
    falling = source
    for index in range(1, 4):
        values = hop(values, index - 1, index, down, source)
        falling = jnp.where(layer == index, values, falling)
    rising = falling
    for index in (2, 1, 0):
        values = hop(values, index + 1, index, up, falling)
        rising = jnp.where(layer == index, values, rising)
    return (falling[None], rising[None])


def solution(mesh):
    return jax.shard_map(
        per_device,
        mesh=mesh,
        in_specs=(
            P("layer", None, None, "tile"),
            P("layer", None, None, "tile", None),
            P("layer", None, None, "tile", None),
        ),
        out_specs=(P("layer", None, None, "tile"), P("layer", None, None, "tile")),
        check_vma=False,
    )
```

time: 187 us -> 69 us (0.37)
  the two profiles are of different devices: /device:TPU:7 before, /device:TPU:6 now
where the time goes in v1:
time: 69 us; the launch traced here: 68.7 us
  waiting for transfers between devices  35.5 us (51%)
  starting transfers between devices  21.3 us (31%)
  Pallas kernels  6.12 us (9%)
  local copies, waits for them, and re-layouts  4.35 us (6%)
  between operations  0.73 us (1%)
  other arithmetic  0.72 us (1%)
    ppermute x6, waiting for transfers between devices, hop(): far = lax.ppermute(values, AXES, hop_pairs(route, far_mate, tiles))  24 us
    ppermute x6, starting transfers between devices, hop(): far = lax.ppermute(values, AXES, hop_pairs(route, far_mate, tiles))  14.8 us
    pallas_call x6, Pallas kernels, step(): pl.pallas_call(step_kernel, out_shape=jax.ShapeDtypeStruct(own.shape, own...  6.12 us
    ppermute x6, waiting for transfers between devices, hop(): own = lax.ppermute(values, AXES, hop_pairs(route, same, tiles))  5.76 us
    ppermute x6, waiting for transfers between devices, hop(): near = lax.ppermute(values, AXES, hop_pairs(route, near_mate, tiles))  5.64 us
    ppermute x6, starting transfers between devices, hop(): near = lax.ppermute(values, AXES, hop_pairs(route, near_mate, tiles))  5.59 us
    unnamed x18, local copies, waits for them, and re-layouts  4.35 us
  transfers between devices with their start and end apart: 18, of which 14 were waited for; matrix products, arithmetic and copies ran while one was open for 0% of the time, Pallas kernels for 0%

profile of v1, /device:TPU:6, one launch (start us, length us, event | category | flops | bytes accessed | tf_op | source)
XLA Modules:
  0.0 68.7 jit_solution(4788756217146842017)
XLA Ops:
  0.6 6.9 %collective-permute-start.2 = (bf16[2,64,512]{2,1,0:T(8,128)(2,1)}, bf16[2,64,512]{2,1,0:T(8,128)(2,1)S(1)}, u32[]{:S(2)}, u32[]{:S(2)}) collective-permute-start(bf16[2,64,512]{2,1,0:T(8,128)(2,1)} %bitcast.14), channel_id=1, source_target_pairs={{0,127},{1,66},{2,65},{3,68},{4,67},{5,70},{6,69},{7,72},{8,71},{9... | collective-permute-start | bytes 393224 | tf_op jit(solution)/shard_map/ppermute | solution.py:90
  7.5 0.0 collective-permute-start.1
  7.5 0.5 collective-permute-start
  8.0 2.3 %collective-permute-done.2.far_ref = bf16[2,64,512]{2,1,0:T(8,128)(2,1)S(1)} collective-permute-done((bf16[2,64,512]{2,1,0:T(8,128)(2,1)}, bf16[2,64,512]{2,1,0:T(8,128)(2,1)S(1)}, u32[]{:S(2)}, u32[]{:S(2)}) %collective-permute-start.2) | collective-permute-done | bytes 131104 | tf_op jit(solution)/shard_map/ppermute | solution.py:90
  10.3 0.0 collective-permute-done.1.near_ref
  10.4 0.0 collective-permute-done.own_ref
  10.4 1.9 %copy-done = bf16[1,3,2,512,512]{4,3,2,1,0:T(8,128)(2,1)S(1)} copy-done((bf16[1,3,2,512,512]{4,3,2,1,0:T(8,128)(2,1)S(1)}, bf16[1,3,2,512,512]{4,3,2,1,0:T(8,128)(2,1)}, u32[]{:S(2)}) %copy-start) | copy-done | bytes 3145752
  12.3 0.9 %copy-done.5 = bf16[1,2,64,512]{3,2,1,0:T(8,128)(2,1)S(1)} copy-done((bf16[1,2,64,512]{3,2,1,0:T(8,128)(2,1)S(1)}, bf16[1,2,64,512]{3,2,1,0:T(8,128)(2,1)}, u32[]{:S(2)}) %copy-start.5) | copy-done | bytes 131096
  13.2 0.6 shard_map.50
  13.8 0.7 %collective-permute-start.5 = (bf16[2,64,512]{2,1,0:T(8,128)(2,1)S(1)}, bf16[2,64,512]{2,1,0:T(8,128)(2,1)S(1)}, u32[]{:S(2)}, u32[]{:S(2)}) collective-permute-start(bf16[2,64,512]{2,1,0:T(8,128)(2,1)S(1)} %shard_map.50), channel_id=1, source_target_pairs={{64,191},{65,130},{66,129},{67,132},{68,131},{69,134},{70,133},{71... | collective-permute-start | bytes 393224 | tf_op jit(solution)/shard_map/ppermute | solution.py:90
  14.5 0.4 collective-permute-start.4
  14.9 0.0 collective-permute-start.3
  14.9 10.6 %collective-permute-done.5.far_ref = bf16[2,64,512]{2,1,0:T(8,128)(2,1)S(1)} collective-permute-done((bf16[2,64,512]{2,1,0:T(8,128)(2,1)S(1)}, bf16[2,64,512]{2,1,0:T(8,128)(2,1)S(1)}, u32[]{:S(2)}, u32[]{:S(2)}) %collective-permute-start.5) | collective-permute-done | bytes 131104 | tf_op jit(solution)/shard_map/ppermute | solution.py:90
  25.5 1.4 %collective-permute-done.4.near_ref = bf16[2,64,512]{2,1,0:T(8,128)(2,1)S(1)} collective-permute-done((bf16[2,64,512]{2,1,0:T(8,128)(2,1)S(1)}, bf16[2,64,512]{2,1,0:T(8,128)(2,1)S(1)}, u32[]{:S(2)}, u32[]{:S(2)}) %collective-permute-start.4) | collective-permute-done | bytes 131104 | tf_op jit(solution)/shard_map/ppermute | solution.py:91
  26.9 2.7 %collective-permute-done.3.own_ref = bf16[2,64,512]{2,1,0:T(8,128)(2,1)S(1)} collective-permute-done((bf16[2,64,512]{2,1,0:T(8,128)(2,1)S(1)}, bf16[2,64,512]{2,1,0:T(8,128)(2,1)S(1)}, u32[]{:S(2)}, u32[]{:S(2)}) %collective-permute-start.3) | collective-permute-done | bytes 131104 | tf_op jit(solution)/shard_map/ppermute | solution.py:92
  29.6 0.6 shard_map.51
  30.2 0.1 collective-permute-start.8
  30.3 0.5 collective-permute-start.7
  30.8 0.1 collective-permute-start.6
  30.9 0.9 %collective-permute-done.8.far_ref = bf16[2,64,512]{2,1,0:T(8,128)(2,1)} collective-permute-done((bf16[2,64,512]{2,1,0:T(8,128)(2,1)S(1)}, bf16[2,64,512]{2,1,0:T(8,128)(2,1)}, u32[]{:S(2)}, u32[]{:S(2)}) %collective-permute-start.8) | collective-permute-done | bytes 131104 | tf_op jit(solution)/shard_map/ppermute | solution.py:90
  31.8 0.2 collective-permute-done.7.near_ref
  32.0 0.3 collective-permute-done.6.own_ref
  32.3 1.6 %shard_map.52 = bf16[2,64,512]{2,1,0:T(8,128)(2,1)S(1)} custom-call(bf16[2,64,512]{2,1,0:T(8,128)(2,1)} %collective-permute-done.6.own_ref, bf16[2,64,512]{2,1,0:T(8,128)(2,1)} %collective-permute-done.7.near_ref, bf16[2,64,512]{2,1,0:T(8,128)(2,1)} %collective-permute-done.8.far_ref, bf16[3,2,512,512]{3,2,1,0:T(8,128)(2,1)S(1)} %bitcast.9, ...), custom_call_target="tpu_custom_call" | custom-call | flops 402653184 | bytes 3801088 | tf_op jit(solution)/shard_map/pallas_call | solution.py:63
  33.9 0.3 collective-permute-start.11
  34.2 0.3 collective-permute-start.10
  34.5 0.2 collective-permute-start.9
  34.7 0.0 copy-start.4
  34.7 0.6 collective-permute-done.11.far_ref
  35.3 0.2 collective-permute-done.10.near_ref
  35.5 0.3 collective-permute-done.9.own_ref
  35.9 0.6 shard_map.53
  36.4 6.9 %collective-permute-start.14 = (bf16[2,64,512]{2,1,0:T(8,128)(2,1)S(1)}, bf16[2,64,512]{2,1,0:T(8,128)(2,1)S(1)}, u32[]{:S(2)}, u32[]{:S(2)}) collective-permute-start(bf16[2,64,512]{2,1,0:T(8,128)(2,1)S(1)} %shard_map.53), channel_id=1, source_target_pairs={{128,127},{129,66},{130,65},{131,68},{132,67},{133,70},{134,69},{1... | collective-permute-start | bytes 393224 | tf_op jit(solution)/shard_map/ppermute | solution.py:90
  43.3 3.4 %collective-permute-start.13 = (bf16[2,64,512]{2,1,0:T(8,128)(2,1)S(1)}, bf16[2,64,512]{2,1,0:T(8,128)(2,1)S(1)}, u32[]{:S(2)}, u32[]{:S(2)}) collective-permute-start(bf16[2,64,512]{2,1,0:T(8,128)(2,1)S(1)} %shard_map.53), channel_id=1, source_target_pairs={{128,65},{129,64},{130,67},{131,66},{132,69},{133,68},{134,71},{13... | collective-permute-start | bytes 393224 | tf_op jit(solution)/shard_map/ppermute | solution.py:91
  46.7 0.1 collective-permute-start.12
  46.8 1.2 %collective-permute-done.14.far_ref = bf16[2,64,512]{2,1,0:T(8,128)(2,1)S(1)} collective-permute-done((bf16[2,64,512]{2,1,0:T(8,128)(2,1)S(1)}, bf16[2,64,512]{2,1,0:T(8,128)(2,1)S(1)}, u32[]{:S(2)}, u32[]{:S(2)}) %collective-permute-start.14) | collective-permute-done | bytes 131104 | tf_op jit(solution)/shard_map/ppermute | solution.py:90
  48.0 3.8 %collective-permute-done.13.near_ref = bf16[2,64,512]{2,1,0:T(8,128)(2,1)S(1)} collective-permute-done((bf16[2,64,512]{2,1,0:T(8,128)(2,1)S(1)}, bf16[2,64,512]{2,1,0:T(8,128)(2,1)S(1)}, u32[]{:S(2)}, u32[]{:S(2)}) %collective-permute-start.13) | collective-permute-done | bytes 131104 | tf_op jit(solution)/shard_map/ppermute | solution.py:91
  51.8 2.4 %collective-permute-done.12.own_ref = bf16[2,64,512]{2,1,0:T(8,128)(2,1)S(1)} collective-permute-done((bf16[2,64,512]{2,1,0:T(8,128)(2,1)S(1)}, bf16[2,64,512]{2,1,0:T(8,128)(2,1)S(1)}, u32[]{:S(2)}, u32[]{:S(2)}) %collective-permute-start.12) | collective-permute-done | bytes 131104 | tf_op jit(solution)/shard_map/ppermute | solution.py:92
  54.2 1.2 %shard_map.54 = bf16[2,64,512]{2,1,0:T(8,128)(2,1)} custom-call(bf16[2,64,512]{2,1,0:T(8,128)(2,1)S(1)} %collective-permute-done.12.own_ref, bf16[2,64,512]{2,1,0:T(8,128)(2,1)S(1)} %collective-permute-done.13.near_ref, bf16[2,64,512]{2,1,0:T(8,128)(2,1)S(1)} %collective-permute-done.14.far_ref, bf16[3,2,512,512]{3,2,1,0:T(8,128)(2,1)S(1)} %bitcast.11, ...), custom_call_target="tpu_custom_call" | custom-call | flops 402653184 | bytes 3801088 | tf_op jit(solution)/shard_map/pallas_call | solution.py:63
  55.5 0.0 collective-permute-start.17
  55.5 0.9 %collective-permute-start.16 = (bf16[2,64,512]{2,1,0:T(8,128)(2,1)}, bf16[2,64,512]{2,1,0:T(8,128)(2,1)}, u32[]{:S(2)}, u32[]{:S(2)}) collective-permute-start(bf16[2,64,512]{2,1,0:T(8,128)(2,1)} %shard_map.54), channel_id=1, source_target_pairs={{64,1},{65,0},{66,3},{67,2},{68,5},{69,4},{70,7},{71,6},{72,9},{73... | collective-permute-start | bytes 393224 | tf_op jit(solution)/shard_map/ppermute | solution.py:91
  56.4 0.0 collective-permute-start.15
  56.4 8.5 %collective-permute-done.17.far_ref = bf16[2,64,512]{2,1,0:T(8,128)(2,1)S(1)} collective-permute-done((bf16[2,64,512]{2,1,0:T(8,128)(2,1)}, bf16[2,64,512]{2,1,0:T(8,128)(2,1)S(1)}, u32[]{:S(2)}, u32[]{:S(2)}) %collective-permute-start.17) | collective-permute-done | bytes 131104 | tf_op jit(solution)/shard_map/ppermute | solution.py:90
  64.9 0.6 copy-done.7
  65.5 0.0 collective-permute-done.16.near_ref
  65.5 0.0 collective-permute-done.15.own_ref
  65.5 0.9 %copy-done.8 = bf16[2,64,512]{2,1,0:T(8,128)(2,1)S(1)} copy-done((bf16[2,64,512]{2,1,0:T(8,128)(2,1)S(1)}, bf16[2,64,512]{2,1,0:T(8,128)(2,1)}, u32[]{:S(2)}) %copy-start.8) | copy-done | bytes 131096
  66.4 1.5 %shard_map.55 = bf16[2,64,512]{2,1,0:T(8,128)(2,1)S(1)} custom-call(bf16[2,64,512]{2,1,0:T(8,128)(2,1)} %collective-permute-done.15.own_ref, bf16[2,64,512]{2,1,0:T(8,128)(2,1)} %collective-permute-done.16.near_ref, bf16[2,64,512]{2,1,0:T(8,128)(2,1)S(1)} %copy-done.8, bf16[3,2,512,512]{3,2,1,0:T(8,128)(2,1)S(1)} %bitcast.12, ...), custom_call_target="tpu_custom_call" | custom-call | flops 402653184 | bytes 3801088 | tf_op jit(solution)/shard_map/pallas_call | solution.py:63
  68.0 0.7 %select_bitcast_fusion = bf16[1,2,64,512]{3,2,1,0:T(8,128)(2,1)} fusion(bf16[2,64,512]{2,1,0:T(8,128)(2,1)S(1)} %shard_map.55, bf16[2,64,512]{2,1,0:T(8,128)(2,1)} %shard_map.54, bf16[2,64,512]{2,1,0:T(8,128)(2,1)S(1)} %shard_map.53, bf16[2,64,512]{2,1,0:T(8,128)(2,1)S(1)} %select_select_fusion.addend_ref, pred[]{:T(512)S(6)} %eq.17, pred[]{:T(512)S(6)} %eq.16, ...), kind=kLoop, calls=%fused_computation | loop fusion | flops 196608 | bytes 655363 | tf_op jit(solution)/shard_map/broadcast_in_dim | solution.py:110
  (14 shorter events, 0.0 us)
Async XLA Ops:
  0.6 9.7 %collective-permute-start.2 = (bf16[2,64,512]{2,1,0:T(8,128)(2,1)}, bf16[2,64,512]{2,1,0:T(8,128)(2,1)S(1)}, u32[]{:S(2)}, u32[]{:S(2)}) collective-permute-start(bf16[2,64,512]{2,1,0:T(8,128)(2,1)} %bitcast.14), channel_id=1, source_target_pairs={{0,127},{1,66},{2,65},{3,68},{4,67},{5,70},{6,69},{7,72},{8,71},{9... | collective-permute-start | bytes 393224 | tf_op jit(solution)/shard_map/ppermute | solution.py:90
  7.5 2.9 %collective-permute-start.1 = (bf16[2,64,512]{2,1,0:T(8,128)(2,1)}, bf16[2,64,512]{2,1,0:T(8,128)(2,1)S(1)}, u32[]{:S(2)}, u32[]{:S(2)}) collective-permute-start(bf16[2,64,512]{2,1,0:T(8,128)(2,1)} %bitcast.15), channel_id=1, source_target_pairs={{0,65},{1,64},{2,67},{3,66},{4,69},{5,68},{6,71},{7,70},{8,73},{9,... | collective-permute-start | bytes 393224 | tf_op jit(solution)/shard_map/ppermute | solution.py:91
  7.5 2.9 %collective-permute-start = (bf16[2,64,512]{2,1,0:T(8,128)(2,1)}, bf16[2,64,512]{2,1,0:T(8,128)(2,1)S(1)}, u32[]{:S(2)}, u32[]{:S(2)}) collective-permute-start(bf16[2,64,512]{2,1,0:T(8,128)(2,1)} %bitcast.16), channel_id=1, source_target_pairs={{0,64},{1,65},{2,66},{3,67},{4,68},{5,69},{6,70},{7,71},{8,72},{9,... | collective-permute-start | bytes 393224 | tf_op jit(solution)/shard_map/ppermute | solution.py:92
  10.4 1.9 %copy-start = (bf16[1,3,2,512,512]{4,3,2,1,0:T(8,128)(2,1)S(1)}, bf16[1,3,2,512,512]{4,3,2,1,0:T(8,128)(2,1)}, u32[]{:S(2)}) copy-start(bf16[1,3,2,512,512]{4,3,2,1,0:T(8,128)(2,1)} %param.4) | copy-start | bytes 9437188
  12.3 0.9 %copy-start.5 = (bf16[1,2,64,512]{3,2,1,0:T(8,128)(2,1)S(1)}, bf16[1,2,64,512]{3,2,1,0:T(8,128)(2,1)}, u32[]{:S(2)}) copy-start(bf16[1,2,64,512]{3,2,1,0:T(8,128)(2,1)} %param.3) | copy-start | bytes 393220
  13.2 16.5 %copy-start.1 = (bf16[1,3,2,512,512]{4,3,2,1,0:T(8,128)(2,1)S(1)}, bf16[1,3,2,512,512]{4,3,2,1,0:T(8,128)(2,1)}, u32[]{:S(2)}) copy-start(bf16[1,3,2,512,512]{4,3,2,1,0:T(8,128)(2,1)} %param.4) | copy-start | bytes 9437188
  13.2 16.5 %copy-start.6 = (bf16[1,2,64,512]{3,2,1,0:T(8,128)(2,1)S(1)}, bf16[1,2,64,512]{3,2,1,0:T(8,128)(2,1)}, u32[]{:S(2)}) copy-start(bf16[1,2,64,512]{3,2,1,0:T(8,128)(2,1)} %param.3) | copy-start | bytes 393220
  13.8 11.8 %collective-permute-start.5 = (bf16[2,64,512]{2,1,0:T(8,128)(2,1)S(1)}, bf16[2,64,512]{2,1,0:T(8,128)(2,1)S(1)}, u32[]{:S(2)}, u32[]{:S(2)}) collective-permute-start(bf16[2,64,512]{2,1,0:T(8,128)(2,1)S(1)} %shard_map.50), channel_id=1, source_target_pairs={{64,191},{65,130},{66,129},{67,132},{68,131},{69,134},{70,133},{71... | collective-permute-start | bytes 393224 | tf_op jit(solution)/shard_map/ppermute | solution.py:90
  14.5 12.4 %collective-permute-start.4 = (bf16[2,64,512]{2,1,0:T(8,128)(2,1)S(1)}, bf16[2,64,512]{2,1,0:T(8,128)(2,1)S(1)}, u32[]{:S(2)}, u32[]{:S(2)}) collective-permute-start(bf16[2,64,512]{2,1,0:T(8,128)(2,1)S(1)} %shard_map.50), channel_id=1, source_target_pairs={{64,129},{65,128},{66,131},{67,130},{68,133},{69,132},{70,135},{71... | collective-permute-start | bytes 393224 | tf_op jit(solution)/shard_map/ppermute | solution.py:91
  14.9 14.7 %collective-permute-start.3 = (bf16[2,64,512]{2,1,0:T(8,128)(2,1)S(1)}, bf16[2,64,512]{2,1,0:T(8,128)(2,1)S(1)}, u32[]{:S(2)}, u32[]{:S(2)}) collective-permute-start(bf16[2,64,512]{2,1,0:T(8,128)(2,1)S(1)} %shard_map.50), channel_id=1, source_target_pairs={{64,128},{65,129},{66,130},{67,131},{68,132},{69,133},{70,134},{71... | collective-permute-start | bytes 393224 | tf_op jit(solution)/shard_map/ppermute | solution.py:92
  30.2 1.6 %collective-permute-start.8 = (bf16[2,64,512]{2,1,0:T(8,128)(2,1)S(1)}, bf16[2,64,512]{2,1,0:T(8,128)(2,1)}, u32[]{:S(2)}, u32[]{:S(2)}) collective-permute-start(bf16[2,64,512]{2,1,0:T(8,128)(2,1)S(1)} %shard_map.51), channel_id=1, source_target_pairs={{128,255},{129,194},{130,193},{131,196},{132,195},{133,198},{134,1... | collective-permute-start | bytes 393224 | tf_op jit(solution)/shard_map/ppermute | solution.py:90
  30.3 1.7 %collective-permute-start.7 = (bf16[2,64,512]{2,1,0:T(8,128)(2,1)S(1)}, bf16[2,64,512]{2,1,0:T(8,128)(2,1)}, u32[]{:S(2)}, u32[]{:S(2)}) collective-permute-start(bf16[2,64,512]{2,1,0:T(8,128)(2,1)S(1)} %shard_map.51), channel_id=1, source_target_pairs={{128,193},{129,192},{130,195},{131,194},{132,197},{133,196},{134,1... | collective-permute-start | bytes 393224 | tf_op jit(solution)/shard_map/ppermute | solution.py:91
  30.8 1.5 %collective-permute-start.6 = (bf16[2,64,512]{2,1,0:T(8,128)(2,1)S(1)}, bf16[2,64,512]{2,1,0:T(8,128)(2,1)}, u32[]{:S(2)}, u32[]{:S(2)}) collective-permute-start(bf16[2,64,512]{2,1,0:T(8,128)(2,1)S(1)} %shard_map.51), channel_id=1, source_target_pairs={{128,192},{129,193},{130,194},{131,195},{132,196},{133,197},{134,1... | collective-permute-start | bytes 393224 | tf_op jit(solution)/shard_map/ppermute | solution.py:92
  30.9 4.9 %copy-start.2 = (bf16[1,3,2,512,512]{4,3,2,1,0:T(8,128)(2,1)S(1)}, bf16[1,3,2,512,512]{4,3,2,1,0:T(8,128)(2,1)}, u32[]{:S(2)}) copy-start(bf16[1,3,2,512,512]{4,3,2,1,0:T(8,128)(2,1)} %param.5) | copy-start | bytes 9437188
  33.9 1.4 %collective-permute-start.11 = (bf16[2,64,512]{2,1,0:T(8,128)(2,1)S(1)}, bf16[2,64,512]{2,1,0:T(8,128)(2,1)S(1)}, u32[]{:S(2)}, u32[]{:S(2)}) collective-permute-start(bf16[2,64,512]{2,1,0:T(8,128)(2,1)S(1)} %shard_map.52), channel_id=1, source_target_pairs={{192,191},{193,130},{194,129},{195,132},{196,131},{197,134},{198,1... | collective-permute-start | bytes 393224 | tf_op jit(solution)/shard_map/ppermute | solution.py:90
  34.2 1.3 %collective-permute-start.10 = (bf16[2,64,512]{2,1,0:T(8,128)(2,1)S(1)}, bf16[2,64,512]{2,1,0:T(8,128)(2,1)S(1)}, u32[]{:S(2)}, u32[]{:S(2)}) collective-permute-start(bf16[2,64,512]{2,1,0:T(8,128)(2,1)S(1)} %shard_map.52), channel_id=1, source_target_pairs={{192,129},{193,128},{194,131},{195,130},{196,133},{197,132},{198,1... | collective-permute-start | bytes 393224 | tf_op jit(solution)/shard_map/ppermute | solution.py:91
  34.5 1.3 %collective-permute-start.9 = (bf16[2,64,512]{2,1,0:T(8,128)(2,1)S(1)}, bf16[2,64,512]{2,1,0:T(8,128)(2,1)S(1)}, u32[]{:S(2)}, u32[]{:S(2)}) collective-permute-start(bf16[2,64,512]{2,1,0:T(8,128)(2,1)S(1)} %shard_map.52), channel_id=1, source_target_pairs={{192,128},{193,129},{194,130},{195,131},{196,132},{197,133},{198,1... | collective-permute-start | bytes 393224 | tf_op jit(solution)/shard_map/ppermute | solution.py:92
  34.7 33.3 %copy-start.4 = (bf16[2,64,512]{2,1,0:T(8,128)(2,1)}, bf16[2,64,512]{2,1,0:T(8,128)(2,1)S(1)}, u32[]{:S(2)}) copy-start(bf16[2,64,512]{2,1,0:T(8,128)(2,1)S(1)} %select_select_fusion.addend_ref) | copy-start | bytes 393220
  35.9 29.7 %copy-start.3 = (bf16[1,3,2,512,512]{4,3,2,1,0:T(8,128)(2,1)S(1)}, bf16[1,3,2,512,512]{4,3,2,1,0:T(8,128)(2,1)}, u32[]{:S(2)}) copy-start(bf16[1,3,2,512,512]{4,3,2,1,0:T(8,128)(2,1)} %param.5) | copy-start | bytes 9437188
  36.4 11.5 %collective-permute-start.14 = (bf16[2,64,512]{2,1,0:T(8,128)(2,1)S(1)}, bf16[2,64,512]{2,1,0:T(8,128)(2,1)S(1)}, u32[]{:S(2)}, u32[]{:S(2)}) collective-permute-start(bf16[2,64,512]{2,1,0:T(8,128)(2,1)S(1)} %shard_map.53), channel_id=1, source_target_pairs={{128,127},{129,66},{130,65},{131,68},{132,67},{133,70},{134,69},{1... | collective-permute-start | bytes 393224 | tf_op jit(solution)/shard_map/ppermute | solution.py:90
  43.3 8.5 %collective-permute-start.13 = (bf16[2,64,512]{2,1,0:T(8,128)(2,1)S(1)}, bf16[2,64,512]{2,1,0:T(8,128)(2,1)S(1)}, u32[]{:S(2)}, u32[]{:S(2)}) collective-permute-start(bf16[2,64,512]{2,1,0:T(8,128)(2,1)S(1)} %shard_map.53), channel_id=1, source_target_pairs={{128,65},{129,64},{130,67},{131,66},{132,69},{133,68},{134,71},{13... | collective-permute-start | bytes 393224 | tf_op jit(solution)/shard_map/ppermute | solution.py:91
  46.7 7.5 %collective-permute-start.12 = (bf16[2,64,512]{2,1,0:T(8,128)(2,1)S(1)}, bf16[2,64,512]{2,1,0:T(8,128)(2,1)S(1)}, u32[]{:S(2)}, u32[]{:S(2)}) collective-permute-start(bf16[2,64,512]{2,1,0:T(8,128)(2,1)S(1)} %shard_map.53), channel_id=1, source_target_pairs={{128,64},{129,65},{130,66},{131,67},{132,68},{133,69},{134,70},{13... | collective-permute-start | bytes 393224 | tf_op jit(solution)/shard_map/ppermute | solution.py:92
  55.5 9.4 %collective-permute-start.17 = (bf16[2,64,512]{2,1,0:T(8,128)(2,1)}, bf16[2,64,512]{2,1,0:T(8,128)(2,1)S(1)}, u32[]{:S(2)}, u32[]{:S(2)}) collective-permute-start(bf16[2,64,512]{2,1,0:T(8,128)(2,1)} %shard_map.54), channel_id=1, source_target_pairs={{64,63},{65,2},{66,1},{67,4},{68,3},{69,6},{70,5},{71,8},{72,7},{7... | collective-permute-start | bytes 393224 | tf_op jit(solution)/shard_map/ppermute | solution.py:90
  55.5 10.1 %collective-permute-start.16 = (bf16[2,64,512]{2,1,0:T(8,128)(2,1)}, bf16[2,64,512]{2,1,0:T(8,128)(2,1)}, u32[]{:S(2)}, u32[]{:S(2)}) collective-permute-start(bf16[2,64,512]{2,1,0:T(8,128)(2,1)} %shard_map.54), channel_id=1, source_target_pairs={{64,1},{65,0},{66,3},{67,2},{68,5},{69,4},{70,7},{71,6},{72,9},{73... | collective-permute-start | bytes 393224 | tf_op jit(solution)/shard_map/ppermute | solution.py:91
  56.4 9.1 %collective-permute-start.15 = (bf16[2,64,512]{2,1,0:T(8,128)(2,1)}, bf16[2,64,512]{2,1,0:T(8,128)(2,1)}, u32[]{:S(2)}, u32[]{:S(2)}) collective-permute-start(bf16[2,64,512]{2,1,0:T(8,128)(2,1)} %shard_map.54), channel_id=1, source_target_pairs={{64,0},{65,1},{66,2},{67,3},{68,4},{69,5},{70,6},{71,7},{72,8},{73... | collective-permute-start | bytes 393224 | tf_op jit(solution)/shard_map/ppermute | solution.py:92
  64.9 0.6 copy-start.7
  65.5 0.9 %copy-start.8 = (bf16[2,64,512]{2,1,0:T(8,128)(2,1)S(1)}, bf16[2,64,512]{2,1,0:T(8,128)(2,1)}, u32[]{:S(2)}) copy-start(bf16[2,64,512]{2,1,0:T(8,128)(2,1)} %copy-done.7) | copy-start | bytes 393220

commit v2 on v1

v2 whole, which is shorter than its diff:
```python
import functools

import jax
import jax.numpy as jnp
from jax import lax
from jax.experimental import pallas as pl
from jax.experimental.pallas import tpu as pltpu
from jax.sharding import PartitionSpec as P

AXES = ("layer", "tile")
VMEM_LIMIT = 16 * 1024 * 1024


def far_mate(tile, tiles):
    mate = tile + 1 if tile % 2 else tile - 1
    return mate if 0 <= mate < tiles else tile


def near_mate(tile, tiles):
    return tile - 1 if tile % 2 else tile + 1


def same(tile, tiles):
    return tile


def mirror(tile, tiles):
    x, z, y = tile // 16, tile // 4 % 4, tile % 4
    return 16 * x + 4 * (3 - z) + y


def pairs_of(route, tiles):
    return [
        (source * tiles + tile, target * tiles + mate(tile, tiles))
        for source, target, mate in route
        for tile in range(tiles)
    ]


def within_chip(source, target, mate):
    one, two = [layer for layer in range(4) if layer not in (source, target)]
    return ((source, target, mate), (target, source, same), (one, two, same), (two, one, same))


def across(source, target, mate):
    beyond = 3 if target == 2 else 0
    behind = 3 - beyond
    return ((source, target, mate), (target, beyond, same), (beyond, behind, mirror), (behind, source, same))


def beside(source, target):
    beyond = 3 if target == 2 else 0
    behind = 3 - beyond
    return ((target, target, near_mate), (beyond, beyond, near_mate), (source, behind, same), (behind, source, same))


def permute(values, route):
    return lax.ppermute(values, AXES, pairs_of(route, lax.axis_size("tile")))


def load_kernel(layer, blocks_ref, after_ref, held_ref, sems):
    @pl.when(lax.axis_index("layer") == layer)
    def _():
        count, parts = blocks_ref.shape[:2]
        copies = [
            pltpu.make_async_copy(blocks_ref.at[i, j], held_ref.at[i, j], sems.at[i, j])
            for i in range(count)
            for j in range(parts)
        ]
        for copy in copies:
            copy.start()
        for copy in copies:
            copy.wait()


def load(blocks, after, layer):
    return pl.pallas_call(
        functools.partial(load_kernel, layer),
        out_shape=pltpu.VMEM(blocks.shape, blocks.dtype),
        in_specs=[pl.BlockSpec(memory_space=pl.ANY)] * 2,
        out_specs=pl.BlockSpec(memory_space=pltpu.VMEM),
        scratch_shapes=[pltpu.SemaphoreType.DMA(blocks.shape[:2])],
        compiler_params=pltpu.CompilerParams(vmem_limit_bytes=VMEM_LIMIT),
        cost_estimate=pl.CostEstimate(flops=0, bytes_accessed=blocks.size * 4, transcendentals=0),
    )(pltpu.with_memory_space_constraint(blocks, pltpu.HBM), after)


def step_kernel(layer, far_ref, near_ref, own_ref, blocks_ref, addend_ref, *rest):
    *kept_ref, out_ref = rest
    tiles = lax.axis_size("tile")
    tile = lax.axis_index("tile")
    odd = lax.rem(tile, 2)
    rows, cells = own_ref.shape[1:]
    edge = jnp.logical_or(tile == 0, tile == tiles - 1)
    here = lax.axis_index("layer") == layer

    def stacked(ref):
        return ref[...].reshape(2 * rows, cells)

    def product(values, number):
        by_real = jnp.dot(values, blocks_ref[number, 0], preferred_element_type=jnp.float32)
        by_imag = jnp.dot(values, blocks_ref[number, 1], preferred_element_type=jnp.float32)
        return by_real, by_imag

    far = stacked(far_ref)
    far = jnp.where(edge, jnp.zeros_like(far), far)
    own_real, own_imag = product(stacked(own_ref), 0)
    near_real, near_imag = product(stacked(near_ref), 2 - odd)
    far_real, far_imag = product(far, 1 + odd)
    by_real = own_real + near_real + far_real
    by_imag = own_imag + near_imag + far_imag
    real = (by_real[:rows] - by_imag[rows:] + addend_ref[0].astype(jnp.float32)).astype(out_ref.dtype)
    imag = (by_imag[:rows] + by_real[rows:] + addend_ref[1].astype(jnp.float32)).astype(out_ref.dtype)
    if kept_ref:
        real = jnp.where(here, real, kept_ref[0][0])
        imag = jnp.where(here, imag, kept_ref[0][1])
    out_ref[0] = real
    out_ref[1] = imag


def step(layer, own, near, far, blocks, addend, *kept):
    vmem = pl.BlockSpec(memory_space=pltpu.VMEM)
    return pl.pallas_call(
        functools.partial(step_kernel, layer),
        out_shape=jax.ShapeDtypeStruct(own.shape, own.dtype),
        in_specs=[vmem] * (5 + len(kept)),
        out_specs=vmem,
        compiler_params=pltpu.CompilerParams(vmem_limit_bytes=VMEM_LIMIT),
        cost_estimate=pl.CostEstimate(
            flops=24 * own.shape[1] * own.shape[2] * own.shape[2],
            bytes_accessed=blocks.size * 2 + own.size * 10,
            transcendentals=0,
        ),
    )(far, near, own, blocks, addend, *kept)


def hop(values, source, target, blocks, addend, *kept):
    if source + target == 3:
        own = permute(values, across(source, target, same))
        far = permute(values, across(source, target, far_mate))
        near = permute(own, beside(source, target))
    else:
        far = permute(values, within_chip(source, target, far_mate))
        near = permute(values, within_chip(source, target, near_mate))
        own = permute(values, within_chip(source, target, same))
    held = load(blocks, values, target)
    return step(target, own, near, far, held, addend, *kept)


def per_device(sources, down_blocks, up_blocks):
    layer = lax.axis_index("layer")
    source = sources[0]
    values = falling = source
    for index in (1, 2, 3):
        values = hop(values, index - 1, index, down_blocks[0], source)
        falling = jnp.where(layer == index, values, falling)
    rising = falling
    for index in (2, 1):
        values = hop(values, index + 1, index, up_blocks[0], falling)
        rising = jnp.where(layer == index, values, rising)
    rising = hop(values, 1, 0, up_blocks[0], falling, rising)
    return (falling[None], rising[None])


def solution(mesh):
    return jax.shard_map(
        per_device,
        mesh=mesh,
        in_specs=(
            P("layer", None, None, "tile"),
            P("layer", None, None, "tile", None),
            P("layer", None, None, "tile", None),
        ),
        out_specs=(P("layer", None, None, "tile"), P("layer", None, None, "tile")),
        check_vma=False,
    )
```

time: 69 us -> 57.7 us (0.84)
  waiting for transfers between devices: 35.5 us -> 17.7 us
  starting transfers between devices: 21.3 us -> 31.9 us
  local copies, waits for them, and re-layouts: 4.35 us -> 0.92 us
    ppermute x18, waiting for transfers between devices: 35.5 us -> 17.7 us  [permute(): return lax.ppermute(values, AXES, pairs_of(route, lax.axis_size('tile')))]
    ppermute x18, starting transfers between devices: 21.3 us -> 31.9 us  [permute(): return lax.ppermute(values, AXES, pairs_of(route, lax.axis_size('tile')))]
    unnamed x18 -> x6, local copies, waits for them, and re-layouts: 4.35 us -> 0.92 us
    broadcast_in_dim x1 -> x0, other arithmetic: 0.69 us -> none  [per_device(): return (falling[None], rising[None])]
    pallas_call x6 -> x12, Pallas kernels: 6.12 us -> 6.29 us  [the longest x6 4.14 us: step(): pl.pallas_call(functools.partial(step_kernel, layer), out_shape=jax.Shape...]
  transfers between devices with their start and end apart: 18 -> 18, of which waited for: 14 -> 12; matrix products, arithmetic and copies ran while one was open for 0% -> 0% of each run, Pallas kernels for 0% -> 4%
where the time goes in v2:
time: 57.7 us; the launch traced here: 57.6 us
  starting transfers between devices  31.9 us (55%)
  waiting for transfers between devices  17.7 us (31%)
  Pallas kernels  6.29 us (11%)
  local copies, waits for them, and re-layouts  0.92 us (2%)
  between operations  0.77 us (1%)
    ppermute x18, starting transfers between devices, permute(): return lax.ppermute(values, AXES, pairs_of(route, lax.axis_size('tile')))  31.9 us
    ppermute x18, waiting for transfers between devices, permute(): return lax.ppermute(values, AXES, pairs_of(route, lax.axis_size('tile')))  17.7 us
    pallas_call x6, Pallas kernels, step(): pl.pallas_call(functools.partial(step_kernel, layer), out_shape=jax.Shape...  4.14 us
    pallas_call x6, Pallas kernels, load(): pl.pallas_call(functools.partial(load_kernel, layer), out_shape=pltpu.VME...  2.15 us
  transfers between devices with their start and end apart: 18, of which 12 were waited for; matrix products, arithmetic and copies ran while one was open for 0% of the time, Pallas kernels for 4%

profile of v2, /device:TPU:6, one launch (start us, length us, event | category | flops | bytes accessed | tf_op | source)
XLA Modules:
  0.0 57.6 jit_solution(16932325945529438800)
XLA Ops:
  0.6 6.9 %collective-permute-start = (bf16[2,64,512]{2,1,0:T(8,128)(2,1)}, bf16[2,64,512]{2,1,0:T(8,128)(2,1)S(1)}, u32[]{:S(2)}, u32[]{:S(2)}) collective-permute-start(bf16[2,64,512]{2,1,0:T(8,128)(2,1)} %bitcast.7), channel_id=1, source_target_pairs={{0,64},{1,66},{2,65},{3,68},{4,67},{5,70},{6,69},{7,72},{8,71},{9,... | collective-permute-start | bytes 393224 | tf_op jit(solution)/shard_map/ppermute | solution.py:58
  7.5 0.5 collective-permute-start.2
  8.0 0.9 %copy-done.1 = bf16[1,2,64,512]{3,2,1,0:T(8,128)(2,1)S(1)} copy-done((bf16[1,2,64,512]{3,2,1,0:T(8,128)(2,1)S(1)}, bf16[1,2,64,512]{3,2,1,0:T(8,128)(2,1)}, u32[]{:S(2)}) %copy-start.1) | copy-done | bytes 131096
  8.9 0.1 shard_map.50.blocks_ref
  9.0 1.4 %collective-permute-done.far_ref = bf16[2,64,512]{2,1,0:T(8,128)(2,1)S(1)} collective-permute-done((bf16[2,64,512]{2,1,0:T(8,128)(2,1)}, bf16[2,64,512]{2,1,0:T(8,128)(2,1)S(1)}, u32[]{:S(2)}, u32[]{:S(2)}) %collective-permute-start) | collective-permute-done | bytes 131104 | tf_op jit(solution)/shard_map/ppermute | solution.py:58
  10.3 0.0 collective-permute-done.1.near_ref
  10.4 0.6 %shard_map.51.after_ref = bf16[2,64,512]{2,1,0:T(8,128)(2,1)S(1)} custom-call(bf16[2,64,512]{2,1,0:T(8,128)(2,1)S(1)} %collective-permute-done.far_ref, bf16[2,64,512]{2,1,0:T(8,128)(2,1)S(1)} %collective-permute-done.1.near_ref, bf16[2,64,512]{2,1,0:T(8,128)(2,1)S(1)} %collective-permute-done.2.own_ref, bf16[3,2,512,512]{3,2,1,0:T(8,128)(2,1)S(1)} %shard_map.50.blocks_ref, ...), custom_call_target="tpu_custom_call" | custom-call | flops 402653184 | bytes 3801088 | tf_op jit(solution)/shard_map/pallas_call | solution.py:123
  10.9 0.0 copy-start.2
  11.0 0.8 %collective-permute-start.4 = (bf16[2,64,512]{2,1,0:T(8,128)(2,1)S(1)}, bf16[2,64,512]{2,1,0:T(8,128)(2,1)S(1)}, u32[]{:S(2)}, u32[]{:S(2)}) collective-permute-start(bf16[2,64,512]{2,1,0:T(8,128)(2,1)S(1)} %shard_map.51.after_ref), channel_id=1, source_target_pairs={{64,128},{65,129},{66,130},{67,131},{68,132},{69,133},{70,134},{71... | collective-permute-start | bytes 393224 | tf_op jit(solution)/shard_map/ppermute | solution.py:58
  11.7 0.1 collective-permute-start.3
  11.8 5.4 %collective-permute-done.4.own_ref = bf16[2,64,512]{2,1,0:T(8,128)(2,1)S(1)} collective-permute-done((bf16[2,64,512]{2,1,0:T(8,128)(2,1)S(1)}, bf16[2,64,512]{2,1,0:T(8,128)(2,1)S(1)}, u32[]{:S(2)}, u32[]{:S(2)}) %collective-permute-start.4) | collective-permute-done | bytes 131104 | tf_op jit(solution)/shard_map/ppermute | solution.py:58
  17.2 0.1 shard_map.52.blocks_ref
  17.3 1.3 %collective-permute-done.3.far_ref = bf16[2,64,512]{2,1,0:T(8,128)(2,1)S(1)} collective-permute-done((bf16[2,64,512]{2,1,0:T(8,128)(2,1)S(1)}, bf16[2,64,512]{2,1,0:T(8,128)(2,1)S(1)}, u32[]{:S(2)}, u32[]{:S(2)}) %collective-permute-start.3) | collective-permute-done | bytes 131104 | tf_op jit(solution)/shard_map/ppermute | solution.py:58
  18.6 0.0 collective-permute-done.5.near_ref
  18.6 0.6 %shard_map.53.after_ref = bf16[2,64,512]{2,1,0:T(8,128)(2,1)S(1)} custom-call(bf16[2,64,512]{2,1,0:T(8,128)(2,1)S(1)} %collective-permute-done.3.far_ref, bf16[2,64,512]{2,1,0:T(8,128)(2,1)S(1)} %collective-permute-done.5.near_ref, bf16[2,64,512]{2,1,0:T(8,128)(2,1)S(1)} %collective-permute-done.4.own_ref, ...), custom_call_target="tpu_custom_call" | custom-call | flops 402653184 | bytes 3801088 | tf_op jit(solution)/shard_map/pallas_call | solution.py:123
  19.2 0.2 collective-permute-start.6
  19.4 0.4 collective-permute-start.7
  19.8 0.1 collective-permute-start.8
  19.9 0.1 shard_map.54.blocks_ref
  20.0 0.7 %collective-permute-done.6.far_ref = bf16[2,64,512]{2,1,0:T(8,128)(2,1)S(1)} collective-permute-done((bf16[2,64,512]{2,1,0:T(8,128)(2,1)S(1)}, bf16[2,64,512]{2,1,0:T(8,128)(2,1)S(1)}, u32[]{:S(2)}, u32[]{:S(2)}) %collective-permute-start.6) | collective-permute-done | bytes 131104 | tf_op jit(solution)/shard_map/ppermute | solution.py:58
  20.6 0.2 collective-permute-done.7.near_ref
  20.8 0.3 collective-permute-done.8.own_ref
  21.1 0.6 %shard_map.55.after_ref = bf16[2,64,512]{2,1,0:T(8,128)(2,1)S(1)} custom-call(bf16[2,64,512]{2,1,0:T(8,128)(2,1)S(1)} %collective-permute-done.6.far_ref, bf16[2,64,512]{2,1,0:T(8,128)(2,1)S(1)} %collective-permute-done.7.near_ref, bf16[2,64,512]{2,1,0:T(8,128)(2,1)S(1)} %collective-permute-done.8.own_ref, ...), custom_call_target="tpu_custom_call" | custom-call | flops 402653184 | bytes 3801088 | tf_op jit(solution)/shard_map/pallas_call | solution.py:123
  21.7 0.3 collective-permute-start.9
  22.0 0.3 collective-permute-start.10
  22.3 0.2 collective-permute-start.11
  22.5 0.1 shard_map.56.blocks_ref
  22.6 0.0 copy-start
  22.6 0.5 collective-permute-done.9.far_ref
  23.2 0.2 collective-permute-done.10.near_ref
  23.3 0.3 collective-permute-done.11.own_ref
  23.7 0.6 %shard_map.57.after_ref = bf16[2,64,512]{2,1,0:T(8,128)(2,1)S(1)} custom-call(bf16[2,64,512]{2,1,0:T(8,128)(2,1)S(1)} %collective-permute-done.9.far_ref, bf16[2,64,512]{2,1,0:T(8,128)(2,1)S(1)} %collective-permute-done.10.near_ref, bf16[2,64,512]{2,1,0:T(8,128)(2,1)S(1)} %collective-permute-done.11.own_ref, ...), custom_call_target="tpu_custom_call" | custom-call | flops 402653184 | bytes 3801088 | tf_op jit(solution)/shard_map/pallas_call | solution.py:123
  24.3 11.3 %collective-permute-start.13 = (bf16[2,64,512]{2,1,0:T(8,128)(2,1)S(1)}, bf16[2,64,512]{2,1,0:T(8,128)(2,1)S(1)}, u32[]{:S(2)}, u32[]{:S(2)}) collective-permute-start(bf16[2,64,512]{2,1,0:T(8,128)(2,1)S(1)} %shard_map.57.after_ref), channel_id=1, source_target_pairs={{128,64},{129,65},{130,66},{131,67},{132,68},{133,69},{134,70},{13... | collective-permute-start | bytes 393224 | tf_op jit(solution)/shard_map/ppermute | solution.py:58
  35.6 2.7 %collective-permute-start.12 = (bf16[2,64,512]{2,1,0:T(8,128)(2,1)S(1)}, bf16[2,64,512]{2,1,0:T(8,128)(2,1)S(1)}, u32[]{:S(2)}, u32[]{:S(2)}) collective-permute-start(bf16[2,64,512]{2,1,0:T(8,128)(2,1)S(1)} %shard_map.57.after_ref), channel_id=1, source_target_pairs={{128,64},{129,66},{130,65},{131,68},{132,67},{133,70},{134,69},{13... | collective-permute-start | bytes 393224 | tf_op jit(solution)/shard_map/ppermute | solution.py:58
  38.2 0.0 collective-permute-done.13.own_ref
  38.2 0.2 collective-permute-start.14
  38.4 0.1 shard_map.58.blocks_ref
  38.5 2.5 %collective-permute-done.12.far_ref = bf16[2,64,512]{2,1,0:T(8,128)(2,1)S(1)} collective-permute-done((bf16[2,64,512]{2,1,0:T(8,128)(2,1)S(1)}, bf16[2,64,512]{2,1,0:T(8,128)(2,1)S(1)}, u32[]{:S(2)}, u32[]{:S(2)}) %collective-permute-start.12) | collective-permute-done | bytes 131104 | tf_op jit(solution)/shard_map/ppermute | solution.py:58
  41.0 2.2 %collective-permute-done.14.near_ref = bf16[2,64,512]{2,1,0:T(8,128)(2,1)S(1)} collective-permute-done((bf16[2,64,512]{2,1,0:T(8,128)(2,1)S(1)}, bf16[2,64,512]{2,1,0:T(8,128)(2,1)S(1)}, u32[]{:S(2)}, u32[]{:S(2)}) %collective-permute-start.14) | collective-permute-done | bytes 131104 | tf_op jit(solution)/shard_map/ppermute | solution.py:58
  43.2 0.6 %shard_map.59.after_ref = bf16[2,64,512]{2,1,0:T(8,128)(2,1)S(1)} custom-call(bf16[2,64,512]{2,1,0:T(8,128)(2,1)S(1)} %collective-permute-done.12.far_ref, bf16[2,64,512]{2,1,0:T(8,128)(2,1)S(1)} %collective-permute-done.14.near_ref, bf16[2,64,512]{2,1,0:T(8,128)(2,1)S(1)} %collective-permute-done.13.own_ref, ...), custom_call_target="tpu_custom_call" | custom-call | flops 402653184 | bytes 3801088 | tf_op jit(solution)/shard_map/pallas_call | solution.py:123
  43.8 7.5 %collective-permute-start.15 = (bf16[2,64,512]{2,1,0:T(8,128)(2,1)S(1)}, bf16[2,64,512]{2,1,0:T(8,128)(2,1)S(1)}, u32[]{:S(2)}, u32[]{:S(2)}) collective-permute-start(bf16[2,64,512]{2,1,0:T(8,128)(2,1)S(1)} %shard_map.59.after_ref), channel_id=1, source_target_pairs={{64,0},{65,2},{66,1},{67,4},{68,3},{69,6},{70,5},{71,8},{72,7},{73... | collective-permute-start | bytes 393224 | tf_op jit(solution)/shard_map/ppermute | solution.py:58
  51.3 0.1 collective-permute-start.16
  51.4 0.4 collective-permute-start.17
  51.9 1.9 %shard_map.60.blocks_ref = bf16[3,2,512,512]{3,2,1,0:T(8,128)(2,1)S(1)} custom-call(bf16[3,2,512,512]{3,2,1,0:T(8,128)(2,1)} %bitcast.19, bf16[2,64,512]{2,1,0:T(8,128)(2,1)S(1)} %shard_map.59.after_ref), custom_call_target="tpu_custom_call" | custom-call | bytes 6291456 | tf_op jit(solution)/shard_map/pallas_call | solution.py:77
  53.8 2.6 %collective-permute-done.15.far_ref = bf16[2,64,512]{2,1,0:T(8,128)(2,1)S(1)} collective-permute-done((bf16[2,64,512]{2,1,0:T(8,128)(2,1)S(1)}, bf16[2,64,512]{2,1,0:T(8,128)(2,1)S(1)}, u32[]{:S(2)}, u32[]{:S(2)}) %collective-permute-start.15) | collective-permute-done | bytes 131104 | tf_op jit(solution)/shard_map/ppermute | solution.py:58
  56.4 0.0 collective-permute-done.16.near_ref
  56.4 0.0 collective-permute-done.17.own_ref
  56.4 1.3 %shard_map.61 = bf16[2,64,512]{2,1,0:T(8,128)(2,1)} custom-call(bf16[2,64,512]{2,1,0:T(8,128)(2,1)S(1)} %collective-permute-done.15.far_ref, bf16[2,64,512]{2,1,0:T(8,128)(2,1)S(1)} %collective-permute-done.16.near_ref, bf16[2,64,512]{2,1,0:T(8,128)(2,1)S(1)} %collective-permute-done.17.own_ref, bf16[3,2,512,512]{3,2,1,0:T(8,128)(2,1)S(1)} %shard_map.60.blocks_ref, ...), custom_call_target="tpu_custom_call" | custom-call | flops 402653184 | bytes 3801088 | tf_op jit(solution)/shard_map/pallas_call | solution.py:123
  (8 shorter events, 0.1 us)
Async XLA Ops:
  0.6 9.7 %collective-permute-start = (bf16[2,64,512]{2,1,0:T(8,128)(2,1)}, bf16[2,64,512]{2,1,0:T(8,128)(2,1)S(1)}, u32[]{:S(2)}, u32[]{:S(2)}) collective-permute-start(bf16[2,64,512]{2,1,0:T(8,128)(2,1)} %bitcast.7), channel_id=1, source_target_pairs={{0,64},{1,66},{2,65},{3,68},{4,67},{5,70},{6,69},{7,72},{8,71},{9,... | collective-permute-start | bytes 393224 | tf_op jit(solution)/shard_map/ppermute | solution.py:58
  7.5 2.9 %collective-permute-start.1 = (bf16[2,64,512]{2,1,0:T(8,128)(2,1)}, bf16[2,64,512]{2,1,0:T(8,128)(2,1)S(1)}, u32[]{:S(2)}, u32[]{:S(2)}) collective-permute-start(bf16[2,64,512]{2,1,0:T(8,128)(2,1)} %bitcast.8), channel_id=1, source_target_pairs={{0,65},{1,64},{2,67},{3,66},{4,69},{5,68},{6,71},{7,70},{8,73},{9,... | collective-permute-start | bytes 393224 | tf_op jit(solution)/shard_map/ppermute | solution.py:58
  7.5 2.9 %collective-permute-start.2 = (bf16[2,64,512]{2,1,0:T(8,128)(2,1)}, bf16[2,64,512]{2,1,0:T(8,128)(2,1)S(1)}, u32[]{:S(2)}, u32[]{:S(2)}) collective-permute-start(bf16[2,64,512]{2,1,0:T(8,128)(2,1)} %bitcast.9), channel_id=1, source_target_pairs={{0,64},{1,65},{2,66},{3,67},{4,68},{5,69},{6,70},{7,71},{8,72},{9,... | collective-permute-start | bytes 393224 | tf_op jit(solution)/shard_map/ppermute | solution.py:58
  8.0 0.9 %copy-start.1 = (bf16[1,2,64,512]{3,2,1,0:T(8,128)(2,1)S(1)}, bf16[1,2,64,512]{3,2,1,0:T(8,128)(2,1)}, u32[]{:S(2)}) copy-start(bf16[1,2,64,512]{3,2,1,0:T(8,128)(2,1)} %param.3) | copy-start | bytes 393220
  10.9 7.7 %copy-start.2 = (bf16[1,2,64,512]{3,2,1,0:T(8,128)(2,1)S(1)}, bf16[1,2,64,512]{3,2,1,0:T(8,128)(2,1)}, u32[]{:S(2)}) copy-start(bf16[1,2,64,512]{3,2,1,0:T(8,128)(2,1)} %param.3) | copy-start | bytes 393220
  11.0 6.2 %collective-permute-start.4 = (bf16[2,64,512]{2,1,0:T(8,128)(2,1)S(1)}, bf16[2,64,512]{2,1,0:T(8,128)(2,1)S(1)}, u32[]{:S(2)}, u32[]{:S(2)}) collective-permute-start(bf16[2,64,512]{2,1,0:T(8,128)(2,1)S(1)} %shard_map.51.after_ref), channel_id=1, source_target_pairs={{64,128},{65,129},{66,130},{67,131},{68,132},{69,133},{70,134},{71... | collective-permute-start | bytes 393224 | tf_op jit(solution)/shard_map/ppermute | solution.py:58
  11.7 6.9 %collective-permute-start.3 = (bf16[2,64,512]{2,1,0:T(8,128)(2,1)S(1)}, bf16[2,64,512]{2,1,0:T(8,128)(2,1)S(1)}, u32[]{:S(2)}, u32[]{:S(2)}) collective-permute-start(bf16[2,64,512]{2,1,0:T(8,128)(2,1)S(1)} %shard_map.51.after_ref), channel_id=1, source_target_pairs={{64,128},{65,130},{66,129},{67,132},{68,131},{69,134},{70,133},{71... | collective-permute-start | bytes 393224 | tf_op jit(solution)/shard_map/ppermute | solution.py:58
  17.2 1.4 %collective-permute-start.5 = (bf16[2,64,512]{2,1,0:T(8,128)(2,1)S(1)}, bf16[2,64,512]{2,1,0:T(8,128)(2,1)S(1)}, u32[]{:S(2)}, u32[]{:S(2)}) collective-permute-start(bf16[2,64,512]{2,1,0:T(8,128)(2,1)S(1)} %collective-permute-done.4.own_ref), channel_id=1, source_target_pairs={{128,129},{129,128},{130,131},{131,130},{132,133},{133,132},{134,1... | collective-permute-start | bytes 393224 | tf_op jit(solution)/shard_map/ppermute | solution.py:58
  19.2 1.4 %collective-permute-start.6 = (bf16[2,64,512]{2,1,0:T(8,128)(2,1)S(1)}, bf16[2,64,512]{2,1,0:T(8,128)(2,1)S(1)}, u32[]{:S(2)}, u32[]{:S(2)}) collective-permute-start(bf16[2,64,512]{2,1,0:T(8,128)(2,1)S(1)} %shard_map.53.after_ref), channel_id=1, source_target_pairs={{128,192},{129,194},{130,193},{131,196},{132,195},{133,198},{134,1... | collective-permute-start | bytes 393224 | tf_op jit(solution)/shard_map/ppermute | solution.py:58
  19.4 1.4 %collective-permute-start.7 = (bf16[2,64,512]{2,1,0:T(8,128)(2,1)S(1)}, bf16[2,64,512]{2,1,0:T(8,128)(2,1)S(1)}, u32[]{:S(2)}, u32[]{:S(2)}) collective-permute-start(bf16[2,64,512]{2,1,0:T(8,128)(2,1)S(1)} %shard_map.53.after_ref), channel_id=1, source_target_pairs={{128,193},{129,192},{130,195},{131,194},{132,197},{133,196},{134,1... | collective-permute-start | bytes 393224 | tf_op jit(solution)/shard_map/ppermute | solution.py:58
  19.8 1.3 %collective-permute-start.8 = (bf16[2,64,512]{2,1,0:T(8,128)(2,1)S(1)}, bf16[2,64,512]{2,1,0:T(8,128)(2,1)S(1)}, u32[]{:S(2)}, u32[]{:S(2)}) collective-permute-start(bf16[2,64,512]{2,1,0:T(8,128)(2,1)S(1)} %shard_map.53.after_ref), channel_id=1, source_target_pairs={{128,192},{129,193},{130,194},{131,195},{132,196},{133,197},{134,1... | collective-permute-start | bytes 393224 | tf_op jit(solution)/shard_map/ppermute | solution.py:58
  21.7 1.4 %collective-permute-start.9 = (bf16[2,64,512]{2,1,0:T(8,128)(2,1)S(1)}, bf16[2,64,512]{2,1,0:T(8,128)(2,1)S(1)}, u32[]{:S(2)}, u32[]{:S(2)}) collective-permute-start(bf16[2,64,512]{2,1,0:T(8,128)(2,1)S(1)} %shard_map.55.after_ref), channel_id=1, source_target_pairs={{192,128},{193,130},{194,129},{195,132},{196,131},{197,134},{198,1... | collective-permute-start | bytes 393224 | tf_op jit(solution)/shard_map/ppermute | solution.py:58
  22.0 1.3 %collective-permute-start.10 = (bf16[2,64,512]{2,1,0:T(8,128)(2,1)S(1)}, bf16[2,64,512]{2,1,0:T(8,128)(2,1)S(1)}, u32[]{:S(2)}, u32[]{:S(2)}) collective-permute-start(bf16[2,64,512]{2,1,0:T(8,128)(2,1)S(1)} %shard_map.55.after_ref), channel_id=1, source_target_pairs={{192,129},{193,128},{194,131},{195,130},{196,133},{197,132},{198,1... | collective-permute-start | bytes 393224 | tf_op jit(solution)/shard_map/ppermute | solution.py:58
  22.3 1.3 %collective-permute-start.11 = (bf16[2,64,512]{2,1,0:T(8,128)(2,1)S(1)}, bf16[2,64,512]{2,1,0:T(8,128)(2,1)S(1)}, u32[]{:S(2)}, u32[]{:S(2)}) collective-permute-start(bf16[2,64,512]{2,1,0:T(8,128)(2,1)S(1)} %shard_map.55.after_ref), channel_id=1, source_target_pairs={{192,128},{193,129},{194,130},{195,131},{196,132},{197,133},{198,1... | collective-permute-start | bytes 393224 | tf_op jit(solution)/shard_map/ppermute | solution.py:58
  22.6 33.8 %copy-start = (bf16[2,64,512]{2,1,0:T(8,128)(2,1)}, bf16[2,64,512]{2,1,0:T(8,128)(2,1)S(1)}, u32[]{:S(2)}) copy-start(bf16[2,64,512]{2,1,0:T(8,128)(2,1)S(1)} %select_select_fusion.1.addend_ref) | copy-start | bytes 393220
  24.3 14.0 %collective-permute-start.13 = (bf16[2,64,512]{2,1,0:T(8,128)(2,1)S(1)}, bf16[2,64,512]{2,1,0:T(8,128)(2,1)S(1)}, u32[]{:S(2)}, u32[]{:S(2)}) collective-permute-start(bf16[2,64,512]{2,1,0:T(8,128)(2,1)S(1)} %shard_map.57.after_ref), channel_id=1, source_target_pairs={{128,64},{129,65},{130,66},{131,67},{132,68},{133,69},{134,70},{13... | collective-permute-start | bytes 393224 | tf_op jit(solution)/shard_map/ppermute | solution.py:58
  35.6 5.5 %collective-permute-start.12 = (bf16[2,64,512]{2,1,0:T(8,128)(2,1)S(1)}, bf16[2,64,512]{2,1,0:T(8,128)(2,1)S(1)}, u32[]{:S(2)}, u32[]{:S(2)}) collective-permute-start(bf16[2,64,512]{2,1,0:T(8,128)(2,1)S(1)} %shard_map.57.after_ref), channel_id=1, source_target_pairs={{128,64},{129,66},{130,65},{131,68},{132,67},{133,70},{134,69},{13... | collective-permute-start | bytes 393224 | tf_op jit(solution)/shard_map/ppermute | solution.py:58
  38.2 5.0 %collective-permute-start.14 = (bf16[2,64,512]{2,1,0:T(8,128)(2,1)S(1)}, bf16[2,64,512]{2,1,0:T(8,128)(2,1)S(1)}, u32[]{:S(2)}, u32[]{:S(2)}) collective-permute-start(bf16[2,64,512]{2,1,0:T(8,128)(2,1)S(1)} %collective-permute-done.13.own_ref), channel_id=1, source_target_pairs={{64,65},{65,64},{66,67},{67,66},{68,69},{69,68},{70,71},{71,70},{7... | collective-permute-start | bytes 393224 | tf_op jit(solution)/shard_map/ppermute | solution.py:58
  43.8 12.6 %collective-permute-start.15 = (bf16[2,64,512]{2,1,0:T(8,128)(2,1)S(1)}, bf16[2,64,512]{2,1,0:T(8,128)(2,1)S(1)}, u32[]{:S(2)}, u32[]{:S(2)}) collective-permute-start(bf16[2,64,512]{2,1,0:T(8,128)(2,1)S(1)} %shard_map.59.after_ref), channel_id=1, source_target_pairs={{64,0},{65,2},{66,1},{67,4},{68,3},{69,6},{70,5},{71,8},{72,7},{73... | collective-permute-start | bytes 393224 | tf_op jit(solution)/shard_map/ppermute | solution.py:58
  51.3 5.0 %collective-permute-start.16 = (bf16[2,64,512]{2,1,0:T(8,128)(2,1)S(1)}, bf16[2,64,512]{2,1,0:T(8,128)(2,1)S(1)}, u32[]{:S(2)}, u32[]{:S(2)}) collective-permute-start(bf16[2,64,512]{2,1,0:T(8,128)(2,1)S(1)} %shard_map.59.after_ref), channel_id=1, source_target_pairs={{64,1},{65,0},{66,3},{67,2},{68,5},{69,4},{70,7},{71,6},{72,9},{73... | collective-permute-start | bytes 393224 | tf_op jit(solution)/shard_map/ppermute | solution.py:58
  51.4 4.9 %collective-permute-start.17 = (bf16[2,64,512]{2,1,0:T(8,128)(2,1)S(1)}, bf16[2,64,512]{2,1,0:T(8,128)(2,1)S(1)}, u32[]{:S(2)}, u32[]{:S(2)}) collective-permute-start(bf16[2,64,512]{2,1,0:T(8,128)(2,1)S(1)} %shard_map.59.after_ref), channel_id=1, source_target_pairs={{64,0},{65,1},{66,2},{67,3},{68,4},{69,5},{70,6},{71,7},{72,8},{73... | collective-permute-start | bytes 393224 | tf_op jit(solution)/shard_map/ppermute | solution.py:58

commit v3 on v2

v3 whole, which is shorter than its diff:
```python
import functools

import jax
import jax.numpy as jnp
from jax import lax
from jax.experimental import pallas as pl
from jax.experimental.pallas import tpu as pltpu
from jax.sharding import PartitionSpec as P

AXES = ("layer", "tile")
VMEM_LIMIT = 16 * 1024 * 1024
FAR_FIRST = ("far", "near", "own")
ORDERS = (FAR_FIRST, FAR_FIRST, ("near", "own", "far"), FAR_FIRST, FAR_FIRST, FAR_FIRST)


def far_mate(tile, tiles):
    mate = tile + 1 if tile % 2 else tile - 1
    return mate if 0 <= mate < tiles else tile


def near_mate(tile, tiles):
    return tile - 1 if tile % 2 else tile + 1


def same(tile, tiles):
    return tile


def mirror(tile, tiles):
    x, z, y = tile // 16, tile // 4 % 4, tile % 4
    return 16 * x + 4 * (3 - z) + y


def at_seam(tile, tiles):
    return tile // 16 != far_mate(tile, tiles) // 16


def pairs_of(route, tiles, select=lambda tile, tiles: True):
    return [
        (source * tiles + tile, target * tiles + mate(tile, tiles))
        for source, target, mate in route
        for tile in range(tiles)
        if select(tile, tiles)
    ]


def within_chip(source, target, mate):
    one, two = [layer for layer in range(4) if layer not in (source, target)]
    return ((source, target, mate), (target, source, same), (one, two, same), (two, one, same))


def across(source, target):
    return (
        (source, target, same),
        (target, target ^ 1, same),
        (target ^ 1, source ^ 1, mirror),
        (source ^ 1, source, same),
    )


ON_CHIP = ((0, 1, same), (1, 0, same), (2, 3, same), (3, 2, same))


def inner_mate(tile, tiles):
    return tile if at_seam(tile, tiles) else far_mate(tile, tiles)


def over_seam(source, target, tiles):
    route = (
        (source, target, far_mate),
        (target, target ^ 1, same),
        (target ^ 1, source ^ 1, far_mate),
        (source ^ 1, source, same),
    )
    return pairs_of(route, tiles, at_seam) + pairs_of(ON_CHIP, tiles, lambda *tile: not at_seam(*tile))


def permute(values, pairs):
    return lax.ppermute(values, AXES, pairs)


def load_kernel(layers, blocks_ref, after_ref, held_ref, sems):
    here = lax.axis_index("layer")

    @pl.when(functools.reduce(jnp.logical_or, [here == layer for layer in layers]))
    def _():
        count, parts = blocks_ref.shape[:2]
        copies = [
            pltpu.make_async_copy(blocks_ref.at[i, j], held_ref.at[i, j], sems.at[i, j])
            for i in range(count)
            for j in range(parts)
        ]
        for copy in copies:
            copy.start()
        for copy in copies:
            copy.wait()


def load(blocks, after, *layers):
    return pl.pallas_call(
        functools.partial(load_kernel, layers),
        out_shape=pltpu.VMEM(blocks.shape, blocks.dtype),
        in_specs=[pl.BlockSpec(memory_space=pl.ANY)] * 2,
        out_specs=pl.BlockSpec(memory_space=pltpu.VMEM),
        scratch_shapes=[pltpu.SemaphoreType.DMA(blocks.shape[:2])],
        compiler_params=pltpu.CompilerParams(vmem_limit_bytes=VMEM_LIMIT),
        cost_estimate=pl.CostEstimate(flops=0, bytes_accessed=blocks.size * 4, transcendentals=0),
    )(pltpu.with_memory_space_constraint(blocks, pltpu.HBM), after)


def step_kernel(layer, names, *refs):
    *refs, out_ref = refs
    refs = dict(zip(names, refs))
    here = lax.axis_index("layer") == layer

    if "kept" in refs:

        @pl.when(jnp.logical_not(here))
        def _():
            out_ref[...] = refs["kept"][...]

    @pl.when(here)
    def _():
        product_and_sum(refs, out_ref)


def product_and_sum(refs, out_ref):
    own_ref, near_ref, far_ref = refs["own"], refs["near"], refs["far"]
    blocks_ref, addend_ref = refs["blocks"], refs["addend"]
    tiles = lax.axis_size("tile")
    tile = lax.axis_index("tile")
    odd = lax.rem(tile, 2)
    rows, cells = own_ref.shape[1:]
    edge = jnp.logical_or(tile == 0, tile == tiles - 1)

    def stacked(ref):
        return ref[...].reshape(2 * rows, cells)

    def product(values, number):
        by_real = jnp.dot(values, blocks_ref[number, 0], preferred_element_type=jnp.float32)
        by_imag = jnp.dot(values, blocks_ref[number, 1], preferred_element_type=jnp.float32)
        return by_real, by_imag

    far = stacked(far_ref)
    if "seam" in refs:
        place = lax.rem(tile, tiles // 4)
        far = jnp.where(jnp.logical_or(place == 0, place == tiles // 4 - 1), stacked(refs["seam"]), far)
    far = jnp.where(edge, jnp.zeros_like(far), far)
    own_real, own_imag = product(stacked(own_ref), 0)
    near_real, near_imag = product(stacked(near_ref), 2 - odd)
    far_real, far_imag = product(far, 1 + odd)
    by_real = own_real + near_real + far_real
    by_imag = own_imag + near_imag + far_imag
    real = (by_real[:rows] - by_imag[rows:] + addend_ref[0].astype(jnp.float32)).astype(out_ref.dtype)
    imag = (by_imag[:rows] + by_real[rows:] + addend_ref[1].astype(jnp.float32)).astype(out_ref.dtype)
    out_ref[0] = real
    out_ref[1] = imag


def step(layer, **operands):
    vmem = pl.BlockSpec(memory_space=pltpu.VMEM)
    addend = operands["addend"]
    return pl.pallas_call(
        functools.partial(step_kernel, layer, tuple(operands)),
        out_shape=jax.ShapeDtypeStruct(addend.shape, addend.dtype),
        in_specs=[vmem] * len(operands),
        out_specs=vmem,
        compiler_params=pltpu.CompilerParams(vmem_limit_bytes=VMEM_LIMIT),
        cost_estimate=pl.CostEstimate(
            flops=24 * addend.shape[1] * addend.shape[2] * addend.shape[2],
            bytes_accessed=operands["blocks"].size * 2 + addend.size * 10,
            transcendentals=0,
        ),
    )(*operands.values())


def spread(values, source, target, far, order):
    tiles = lax.axis_size("tile")
    mates = {"far": far, "near": near_mate, "own": same}
    return {name: permute(values, pairs_of(within_chip(source, target, mates[name]), tiles)) for name in order}


def hop(values, source, target, blocks, order, after=None, **rest):
    arrived = spread(values, source, target, far_mate, order)
    held = load(blocks, values if after is None else after, target)
    return step(target, **arrived, blocks=held, **rest)


def crossing_hop(values, source, target, blocks, order, **rest):
    tiles = lax.axis_size("tile")
    crossed = permute(values, pairs_of(across(source, target ^ 1), tiles))
    seam = permute(values, over_seam(source, target, tiles))
    arrived = spread(crossed, target ^ 1, target, inner_mate, order)
    return step(target, **arrived, seam=seam, blocks=load(blocks, values, target), **rest)


def per_device(sources, down_blocks, up_blocks):
    layer = lax.axis_index("layer")
    source, down, up = sources[0], down_blocks[0], up_blocks[0]
    down_1 = hop(source, 0, 1, down, ORDERS[0], addend=source)
    down_2 = crossing_hop(down_1, 1, 2, down, ORDERS[1], addend=source)
    down_3 = hop(down_2, 2, 3, down, ORDERS[2], addend=source)
    falling = jnp.where(layer == 0, source, jnp.where(layer == 1, down_1, jnp.where(layer == 2, down_2, down_3)))
    up_2 = hop(down_3, 3, 2, up, ORDERS[3], addend=down_2)
    up_1 = crossing_hop(up_2, 2, 1, up, ORDERS[4], addend=down_1)
    rising = jnp.where(layer == 1, up_1, jnp.where(layer == 2, up_2, down_3))
    rising = hop(up_1, 1, 0, up, ORDERS[5], down_3, addend=source, kept=rising)
    return (falling[None], rising[None])


def solution(mesh):
    return jax.shard_map(
        per_device,
        mesh=mesh,
        in_specs=(
            P("layer", None, None, "tile"),
            P("layer", None, None, "tile", None),
            P("layer", None, None, "tile", None),
        ),
        out_specs=(P("layer", None, None, "tile"), P("layer", None, None, "tile")),
        check_vma=False,
    )
```

time: 57.7 us -> 57 us (0.988)
  Pallas kernels: 6.29 us -> 3.45 us
  waiting for transfers between devices: 17.7 us -> 19.1 us
  other arithmetic: 0.05 us -> 0.69 us
    pallas_call x12, Pallas kernels: 6.29 us -> 3.45 us  [the longest x6 2.17 us: load(): pl.pallas_call(functools.partial(load_kernel, layers), out_shape=pltpu.VM...]
    ppermute x18 -> x22, waiting for transfers between devices: 17.7 us -> 19.1 us  [permute(): return lax.ppermute(values, AXES, pairs)]
    select_n x2 -> x1, other arithmetic: 0.05 us -> 0.69 us  [per_device(): rising = jnp.where(layer == 1, up_1, jnp.where(layer == 2, up_2, down_3))]
    ppermute x18 -> x22, starting transfers between devices: 31.9 us -> 32 us  [permute(): return lax.ppermute(values, AXES, pairs)]
  transfers between devices with their start and end apart: 18 -> 22, of which waited for: 12 -> 11; matrix products, arithmetic and copies ran while one was open for 0% -> 1% of each run, Pallas kernels for 4% -> 4%
where the time goes in v3:
time: 57 us; the launch traced here: 56.9 us
  starting transfers between devices  32 us (56%)
  waiting for transfers between devices  19.1 us (34%)
  Pallas kernels  3.45 us (6%)
  local copies, waits for them, and re-layouts  0.91 us (2%)
  between operations  0.75 us (1%)
  other arithmetic  0.69 us (1%)
    ppermute x22, starting transfers between devices, permute(): return lax.ppermute(values, AXES, pairs)  32 us
    ppermute x22, waiting for transfers between devices, permute(): return lax.ppermute(values, AXES, pairs)  19.1 us
    pallas_call x6, Pallas kernels, load(): pl.pallas_call(functools.partial(load_kernel, layers), out_shape=pltpu.VM...  2.17 us
    pallas_call x6, Pallas kernels, step(): pl.pallas_call(functools.partial(step_kernel, layer, tuple(operands)), ou...  1.28 us
  transfers between devices with their start and end apart: 22, of which 11 were waited for; matrix products, arithmetic and copies ran while one was open for 1% of the time, Pallas kernels for 4%

profile of v3, /device:TPU:6, one launch (start us, length us, event | category | flops | bytes accessed | tf_op | source)
XLA Modules:
  0.0 56.9 jit_solution(5476338069991073670)
XLA Ops:
  0.6 6.9 %collective-permute-start = (bf16[2,64,512]{2,1,0:T(8,128)(2,1)}, bf16[2,64,512]{2,1,0:T(8,128)(2,1)S(1)}, u32[]{:S(2)}, u32[]{:S(2)}) collective-permute-start(bf16[2,64,512]{2,1,0:T(8,128)(2,1)} %bitcast.7), channel_id=1, source_target_pairs={{0,64},{1,66},{2,65},{3,68},{4,67},{5,70},{6,69},{7,72},{8,71},{9,... | collective-permute-start | bytes 393224 | tf_op jit(solution)/shard_map/ppermute | solution.py:79
  7.5 0.0 collective-permute-start.1
  7.5 0.5 collective-permute-start.2
  8.0 0.9 %copy-done = bf16[1,2,64,512]{3,2,1,0:T(8,128)(2,1)S(1)} copy-done((bf16[1,2,64,512]{3,2,1,0:T(8,128)(2,1)S(1)}, bf16[1,2,64,512]{3,2,1,0:T(8,128)(2,1)}, u32[]{:S(2)}) %copy-start) | copy-done | bytes 131096
  8.9 0.1 shard_map.50.refs_3_
  9.0 1.4 %collective-permute-done.refs_0_ = bf16[2,64,512]{2,1,0:T(8,128)(2,1)S(1)} collective-permute-done((bf16[2,64,512]{2,1,0:T(8,128)(2,1)}, bf16[2,64,512]{2,1,0:T(8,128)(2,1)S(1)}, u32[]{:S(2)}, u32[]{:S(2)}) %collective-permute-start) | collective-permute-done | bytes 131104 | tf_op jit(solution)/shard_map/ppermute | solution.py:79
  10.3 0.0 collective-permute-done.1.refs_1_
  10.4 0.0 collective-permute-done.2.refs_2_
  10.4 1.4 %collective-permute-start.3 = (bf16[2,64,512]{2,1,0:T(8,128)(2,1)S(1)}, bf16[2,64,512]{2,1,0:T(8,128)(2,1)S(1)}, u32[]{:S(2)}, u32[]{:S(2)}) collective-permute-start(bf16[2,64,512]{2,1,0:T(8,128)(2,1)S(1)} %shard_map.51.after_ref.refs_5_), channel_id=1, source_target_pairs={{64,192},{65,193},{66,194},{67,195},{68,196},{69,197},{70,198},{71... | collective-permute-start | bytes 393224 | tf_op jit(solution)/shard_map/ppermute | solution.py:79
  11.7 0.1 collective-permute-start.7
  11.8 4.8 %collective-permute-done.3 = bf16[2,64,512]{2,1,0:T(8,128)(2,1)S(1)} collective-permute-done((bf16[2,64,512]{2,1,0:T(8,128)(2,1)S(1)}, bf16[2,64,512]{2,1,0:T(8,128)(2,1)S(1)}, u32[]{:S(2)}, u32[]{:S(2)}) %collective-permute-start.3) | collective-permute-done | bytes 131104 | tf_op jit(solution)/shard_map/ppermute | solution.py:79
  16.6 0.0 collective-permute-start.4
  16.6 0.5 collective-permute-start.5
  17.1 0.0 collective-permute-start.6
  17.1 0.1 shard_map.52.refs_4_
  17.2 3.2 %collective-permute-done.7.refs_3_ = bf16[2,64,512]{2,1,0:T(8,128)(2,1)S(1)} collective-permute-done((bf16[2,64,512]{2,1,0:T(8,128)(2,1)S(1)}, bf16[2,64,512]{2,1,0:T(8,128)(2,1)S(1)}, u32[]{:S(2)}, u32[]{:S(2)}) %collective-permute-start.7) | collective-permute-done | bytes 131104 | tf_op jit(solution)/shard_map/ppermute | solution.py:79
  20.3 0.0 collective-permute-done.4.refs_0_
  20.3 0.0 collective-permute-done.5.refs_1_
  20.4 0.1 collective-permute-start.10
  20.5 0.5 collective-permute-start.8
  21.0 0.1 collective-permute-start.9
  21.1 0.1 shard_map.54.refs_3_
  21.1 0.7 %collective-permute-done.10.refs_2_ = bf16[2,64,512]{2,1,0:T(8,128)(2,1)S(1)} collective-permute-done((bf16[2,64,512]{2,1,0:T(8,128)(2,1)S(1)}, bf16[2,64,512]{2,1,0:T(8,128)(2,1)S(1)}, u32[]{:S(2)}, u32[]{:S(2)}) %collective-permute-start.10) | collective-permute-done | bytes 131104 | tf_op jit(solution)/shard_map/ppermute | solution.py:79
  21.8 0.2 collective-permute-done.8.refs_0_
  22.0 0.3 collective-permute-done.9.refs_1_
  22.3 0.2 collective-permute-start.11
  22.5 0.3 collective-permute-start.12
  22.8 0.2 collective-permute-start.13
  23.0 0.1 shard_map.56.refs_3_
  23.1 0.6 %collective-permute-done.11.refs_0_ = bf16[2,64,512]{2,1,0:T(8,128)(2,1)S(1)} collective-permute-done((bf16[2,64,512]{2,1,0:T(8,128)(2,1)S(1)}, bf16[2,64,512]{2,1,0:T(8,128)(2,1)S(1)}, u32[]{:S(2)}, u32[]{:S(2)}) %collective-permute-start.11) | collective-permute-done | bytes 131104 | tf_op jit(solution)/shard_map/ppermute | solution.py:79
  23.7 0.2 collective-permute-done.12.refs_1_
  23.9 0.3 collective-permute-done.13.refs_2_
  24.2 0.2 collective-permute-start.14
  24.4 16.8 %collective-permute-start.18 = (bf16[2,64,512]{2,1,0:T(8,128)(2,1)S(1)}, bf16[2,64,512]{2,1,0:T(8,128)(2,1)S(1)}, u32[]{:S(2)}, u32[]{:S(2)}) collective-permute-start(bf16[2,64,512]{2,1,0:T(8,128)(2,1)S(1)} %shard_map.57.after_ref), channel_id=1, source_target_pairs={{143,80},{144,79},{159,96},{160,95},{175,112},{176,111},{79,15},{8... | collective-permute-start | bytes 393224 | tf_op jit(solution)/shard_map/ppermute | solution.py:79
  41.2 2.6 %collective-permute-done.14 = bf16[2,64,512]{2,1,0:T(8,128)(2,1)S(1)} collective-permute-done((bf16[2,64,512]{2,1,0:T(8,128)(2,1)S(1)}, bf16[2,64,512]{2,1,0:T(8,128)(2,1)S(1)}, u32[]{:S(2)}, u32[]{:S(2)}) %collective-permute-start.14) | collective-permute-done | bytes 131104 | tf_op jit(solution)/shard_map/ppermute | solution.py:79
  43.8 0.5 collective-permute-start.17
  44.3 1.9 %shard_map.60.refs_3_ = bf16[3,2,512,512]{3,2,1,0:T(8,128)(2,1)S(1)} custom-call(bf16[3,2,512,512]{3,2,1,0:T(8,128)(2,1)} %bitcast.19, bf16[2,64,512]{2,1,0:T(8,128)(2,1)S(1)} %shard_map.55.after_ref), custom_call_target="tpu_custom_call" | custom-call | bytes 6291456 | tf_op jit(solution)/shard_map/pallas_call | solution.py:100
  46.2 0.1 shard_map.58.refs_4_
  46.3 0.0 collective-permute-done.15.refs_0_
  46.3 0.0 collective-permute-done.16.refs_1_
  46.4 3.0 %collective-permute-start.19 = (bf16[2,64,512]{2,1,0:T(8,128)(2,1)S(1)}, bf16[2,64,512]{2,1,0:T(8,128)(2,1)S(1)}, u32[]{:S(2)}, u32[]{:S(2)}) collective-permute-start(bf16[2,64,512]{2,1,0:T(8,128)(2,1)S(1)} %shard_map.59), channel_id=1, source_target_pairs={{64,0},{65,2},{66,1},{67,4},{68,3},{69,6},{70,5},{71,8},{72,7},{73... | collective-permute-start | bytes 393224 | tf_op jit(solution)/shard_map/ppermute | solution.py:79
  49.4 0.7 %collective-permute-start.20 = (bf16[2,64,512]{2,1,0:T(8,128)(2,1)S(1)}, bf16[2,64,512]{2,1,0:T(8,128)(2,1)S(1)}, u32[]{:S(2)}, u32[]{:S(2)}) collective-permute-start(bf16[2,64,512]{2,1,0:T(8,128)(2,1)S(1)} %shard_map.59), channel_id=1, source_target_pairs={{64,1},{65,0},{66,3},{67,2},{68,5},{69,4},{70,7},{71,6},{72,9},{73... | collective-permute-start | bytes 393224 | tf_op jit(solution)/shard_map/ppermute | solution.py:79
  50.1 0.0 collective-permute-start.21
  50.1 0.7 %select_select_fusion = (bf16[2,64,512]{2,1,0:T(8,128)(2,1)S(1)}, bf16[1,2,64,512]{3,2,1,0:T(8,128)(2,1)}) fusion(bf16[2,64,512]{2,1,0:T(8,128)(2,1)S(1)} %shard_map.59, bf16[2,64,512]{2,1,0:T(8,128)(2,1)S(1)} %shard_map.57.after_ref, bf16[2,64,512]{2,1,0:T(8,128)(2,1)S(1)} %shard_map.55.after_ref, pred[]{:T(512)S(6)} %eq.13, pred[]{:T(512)S(6)} %eq.12, ...), kind=kLoop, calls=%fused_computation | loop fusion | flops 327680 | bytes 1048579 | tf_op jit(solution)/shard_map/jit(_where)/select_n | solution.py:206
  50.8 4.9 %collective-permute-done.19.refs_0_ = bf16[2,64,512]{2,1,0:T(8,128)(2,1)S(1)} collective-permute-done((bf16[2,64,512]{2,1,0:T(8,128)(2,1)S(1)}, bf16[2,64,512]{2,1,0:T(8,128)(2,1)S(1)}, u32[]{:S(2)}, u32[]{:S(2)}) %collective-permute-start.19) | collective-permute-done | bytes 131104 | tf_op jit(solution)/shard_map/ppermute | solution.py:79
  55.6 0.0 collective-permute-done.20.refs_1_
  55.6 0.0 collective-permute-done.21.refs_2_
  55.6 1.2 %shard_map.61 = bf16[2,64,512]{2,1,0:T(8,128)(2,1)} custom-call(bf16[2,64,512]{2,1,0:T(8,128)(2,1)S(1)} %collective-permute-done.19.refs_0_, bf16[2,64,512]{2,1,0:T(8,128)(2,1)S(1)} %collective-permute-done.20.refs_1_, bf16[2,64,512]{2,1,0:T(8,128)(2,1)S(1)} %collective-permute-done.21.refs_2_, bf16[3,2,512,512]{3,2,1,0:T(8,128)(2,1)S(1)} %shard_map.60.refs_3_, ...), custom_call_target="tpu_custom_call" | custom-call | flops 402653184 | bytes 3801088 | tf_op jit(solution)/shard_map/pallas_call | solution.py:163
  (13 shorter events, 0.1 us)
Async XLA Ops:
  0.6 9.7 %collective-permute-start = (bf16[2,64,512]{2,1,0:T(8,128)(2,1)}, bf16[2,64,512]{2,1,0:T(8,128)(2,1)S(1)}, u32[]{:S(2)}, u32[]{:S(2)}) collective-permute-start(bf16[2,64,512]{2,1,0:T(8,128)(2,1)} %bitcast.7), channel_id=1, source_target_pairs={{0,64},{1,66},{2,65},{3,68},{4,67},{5,70},{6,69},{7,72},{8,71},{9,... | collective-permute-start | bytes 393224 | tf_op jit(solution)/shard_map/ppermute | solution.py:79
  7.5 2.9 %collective-permute-start.1 = (bf16[2,64,512]{2,1,0:T(8,128)(2,1)}, bf16[2,64,512]{2,1,0:T(8,128)(2,1)S(1)}, u32[]{:S(2)}, u32[]{:S(2)}) collective-permute-start(bf16[2,64,512]{2,1,0:T(8,128)(2,1)} %bitcast.8), channel_id=1, source_target_pairs={{0,65},{1,64},{2,67},{3,66},{4,69},{5,68},{6,71},{7,70},{8,73},{9,... | collective-permute-start | bytes 393224 | tf_op jit(solution)/shard_map/ppermute | solution.py:79
  7.5 2.9 %collective-permute-start.2 = (bf16[2,64,512]{2,1,0:T(8,128)(2,1)}, bf16[2,64,512]{2,1,0:T(8,128)(2,1)S(1)}, u32[]{:S(2)}, u32[]{:S(2)}) collective-permute-start(bf16[2,64,512]{2,1,0:T(8,128)(2,1)} %bitcast.9), channel_id=1, source_target_pairs={{0,64},{1,65},{2,66},{3,67},{4,68},{5,69},{6,70},{7,71},{8,72},{9,... | collective-permute-start | bytes 393224 | tf_op jit(solution)/shard_map/ppermute | solution.py:79
  8.0 0.9 %copy-start = (bf16[1,2,64,512]{3,2,1,0:T(8,128)(2,1)S(1)}, bf16[1,2,64,512]{3,2,1,0:T(8,128)(2,1)}, u32[]{:S(2)}) copy-start(bf16[1,2,64,512]{3,2,1,0:T(8,128)(2,1)} %param.3) | copy-start | bytes 393220
  10.4 10.0 %copy-start.1 = (bf16[1,2,64,512]{3,2,1,0:T(8,128)(2,1)S(1)}, bf16[1,2,64,512]{3,2,1,0:T(8,128)(2,1)}, u32[]{:S(2)}) copy-start(bf16[1,2,64,512]{3,2,1,0:T(8,128)(2,1)} %param.3) | copy-start | bytes 393220
  10.4 6.2 %collective-permute-start.3 = (bf16[2,64,512]{2,1,0:T(8,128)(2,1)S(1)}, bf16[2,64,512]{2,1,0:T(8,128)(2,1)S(1)}, u32[]{:S(2)}, u32[]{:S(2)}) collective-permute-start(bf16[2,64,512]{2,1,0:T(8,128)(2,1)S(1)} %shard_map.51.after_ref.refs_5_), channel_id=1, source_target_pairs={{64,192},{65,193},{66,194},{67,195},{68,196},{69,197},{70,198},{71... | collective-permute-start | bytes 393224 | tf_op jit(solution)/shard_map/ppermute | solution.py:79
  11.7 8.6 %collective-permute-start.7 = (bf16[2,64,512]{2,1,0:T(8,128)(2,1)S(1)}, bf16[2,64,512]{2,1,0:T(8,128)(2,1)S(1)}, u32[]{:S(2)}, u32[]{:S(2)}) collective-permute-start(bf16[2,64,512]{2,1,0:T(8,128)(2,1)S(1)} %shard_map.51.after_ref.refs_5_), channel_id=1, source_target_pairs={{79,144},{80,143},{95,160},{96,159},{111,176},{112,175},{143,207},... | collective-permute-start | bytes 393224 | tf_op jit(solution)/shard_map/ppermute | solution.py:79
  16.6 3.7 %collective-permute-start.4 = (bf16[2,64,512]{2,1,0:T(8,128)(2,1)S(1)}, bf16[2,64,512]{2,1,0:T(8,128)(2,1)S(1)}, u32[]{:S(2)}, u32[]{:S(2)}) collective-permute-start(bf16[2,64,512]{2,1,0:T(8,128)(2,1)S(1)} %collective-permute-done.3), channel_id=1, source_target_pairs={{192,128},{193,130},{194,129},{195,132},{196,131},{197,134},{198,1... | collective-permute-start | bytes 393224 | tf_op jit(solution)/shard_map/ppermute | solution.py:79
  16.6 3.7 %collective-permute-start.5 = (bf16[2,64,512]{2,1,0:T(8,128)(2,1)S(1)}, bf16[2,64,512]{2,1,0:T(8,128)(2,1)S(1)}, u32[]{:S(2)}, u32[]{:S(2)}) collective-permute-start(bf16[2,64,512]{2,1,0:T(8,128)(2,1)S(1)} %collective-permute-done.3), channel_id=1, source_target_pairs={{192,129},{193,128},{194,131},{195,130},{196,133},{197,132},{198,1... | collective-permute-start | bytes 393224 | tf_op jit(solution)/shard_map/ppermute | solution.py:79
  17.1 3.2 %collective-permute-start.6 = (bf16[2,64,512]{2,1,0:T(8,128)(2,1)S(1)}, bf16[2,64,512]{2,1,0:T(8,128)(2,1)S(1)}, u32[]{:S(2)}, u32[]{:S(2)}) collective-permute-start(bf16[2,64,512]{2,1,0:T(8,128)(2,1)S(1)} %collective-permute-done.3), channel_id=1, source_target_pairs={{192,128},{193,129},{194,130},{195,131},{196,132},{197,133},{198,1... | collective-permute-start | bytes 393224 | tf_op jit(solution)/shard_map/ppermute | solution.py:79
  20.4 1.4 %collective-permute-start.10 = (bf16[2,64,512]{2,1,0:T(8,128)(2,1)S(1)}, bf16[2,64,512]{2,1,0:T(8,128)(2,1)S(1)}, u32[]{:S(2)}, u32[]{:S(2)}) collective-permute-start(bf16[2,64,512]{2,1,0:T(8,128)(2,1)S(1)} %shard_map.53.after_ref.refs_4_), channel_id=1, source_target_pairs={{128,192},{129,194},{130,193},{131,196},{132,195},{133,198},{134,1... | collective-permute-start | bytes 393224 | tf_op jit(solution)/shard_map/ppermute | solution.py:79
  20.5 1.5 %collective-permute-start.8 = (bf16[2,64,512]{2,1,0:T(8,128)(2,1)S(1)}, bf16[2,64,512]{2,1,0:T(8,128)(2,1)S(1)}, u32[]{:S(2)}, u32[]{:S(2)}) collective-permute-start(bf16[2,64,512]{2,1,0:T(8,128)(2,1)S(1)} %shard_map.53.after_ref.refs_4_), channel_id=1, source_target_pairs={{128,193},{129,192},{130,195},{131,194},{132,197},{133,196},{134,1... | collective-permute-start | bytes 393224 | tf_op jit(solution)/shard_map/ppermute | solution.py:79
  21.0 1.3 %collective-permute-start.9 = (bf16[2,64,512]{2,1,0:T(8,128)(2,1)S(1)}, bf16[2,64,512]{2,1,0:T(8,128)(2,1)S(1)}, u32[]{:S(2)}, u32[]{:S(2)}) collective-permute-start(bf16[2,64,512]{2,1,0:T(8,128)(2,1)S(1)} %shard_map.53.after_ref.refs_4_), channel_id=1, source_target_pairs={{128,192},{129,193},{130,194},{131,195},{132,196},{133,197},{134,1... | collective-permute-start | bytes 393224 | tf_op jit(solution)/shard_map/ppermute | solution.py:79
  22.3 1.3 %collective-permute-start.11 = (bf16[2,64,512]{2,1,0:T(8,128)(2,1)S(1)}, bf16[2,64,512]{2,1,0:T(8,128)(2,1)S(1)}, u32[]{:S(2)}, u32[]{:S(2)}) collective-permute-start(bf16[2,64,512]{2,1,0:T(8,128)(2,1)S(1)} %shard_map.55.after_ref), channel_id=1, source_target_pairs={{192,128},{193,130},{194,129},{195,132},{196,131},{197,134},{198,1... | collective-permute-start | bytes 393224 | tf_op jit(solution)/shard_map/ppermute | solution.py:79
  22.5 1.3 %collective-permute-start.12 = (bf16[2,64,512]{2,1,0:T(8,128)(2,1)S(1)}, bf16[2,64,512]{2,1,0:T(8,128)(2,1)S(1)}, u32[]{:S(2)}, u32[]{:S(2)}) collective-permute-start(bf16[2,64,512]{2,1,0:T(8,128)(2,1)S(1)} %shard_map.55.after_ref), channel_id=1, source_target_pairs={{192,129},{193,128},{194,131},{195,130},{196,133},{197,132},{198,1... | collective-permute-start | bytes 393224 | tf_op jit(solution)/shard_map/ppermute | solution.py:79
  22.8 1.3 %collective-permute-start.13 = (bf16[2,64,512]{2,1,0:T(8,128)(2,1)S(1)}, bf16[2,64,512]{2,1,0:T(8,128)(2,1)S(1)}, u32[]{:S(2)}, u32[]{:S(2)}) collective-permute-start(bf16[2,64,512]{2,1,0:T(8,128)(2,1)S(1)} %shard_map.55.after_ref), channel_id=1, source_target_pairs={{192,128},{193,129},{194,130},{195,131},{196,132},{197,133},{198,1... | collective-permute-start | bytes 393224 | tf_op jit(solution)/shard_map/ppermute | solution.py:79
  24.2 19.6 %collective-permute-start.14 = (bf16[2,64,512]{2,1,0:T(8,128)(2,1)S(1)}, bf16[2,64,512]{2,1,0:T(8,128)(2,1)S(1)}, u32[]{:S(2)}, u32[]{:S(2)}) collective-permute-start(bf16[2,64,512]{2,1,0:T(8,128)(2,1)S(1)} %shard_map.57.after_ref), channel_id=1, source_target_pairs={{128,0},{129,1},{130,2},{131,3},{132,4},{133,5},{134,6},{135,7},{1... | collective-permute-start | bytes 393224 | tf_op jit(solution)/shard_map/ppermute | solution.py:79
  24.4 21.9 %collective-permute-start.18 = (bf16[2,64,512]{2,1,0:T(8,128)(2,1)S(1)}, bf16[2,64,512]{2,1,0:T(8,128)(2,1)S(1)}, u32[]{:S(2)}, u32[]{:S(2)}) collective-permute-start(bf16[2,64,512]{2,1,0:T(8,128)(2,1)S(1)} %shard_map.57.after_ref), channel_id=1, source_target_pairs={{143,80},{144,79},{159,96},{160,95},{175,112},{176,111},{79,15},{8... | collective-permute-start | bytes 393224 | tf_op jit(solution)/shard_map/ppermute | solution.py:79
  43.8 2.5 %collective-permute-start.15 = (bf16[2,64,512]{2,1,0:T(8,128)(2,1)S(1)}, bf16[2,64,512]{2,1,0:T(8,128)(2,1)S(1)}, u32[]{:S(2)}, u32[]{:S(2)}) collective-permute-start(bf16[2,64,512]{2,1,0:T(8,128)(2,1)S(1)} %collective-permute-done.14), channel_id=1, source_target_pairs={{0,64},{1,66},{2,65},{3,68},{4,67},{5,70},{6,69},{7,72},{8,71},{9,... | collective-permute-start | bytes 393224 | tf_op jit(solution)/shard_map/ppermute | solution.py:79
  43.8 2.5 %collective-permute-start.16 = (bf16[2,64,512]{2,1,0:T(8,128)(2,1)S(1)}, bf16[2,64,512]{2,1,0:T(8,128)(2,1)S(1)}, u32[]{:S(2)}, u32[]{:S(2)}) collective-permute-start(bf16[2,64,512]{2,1,0:T(8,128)(2,1)S(1)} %collective-permute-done.14), channel_id=1, source_target_pairs={{0,65},{1,64},{2,67},{3,66},{4,69},{5,68},{6,71},{7,70},{8,73},{9,... | collective-permute-start | bytes 393224 | tf_op jit(solution)/shard_map/ppermute | solution.py:79
  43.8 2.5 %collective-permute-start.17 = (bf16[2,64,512]{2,1,0:T(8,128)(2,1)S(1)}, bf16[2,64,512]{2,1,0:T(8,128)(2,1)S(1)}, u32[]{:S(2)}, u32[]{:S(2)}) collective-permute-start(bf16[2,64,512]{2,1,0:T(8,128)(2,1)S(1)} %collective-permute-done.14), channel_id=1, source_target_pairs={{0,64},{1,65},{2,66},{3,67},{4,68},{5,69},{6,70},{7,71},{8,72},{9,... | collective-permute-start | bytes 393224 | tf_op jit(solution)/shard_map/ppermute | solution.py:79
  46.4 9.3 %collective-permute-start.19 = (bf16[2,64,512]{2,1,0:T(8,128)(2,1)S(1)}, bf16[2,64,512]{2,1,0:T(8,128)(2,1)S(1)}, u32[]{:S(2)}, u32[]{:S(2)}) collective-permute-start(bf16[2,64,512]{2,1,0:T(8,128)(2,1)S(1)} %shard_map.59), channel_id=1, source_target_pairs={{64,0},{65,2},{66,1},{67,4},{68,3},{69,6},{70,5},{71,8},{72,7},{73... | collective-permute-start | bytes 393224 | tf_op jit(solution)/shard_map/ppermute | solution.py:79
  49.4 6.3 %collective-permute-start.20 = (bf16[2,64,512]{2,1,0:T(8,128)(2,1)S(1)}, bf16[2,64,512]{2,1,0:T(8,128)(2,1)S(1)}, u32[]{:S(2)}, u32[]{:S(2)}) collective-permute-start(bf16[2,64,512]{2,1,0:T(8,128)(2,1)S(1)} %shard_map.59), channel_id=1, source_target_pairs={{64,1},{65,0},{66,3},{67,2},{68,5},{69,4},{70,7},{71,6},{72,9},{73... | collective-permute-start | bytes 393224 | tf_op jit(solution)/shard_map/ppermute | solution.py:79
  50.1 5.6 %collective-permute-start.21 = (bf16[2,64,512]{2,1,0:T(8,128)(2,1)S(1)}, bf16[2,64,512]{2,1,0:T(8,128)(2,1)S(1)}, u32[]{:S(2)}, u32[]{:S(2)}) collective-permute-start(bf16[2,64,512]{2,1,0:T(8,128)(2,1)S(1)} %shard_map.59), channel_id=1, source_target_pairs={{64,0},{65,1},{66,2},{67,3},{68,4},{69,5},{70,6},{71,7},{72,8},{73... | collective-permute-start | bytes 393224 | tf_op jit(solution)/shard_map/ppermute | solution.py:79

commit v4 on v3

--- a/solution.py
+++ b/solution.py
@@ -10,7 +10,7 @@
 AXES = ("layer", "tile")
 VMEM_LIMIT = 16 * 1024 * 1024
 FAR_FIRST = ("far", "near", "own")
-ORDERS = (FAR_FIRST, FAR_FIRST, ("near", "own", "far"), FAR_FIRST, FAR_FIRST, FAR_FIRST)
+ORDERS = (FAR_FIRST, FAR_FIRST, ("own", "far", "near"), FAR_FIRST, FAR_FIRST, FAR_FIRST)
 
 
 def far_mate(tile, tiles):
@@ -33,6 +33,22 @@
 
 def at_seam(tile, tiles):
     return tile // 16 != far_mate(tile, tiles) // 16
+
+
+def by_seam(tile, tiles):
+    return at_seam(tile, tiles) or at_seam(near_mate(tile, tiles), tiles)
+
+
+def inner_mate(tile, tiles):
+    return tile if at_seam(tile, tiles) else far_mate(tile, tiles)
+
+
+def plain_mate(tile, tiles):
+    return tile if by_seam(tile, tiles) else near_mate(tile, tiles)
+
+
+def over(tile, tiles):
+    return (tile + 8) // 16 * 32 - 1 - tile
 
 
 def pairs_of(route, tiles, select=lambda tile, tiles: True):
@@ -44,35 +60,31 @@
     ]
 
 
+ON_CHIP = ((0, 1, same), (1, 0, same), (2, 3, same), (3, 2, same))
+
+
+def else_on_chip(route, tiles, select):
+    return pairs_of(route, tiles, select) + pairs_of(ON_CHIP, tiles, lambda *tile: not select(*tile))
+
+
 def within_chip(source, target, mate):
     one, two = [layer for layer in range(4) if layer not in (source, target)]
     return ((source, target, mate), (target, source, same), (one, two, same), (two, one, same))
 
 
-def across(source, target):
+def around(source, target, mate, back):
     return (
-        (source, target, same),
+        (source, target, mate),
         (target, target ^ 1, same),
-        (target ^ 1, source ^ 1, mirror),
+        (target ^ 1, source ^ 1, back),
         (source ^ 1, source, same),
     )
 
 
-ON_CHIP = ((0, 1, same), (1, 0, same), (2, 3, same), (3, 2, same))
-
-
-def inner_mate(tile, tiles):
-    return tile if at_seam(tile, tiles) else far_mate(tile, tiles)
-
-
-def over_seam(source, target, tiles):
-    route = (
-        (source, target, far_mate),
-        (target, target ^ 1, same),
-        (target ^ 1, source ^ 1, far_mate),
-        (source ^ 1, source, same),
+def across(source, target, tiles):
+    return pairs_of(around(source, target, same, mirror), tiles, at_seam) + pairs_of(
+        around(source, target ^ 1, same, mirror), tiles, lambda *tile: not at_seam(*tile)
     )
-    return pairs_of(route, tiles, at_seam) + pairs_of(ON_CHIP, tiles, lambda *tile: not at_seam(*tile))
 
 
 def permute(values, pairs):
@@ -108,10 +120,27 @@
     )(pltpu.with_memory_space_constraint(blocks, pltpu.HBM), after)
 
 
+def seam_here(shift):
+    tiles = lax.axis_size("tile")
+    tile = lax.axis_index("tile")
+    run = tiles // 4
+    place = lax.rem(tile, run)
+    outer = jnp.logical_or(tile == shift, tile == tiles - 1 - shift)
+    return jnp.logical_and(jnp.logical_or(place == shift, place == run - 1 - shift), jnp.logical_not(outer))
+
+
 def step_kernel(layer, names, *refs):
     *refs, out_ref = refs
     refs = dict(zip(names, refs))
     here = lax.axis_index("layer") == layer
+    if "early" in refs:
+        seam = seam_here(0)
+
+        @pl.when(jnp.logical_and(here, seam))
+        def _():
+            out_ref[...] = refs["early"][...]
+
+        here = jnp.logical_and(here, jnp.logical_not(seam))
 
     if "kept" in refs:
 
@@ -122,6 +151,14 @@
     @pl.when(here)
     def _():
         product_and_sum(refs, out_ref)
+
+
+def seam_kernel(layer, names, *refs):
+    *refs, out_ref = refs
+
+    @pl.when(jnp.logical_and(lax.axis_index("layer") == layer, seam_here(0)))
+    def _():
+        product_and_sum(dict(zip(names, refs)), out_ref)
 
 
 def product_and_sum(refs, out_ref):
@@ -142,12 +179,14 @@
         return by_real, by_imag
 
     far = stacked(far_ref)
-    if "seam" in refs:
-        place = lax.rem(tile, tiles // 4)
-        far = jnp.where(jnp.logical_or(place == 0, place == tiles // 4 - 1), stacked(refs["seam"]), far)
+    if "passed" in refs:
+        far = jnp.where(seam_here(0), stacked(refs["passed"]), far)
     far = jnp.where(edge, jnp.zeros_like(far), far)
+    near = stacked(near_ref)
+    if "direct" in refs:
+        near = jnp.where(seam_here(1), stacked(refs["direct"]), near)
     own_real, own_imag = product(stacked(own_ref), 0)
-    near_real, near_imag = product(stacked(near_ref), 2 - odd)
+    near_real, near_imag = product(near, 2 - odd)
     far_real, far_imag = product(far, 1 + odd)
     by_real = own_real + near_real + far_real
     by_imag = own_imag + near_imag + far_imag
@@ -157,11 +196,11 @@
     out_ref[1] = imag
 
 
-def step(layer, **operands):
+def step(layer, kernel=step_kernel, **operands):
     vmem = pl.BlockSpec(memory_space=pltpu.VMEM)
     addend = operands["addend"]
     return pl.pallas_call(
-        functools.partial(step_kernel, layer, tuple(operands)),
+        functools.partial(kernel, layer, tuple(operands)),
         out_shape=jax.ShapeDtypeStruct(addend.shape, addend.dtype),
         in_specs=[vmem] * len(operands),
         out_specs=vmem,
@@ -174,37 +213,47 @@
     )(*operands.values())
 
 
-def spread(values, source, target, far, order):
-    tiles = lax.axis_size("tile")
-    mates = {"far": far, "near": near_mate, "own": same}
+def spread(values, source, target, order, near=near_mate, far=far_mate):
+    tiles = lax.axis_size("tile")
+    mates = {"far": far, "near": near, "own": same}
     return {name: permute(values, pairs_of(within_chip(source, target, mates[name]), tiles)) for name in order}
 
 
-def hop(values, source, target, blocks, order, after=None, **rest):
-    arrived = spread(values, source, target, far_mate, order)
+def hop(values, source, target, blocks, order, after=None, passed=None, **rest):
+    if passed is None:
+        arrived = spread(values, source, target, order)
+    else:
+        arrived = spread(values, source, target, order, far=inner_mate)
+        rest = {"passed": passed, **rest}
     held = load(blocks, values if after is None else after, target)
     return step(target, **arrived, blocks=held, **rest)
 
 
-def crossing_hop(values, source, target, blocks, order, **rest):
-    tiles = lax.axis_size("tile")
-    crossed = permute(values, pairs_of(across(source, target ^ 1), tiles))
-    seam = permute(values, over_seam(source, target, tiles))
-    arrived = spread(crossed, target ^ 1, target, inner_mate, order)
-    return step(target, **arrived, seam=seam, blocks=load(blocks, values, target), **rest)
+def crossing_hop(values, source, target, blocks, order, addend):
+    tiles = lax.axis_size("tile")
+    relay = target ^ 1
+    held = load(blocks, values, target)
+    crossed = permute(values, across(source, target, tiles))
+    seam = permute(values, else_on_chip(around(source, target, far_mate, far_mate), tiles, at_seam))
+    direct = permute(values, else_on_chip(around(source, target, near_mate, over), tiles, by_seam))
+    early = step(target, seam_kernel, far=seam, near=direct, own=crossed, blocks=held, addend=addend)
+    passed = permute(early, else_on_chip(within_chip(target, relay, far_mate), tiles, at_seam))
+    arrived = spread(crossed, relay, target, order, plain_mate, inner_mate)
+    result = step(target, **arrived, direct=direct, early=early, blocks=held, addend=addend)
+    return result, passed
 
 
 def per_device(sources, down_blocks, up_blocks):
     layer = lax.axis_index("layer")
     source, down, up = sources[0], down_blocks[0], up_blocks[0]
     down_1 = hop(source, 0, 1, down, ORDERS[0], addend=source)
-    down_2 = crossing_hop(down_1, 1, 2, down, ORDERS[1], addend=source)
-    down_3 = hop(down_2, 2, 3, down, ORDERS[2], addend=source)
+    down_2, passed = crossing_hop(down_1, 1, 2, down, ORDERS[1], addend=source)
+    down_3 = hop(down_2, 2, 3, down, ORDERS[2], passed=passed, addend=source)
     falling = jnp.where(layer == 0, source, jnp.where(layer == 1, down_1, jnp.where(layer == 2, down_2, down_3)))
     up_2 = hop(down_3, 3, 2, up, ORDERS[3], addend=down_2)
-    up_1 = crossing_hop(up_2, 2, 1, up, ORDERS[4], addend=down_1)
+    up_1, passed = crossing_hop(up_2, 2, 1, up, ORDERS[4], addend=down_1)
     rising = jnp.where(layer == 1, up_1, jnp.where(layer == 2, up_2, down_3))
-    rising = hop(up_1, 1, 0, up, ORDERS[5], down_3, addend=source, kept=rising)
+    rising = hop(up_1, 1, 0, up, ORDERS[5], down_3, passed, addend=source, kept=rising)
     return (falling[None], rising[None])
 
 

time: 57 us -> 56.3 us (0.988)
  waiting for transfers between devices: 19.1 us -> 16 us
  starting transfers between devices: 32 us -> 34.3 us
    ppermute x22 -> x26, waiting for transfers between devices: 19.1 us -> 16 us  [permute(): return lax.ppermute(values, AXES, pairs)]
    ppermute x22 -> x26, starting transfers between devices: 32 us -> 34.3 us  [permute(): return lax.ppermute(values, AXES, pairs)]
    pallas_call x6 -> x8, Pallas kernels: 1.28 us -> 1.34 us  [step(): pl.pallas_call(functools.partial(kernel, layer, tuple(operands)), out_sha...]
  transfers between devices with their start and end apart: 22 -> 26, of which waited for: 11 -> 12; matrix products, arithmetic and copies ran while one was open for 1% -> 1% of each run, Pallas kernels for 4% -> 4%
where the time goes in v4:
time: 56.3 us; the launch traced here: 56.2 us
  starting transfers between devices  34.3 us (61%)
  waiting for transfers between devices  16 us (28%)
  Pallas kernels  3.51 us (6%)
  local copies, waits for them, and re-layouts  0.91 us (2%)
  between operations  0.77 us (1%)
  other arithmetic  0.69 us (1%)
    ppermute x26, starting transfers between devices, permute(): return lax.ppermute(values, AXES, pairs)  34.3 us
    ppermute x26, waiting for transfers between devices, permute(): return lax.ppermute(values, AXES, pairs)  16 us
    pallas_call x6, Pallas kernels, load(): pl.pallas_call(functools.partial(load_kernel, layers), out_shape=pltpu.VM...  2.17 us
    pallas_call x8, Pallas kernels, step(): pl.pallas_call(functools.partial(kernel, layer, tuple(operands)), out_sha...  1.34 us
  transfers between devices with their start and end apart: 26, of which 12 were waited for; matrix products, arithmetic and copies ran while one was open for 1% of the time, Pallas kernels for 4%

profile of v4, /device:TPU:6, one launch (start us, length us, event | category | flops | bytes accessed | tf_op | source)
XLA Modules:
  0.0 56.2 jit_solution(16616208245012866927)
XLA Ops:
  0.6 6.9 %collective-permute-start = (bf16[2,64,512]{2,1,0:T(8,128)(2,1)}, bf16[2,64,512]{2,1,0:T(8,128)(2,1)S(1)}, u32[]{:S(2)}, u32[]{:S(2)}) collective-permute-start(bf16[2,64,512]{2,1,0:T(8,128)(2,1)} %bitcast.7), channel_id=1, source_target_pairs={{0,64},{1,66},{2,65},{3,68},{4,67},{5,70},{6,69},{7,72},{8,71},{9,... | collective-permute-start | bytes 393224 | tf_op jit(solution)/shard_map/ppermute | solution.py:91
  7.5 0.5 collective-permute-start.2
  8.0 0.9 %copy-done = bf16[1,2,64,512]{3,2,1,0:T(8,128)(2,1)S(1)} copy-done((bf16[1,2,64,512]{3,2,1,0:T(8,128)(2,1)S(1)}, bf16[1,2,64,512]{3,2,1,0:T(8,128)(2,1)}, u32[]{:S(2)}) %copy-start) | copy-done | bytes 131096
  8.9 0.1 shard_map.50.refs_3_
  9.0 1.4 %collective-permute-done.refs_0_ = bf16[2,64,512]{2,1,0:T(8,128)(2,1)S(1)} collective-permute-done((bf16[2,64,512]{2,1,0:T(8,128)(2,1)}, bf16[2,64,512]{2,1,0:T(8,128)(2,1)S(1)}, u32[]{:S(2)}, u32[]{:S(2)}) %collective-permute-start) | collective-permute-done | bytes 131104 | tf_op jit(solution)/shard_map/ppermute | solution.py:91
  10.3 0.0 collective-permute-done.1.refs_1_
  10.4 1.4 %collective-permute-start.3 = (bf16[2,64,512]{2,1,0:T(8,128)(2,1)S(1)}, bf16[2,64,512]{2,1,0:T(8,128)(2,1)S(1)}, u32[]{:S(2)}, u32[]{:S(2)}) collective-permute-start(bf16[2,64,512]{2,1,0:T(8,128)(2,1)S(1)} %shard_map.51.after_ref.refs_4_.refs_6_), channel_id=1, source_target_pairs={{79,143},{80,144},{95,159},{96,160},{111,175},{112,176},{143,207},... | collective-permute-start | bytes 393224 | tf_op jit(solution)/shard_map/ppermute | solution.py:91
  11.7 0.1 collective-permute-start.7
  11.8 1.2 %collective-permute-start.8 = (bf16[2,64,512]{2,1,0:T(8,128)(2,1)S(1)}, bf16[2,64,512]{2,1,0:T(8,128)(2,1)S(1)}, u32[]{:S(2)}, u32[]{:S(2)}) collective-permute-start(bf16[2,64,512]{2,1,0:T(8,128)(2,1)S(1)} %shard_map.51.after_ref.refs_4_.refs_6_), channel_id=1, source_target_pairs={{79,144},{80,143},{95,160},{96,159},{111,176},{112,175},{143,207},... | collective-permute-start | bytes 393224 | tf_op jit(solution)/shard_map/ppermute | solution.py:91
  13.1 3.5 %collective-permute-done.3.refs_2_ = bf16[2,64,512]{2,1,0:T(8,128)(2,1)S(1)} collective-permute-done((bf16[2,64,512]{2,1,0:T(8,128)(2,1)S(1)}, bf16[2,64,512]{2,1,0:T(8,128)(2,1)S(1)}, u32[]{:S(2)}, u32[]{:S(2)}) %collective-permute-start.3) | collective-permute-done | bytes 131104 | tf_op jit(solution)/shard_map/ppermute | solution.py:91
  16.6 0.0 collective-permute-start.4
  16.6 0.5 collective-permute-start.5
  17.1 0.0 collective-permute-start.6
  17.1 0.1 shard_map.52.refs_3_.refs_5_
  17.2 3.2 %collective-permute-done.7.refs_1_.refs_3_ = bf16[2,64,512]{2,1,0:T(8,128)(2,1)S(1)} collective-permute-done((bf16[2,64,512]{2,1,0:T(8,128)(2,1)S(1)}, bf16[2,64,512]{2,1,0:T(8,128)(2,1)S(1)}, u32[]{:S(2)}, u32[]{:S(2)}) %collective-permute-start.7) | collective-permute-done | bytes 131104 | tf_op jit(solution)/shard_map/ppermute | solution.py:91
  20.3 1.4 %collective-permute-done.8.refs_0_ = bf16[2,64,512]{2,1,0:T(8,128)(2,1)S(1)} collective-permute-done((bf16[2,64,512]{2,1,0:T(8,128)(2,1)S(1)}, bf16[2,64,512]{2,1,0:T(8,128)(2,1)S(1)}, u32[]{:S(2)}, u32[]{:S(2)}) %collective-permute-start.8) | collective-permute-done | bytes 131104 | tf_op jit(solution)/shard_map/ppermute | solution.py:91
  21.7 0.0 collective-permute-start.12
  21.8 0.0 collective-permute-done.6.refs_2_
  21.8 0.6 %collective-permute-start.10 = (bf16[2,64,512]{2,1,0:T(8,128)(2,1)S(1)}, bf16[2,64,512]{2,1,0:T(8,128)(2,1)S(1)}, u32[]{:S(2)}, u32[]{:S(2)}) collective-permute-start(bf16[2,64,512]{2,1,0:T(8,128)(2,1)S(1)} %shard_map.54.after_ref.refs_4_), channel_id=1, source_target_pairs={{128,192},{129,194},{130,193},{131,196},{132,195},{133,198},{134,1... | collective-permute-start | bytes 393224 | tf_op jit(solution)/shard_map/ppermute | solution.py:91
  22.4 0.1 collective-permute-start.11
  22.5 0.4 collective-permute-start.9
  22.9 0.1 shard_map.55.refs_3_
  23.0 0.1 collective-permute-done.12.refs_4_
  23.1 0.3 collective-permute-done.10.refs_1_
  23.4 0.4 collective-permute-done.11.refs_2_
  23.7 0.2 collective-permute-done.9.refs_0_
  23.9 0.3 collective-permute-start.13
  24.3 0.2 collective-permute-start.14
  24.4 0.3 collective-permute-start.15
  24.8 0.1 shard_map.57.refs_3_
  24.8 0.5 collective-permute-done.13.refs_0_
  25.3 0.3 collective-permute-done.14.refs_1_
  25.6 0.2 collective-permute-done.15.refs_2_
  25.8 6.1 %collective-permute-start.16 = (bf16[2,64,512]{2,1,0:T(8,128)(2,1)S(1)}, bf16[2,64,512]{2,1,0:T(8,128)(2,1)S(1)}, u32[]{:S(2)}, u32[]{:S(2)}) collective-permute-start(bf16[2,64,512]{2,1,0:T(8,128)(2,1)S(1)} %shard_map.58.after_ref), channel_id=1, source_target_pairs={{143,79},{144,80},{159,95},{160,96},{175,111},{176,112},{79,15},{8... | collective-permute-start | bytes 393224 | tf_op jit(solution)/shard_map/ppermute | solution.py:91
  31.8 8.8 %collective-permute-start.20 = (bf16[2,64,512]{2,1,0:T(8,128)(2,1)S(1)}, bf16[2,64,512]{2,1,0:T(8,128)(2,1)S(1)}, u32[]{:S(2)}, u32[]{:S(2)}) collective-permute-start(bf16[2,64,512]{2,1,0:T(8,128)(2,1)S(1)} %shard_map.58.after_ref), channel_id=1, source_target_pairs={{142,79},{143,78},{144,81},{145,80},{158,95},{159,94},{160,97},{16... | collective-permute-start | bytes 393224 | tf_op jit(solution)/shard_map/ppermute | solution.py:91
  40.7 0.1 collective-permute-start.21
  40.8 2.3 %collective-permute-start.17 = (bf16[2,64,512]{2,1,0:T(8,128)(2,1)S(1)}, bf16[2,64,512]{2,1,0:T(8,128)(2,1)S(1)}, u32[]{:S(2)}, u32[]{:S(2)}) collective-permute-start(bf16[2,64,512]{2,1,0:T(8,128)(2,1)S(1)} %collective-permute-done.16.refs_2_), channel_id=1, source_target_pairs={{0,64},{1,66},{2,65},{3,68},{4,67},{5,70},{6,69},{7,72},{8,71},{9,... | collective-permute-start | bytes 393224 | tf_op jit(solution)/shard_map/ppermute | solution.py:91
  43.1 0.0 collective-permute-start.18
  43.1 0.5 collective-permute-start.19
  43.6 1.9 %shard_map.62.refs_3_ = bf16[3,2,512,512]{3,2,1,0:T(8,128)(2,1)S(1)} custom-call(bf16[3,2,512,512]{3,2,1,0:T(8,128)(2,1)} %bitcast.20, bf16[2,64,512]{2,1,0:T(8,128)(2,1)S(1)} %shard_map.56.after_ref), custom_call_target="tpu_custom_call" | custom-call | bytes 6291456 | tf_op jit(solution)/shard_map/pallas_call | solution.py:112
  45.5 0.1 shard_map.59.refs_3_.refs_5_
  45.6 0.7 %collective-permute-start.25 = (bf16[2,64,512]{2,1,0:T(8,128)(2,1)S(1)}, bf16[2,64,512]{2,1,0:T(8,128)(2,1)S(1)}, u32[]{:S(2)}, u32[]{:S(2)}) collective-permute-start(bf16[2,64,512]{2,1,0:T(8,128)(2,1)S(1)} %shard_map.60.refs_4_), channel_id=1, source_target_pairs={{79,16},{80,15},{95,32},{96,31},{111,48},{112,47},{15,79},{16,80},... | collective-permute-start | bytes 393224 | tf_op jit(solution)/shard_map/ppermute | solution.py:91
  46.3 3.1 %collective-permute-start.22 = (bf16[2,64,512]{2,1,0:T(8,128)(2,1)S(1)}, bf16[2,64,512]{2,1,0:T(8,128)(2,1)S(1)}, u32[]{:S(2)}, u32[]{:S(2)}) collective-permute-start(bf16[2,64,512]{2,1,0:T(8,128)(2,1)S(1)} %shard_map.61), channel_id=1, source_target_pairs={{64,0},{65,2},{66,1},{67,4},{68,3},{69,6},{70,5},{71,8},{72,7},{73... | collective-permute-start | bytes 393224 | tf_op jit(solution)/shard_map/ppermute | solution.py:91
  49.5 0.1 collective-permute-start.23
  49.6 0.1 collective-permute-start.24
  49.7 0.7 %select_select_fusion = (bf16[2,64,512]{2,1,0:T(8,128)(2,1)S(1)}, bf16[1,2,64,512]{3,2,1,0:T(8,128)(2,1)}) fusion(bf16[2,64,512]{2,1,0:T(8,128)(2,1)S(1)} %shard_map.61, bf16[2,64,512]{2,1,0:T(8,128)(2,1)S(1)} %shard_map.58.after_ref, bf16[2,64,512]{2,1,0:T(8,128)(2,1)S(1)} %shard_map.56.after_ref, pred[]{:T(512)S(6)} %eq.13, pred[]{:T(512)S(6)} %eq.12, ...), kind=kLoop, calls=%fused_computation | loop fusion | flops 327680 | bytes 1048579 | tf_op jit(solution)/shard_map/jit(_where)/select_n | solution.py:255
  50.4 4.6 %collective-permute-done.25.refs_4_ = bf16[2,64,512]{2,1,0:T(8,128)(2,1)S(1)} collective-permute-done((bf16[2,64,512]{2,1,0:T(8,128)(2,1)S(1)}, bf16[2,64,512]{2,1,0:T(8,128)(2,1)S(1)}, u32[]{:S(2)}, u32[]{:S(2)}) %collective-permute-start.25) | collective-permute-done | bytes 131104 | tf_op jit(solution)/shard_map/ppermute | solution.py:91
  54.9 1.3 %shard_map.63 = bf16[2,64,512]{2,1,0:T(8,128)(2,1)} custom-call(bf16[2,64,512]{2,1,0:T(8,128)(2,1)S(1)} %collective-permute-done.22.refs_0_, bf16[2,64,512]{2,1,0:T(8,128)(2,1)S(1)} %collective-permute-done.23.refs_1_, bf16[2,64,512]{2,1,0:T(8,128)(2,1)S(1)} %collective-permute-done.24.refs_2_, bf16[3,2,512,512]{3,2,1,0:T(8,128)(2,1)S(1)} %shard_map.62.refs_3_, ...), custom_call_target="tpu_custom_call" | custom-call | flops 402653184 | bytes 3801088 | tf_op jit(solution)/shard_map/pallas_call | solution.py:202
  (23 shorter events, 0.1 us)
Async XLA Ops:
  0.6 9.7 %collective-permute-start = (bf16[2,64,512]{2,1,0:T(8,128)(2,1)}, bf16[2,64,512]{2,1,0:T(8,128)(2,1)S(1)}, u32[]{:S(2)}, u32[]{:S(2)}) collective-permute-start(bf16[2,64,512]{2,1,0:T(8,128)(2,1)} %bitcast.7), channel_id=1, source_target_pairs={{0,64},{1,66},{2,65},{3,68},{4,67},{5,70},{6,69},{7,72},{8,71},{9,... | collective-permute-start | bytes 393224 | tf_op jit(solution)/shard_map/ppermute | solution.py:91
  7.5 2.9 %collective-permute-start.1 = (bf16[2,64,512]{2,1,0:T(8,128)(2,1)}, bf16[2,64,512]{2,1,0:T(8,128)(2,1)S(1)}, u32[]{:S(2)}, u32[]{:S(2)}) collective-permute-start(bf16[2,64,512]{2,1,0:T(8,128)(2,1)} %bitcast.8), channel_id=1, source_target_pairs={{0,65},{1,64},{2,67},{3,66},{4,69},{5,68},{6,71},{7,70},{8,73},{9,... | collective-permute-start | bytes 393224 | tf_op jit(solution)/shard_map/ppermute | solution.py:91
  7.5 2.9 %collective-permute-start.2 = (bf16[2,64,512]{2,1,0:T(8,128)(2,1)}, bf16[2,64,512]{2,1,0:T(8,128)(2,1)S(1)}, u32[]{:S(2)}, u32[]{:S(2)}) collective-permute-start(bf16[2,64,512]{2,1,0:T(8,128)(2,1)} %bitcast.9), channel_id=1, source_target_pairs={{0,64},{1,65},{2,66},{3,67},{4,68},{5,69},{6,70},{7,71},{8,72},{9,... | collective-permute-start | bytes 393224 | tf_op jit(solution)/shard_map/ppermute | solution.py:91
  8.0 0.9 %copy-start = (bf16[1,2,64,512]{3,2,1,0:T(8,128)(2,1)S(1)}, bf16[1,2,64,512]{3,2,1,0:T(8,128)(2,1)}, u32[]{:S(2)}) copy-start(bf16[1,2,64,512]{3,2,1,0:T(8,128)(2,1)} %param.3) | copy-start | bytes 393220
  10.4 11.4 %copy-start.1 = (bf16[1,2,64,512]{3,2,1,0:T(8,128)(2,1)S(1)}, bf16[1,2,64,512]{3,2,1,0:T(8,128)(2,1)}, u32[]{:S(2)}) copy-start(bf16[1,2,64,512]{3,2,1,0:T(8,128)(2,1)} %param.3) | copy-start | bytes 393220
  10.4 6.2 %collective-permute-start.3 = (bf16[2,64,512]{2,1,0:T(8,128)(2,1)S(1)}, bf16[2,64,512]{2,1,0:T(8,128)(2,1)S(1)}, u32[]{:S(2)}, u32[]{:S(2)}) collective-permute-start(bf16[2,64,512]{2,1,0:T(8,128)(2,1)S(1)} %shard_map.51.after_ref.refs_4_.refs_6_), channel_id=1, source_target_pairs={{79,143},{80,144},{95,159},{96,160},{111,175},{112,176},{143,207},... | collective-permute-start | bytes 393224 | tf_op jit(solution)/shard_map/ppermute | solution.py:91
  11.7 8.6 %collective-permute-start.7 = (bf16[2,64,512]{2,1,0:T(8,128)(2,1)S(1)}, bf16[2,64,512]{2,1,0:T(8,128)(2,1)S(1)}, u32[]{:S(2)}, u32[]{:S(2)}) collective-permute-start(bf16[2,64,512]{2,1,0:T(8,128)(2,1)S(1)} %shard_map.51.after_ref.refs_4_.refs_6_), channel_id=1, source_target_pairs={{78,143},{79,142},{80,145},{81,144},{94,159},{95,158},{96,161},{97... | collective-permute-start | bytes 393224 | tf_op jit(solution)/shard_map/ppermute | solution.py:91
  11.8 9.9 %collective-permute-start.8 = (bf16[2,64,512]{2,1,0:T(8,128)(2,1)S(1)}, bf16[2,64,512]{2,1,0:T(8,128)(2,1)S(1)}, u32[]{:S(2)}, u32[]{:S(2)}) collective-permute-start(bf16[2,64,512]{2,1,0:T(8,128)(2,1)S(1)} %shard_map.51.after_ref.refs_4_.refs_6_), channel_id=1, source_target_pairs={{79,144},{80,143},{95,160},{96,159},{111,176},{112,175},{143,207},... | collective-permute-start | bytes 393224 | tf_op jit(solution)/shard_map/ppermute | solution.py:91
  16.6 5.2 %collective-permute-start.4 = (bf16[2,64,512]{2,1,0:T(8,128)(2,1)S(1)}, bf16[2,64,512]{2,1,0:T(8,128)(2,1)S(1)}, u32[]{:S(2)}, u32[]{:S(2)}) collective-permute-start(bf16[2,64,512]{2,1,0:T(8,128)(2,1)S(1)} %collective-permute-done.3.refs_2_), channel_id=1, source_target_pairs={{192,128},{193,130},{194,129},{195,132},{196,131},{197,134},{198,1... | collective-permute-start | bytes 393224 | tf_op jit(solution)/shard_map/ppermute | solution.py:91
  16.6 5.2 %collective-permute-start.5 = (bf16[2,64,512]{2,1,0:T(8,128)(2,1)S(1)}, bf16[2,64,512]{2,1,0:T(8,128)(2,1)S(1)}, u32[]{:S(2)}, u32[]{:S(2)}) collective-permute-start(bf16[2,64,512]{2,1,0:T(8,128)(2,1)S(1)} %collective-permute-done.3.refs_2_), channel_id=1, source_target_pairs={{192,129},{193,128},{194,131},{195,130},{196,133},{197,132},{198,1... | collective-permute-start | bytes 393224 | tf_op jit(solution)/shard_map/ppermute | solution.py:91
  17.1 4.7 %collective-permute-start.6 = (bf16[2,64,512]{2,1,0:T(8,128)(2,1)S(1)}, bf16[2,64,512]{2,1,0:T(8,128)(2,1)S(1)}, u32[]{:S(2)}, u32[]{:S(2)}) collective-permute-start(bf16[2,64,512]{2,1,0:T(8,128)(2,1)S(1)} %collective-permute-done.3.refs_2_), channel_id=1, source_target_pairs={{192,128},{193,129},{194,130},{195,131},{196,132},{197,133},{198,1... | collective-permute-start | bytes 393224 | tf_op jit(solution)/shard_map/ppermute | solution.py:91
  21.7 1.3 %collective-permute-start.12 = (bf16[2,64,512]{2,1,0:T(8,128)(2,1)S(1)}, bf16[2,64,512]{2,1,0:T(8,128)(2,1)S(1)}, u32[]{:S(2)}, u32[]{:S(2)}) collective-permute-start(bf16[2,64,512]{2,1,0:T(8,128)(2,1)S(1)} %shard_map.53.refs_4_), channel_id=1, source_target_pairs={{143,208},{144,207},{159,224},{160,223},{175,240},{176,239},{207,1... | collective-permute-start | bytes 393224 | tf_op jit(solution)/shard_map/ppermute | solution.py:91
  21.8 1.6 %collective-permute-start.10 = (bf16[2,64,512]{2,1,0:T(8,128)(2,1)S(1)}, bf16[2,64,512]{2,1,0:T(8,128)(2,1)S(1)}, u32[]{:S(2)}, u32[]{:S(2)}) collective-permute-start(bf16[2,64,512]{2,1,0:T(8,128)(2,1)S(1)} %shard_map.54.after_ref.refs_4_), channel_id=1, source_target_pairs={{128,192},{129,194},{130,193},{131,196},{132,195},{133,198},{134,1... | collective-permute-start | bytes 393224 | tf_op jit(solution)/shard_map/ppermute | solution.py:91
  22.4 1.3 %collective-permute-start.11 = (bf16[2,64,512]{2,1,0:T(8,128)(2,1)S(1)}, bf16[2,64,512]{2,1,0:T(8,128)(2,1)S(1)}, u32[]{:S(2)}, u32[]{:S(2)}) collective-permute-start(bf16[2,64,512]{2,1,0:T(8,128)(2,1)S(1)} %shard_map.54.after_ref.refs_4_), channel_id=1, source_target_pairs={{128,193},{129,192},{130,195},{131,194},{132,197},{133,196},{134,1... | collective-permute-start | bytes 393224 | tf_op jit(solution)/shard_map/ppermute | solution.py:91
  22.5 1.4 %collective-permute-start.9 = (bf16[2,64,512]{2,1,0:T(8,128)(2,1)S(1)}, bf16[2,64,512]{2,1,0:T(8,128)(2,1)S(1)}, u32[]{:S(2)}, u32[]{:S(2)}) collective-permute-start(bf16[2,64,512]{2,1,0:T(8,128)(2,1)S(1)} %shard_map.54.after_ref.refs_4_), channel_id=1, source_target_pairs={{128,192},{129,193},{130,194},{131,195},{132,196},{133,197},{134,1... | collective-permute-start | bytes 393224 | tf_op jit(solution)/shard_map/ppermute | solution.py:91
  23.9 1.3 %collective-permute-start.13 = (bf16[2,64,512]{2,1,0:T(8,128)(2,1)S(1)}, bf16[2,64,512]{2,1,0:T(8,128)(2,1)S(1)}, u32[]{:S(2)}, u32[]{:S(2)}) collective-permute-start(bf16[2,64,512]{2,1,0:T(8,128)(2,1)S(1)} %shard_map.56.after_ref), channel_id=1, source_target_pairs={{192,128},{193,130},{194,129},{195,132},{196,131},{197,134},{198,1... | collective-permute-start | bytes 393224 | tf_op jit(solution)/shard_map/ppermute | solution.py:91
  24.3 1.3 %collective-permute-start.14 = (bf16[2,64,512]{2,1,0:T(8,128)(2,1)S(1)}, bf16[2,64,512]{2,1,0:T(8,128)(2,1)S(1)}, u32[]{:S(2)}, u32[]{:S(2)}) collective-permute-start(bf16[2,64,512]{2,1,0:T(8,128)(2,1)S(1)} %shard_map.56.after_ref), channel_id=1, source_target_pairs={{192,129},{193,128},{194,131},{195,130},{196,133},{197,132},{198,1... | collective-permute-start | bytes 393224 | tf_op jit(solution)/shard_map/ppermute | solution.py:91
  24.4 1.3 %collective-permute-start.15 = (bf16[2,64,512]{2,1,0:T(8,128)(2,1)S(1)}, bf16[2,64,512]{2,1,0:T(8,128)(2,1)S(1)}, u32[]{:S(2)}, u32[]{:S(2)}) collective-permute-start(bf16[2,64,512]{2,1,0:T(8,128)(2,1)S(1)} %shard_map.56.after_ref), channel_id=1, source_target_pairs={{192,128},{193,129},{194,130},{195,131},{196,132},{197,133},{198,1... | collective-permute-start | bytes 393224 | tf_op jit(solution)/shard_map/ppermute | solution.py:91
  25.8 15.0 %collective-permute-start.16 = (bf16[2,64,512]{2,1,0:T(8,128)(2,1)S(1)}, bf16[2,64,512]{2,1,0:T(8,128)(2,1)S(1)}, u32[]{:S(2)}, u32[]{:S(2)}) collective-permute-start(bf16[2,64,512]{2,1,0:T(8,128)(2,1)S(1)} %shard_map.58.after_ref), channel_id=1, source_target_pairs={{143,79},{144,80},{159,95},{160,96},{175,111},{176,112},{79,15},{8... | collective-permute-start | bytes 393224 | tf_op jit(solution)/shard_map/ppermute | solution.py:91
  31.8 13.7 %collective-permute-start.20 = (bf16[2,64,512]{2,1,0:T(8,128)(2,1)S(1)}, bf16[2,64,512]{2,1,0:T(8,128)(2,1)S(1)}, u32[]{:S(2)}, u32[]{:S(2)}) collective-permute-start(bf16[2,64,512]{2,1,0:T(8,128)(2,1)S(1)} %shard_map.58.after_ref), channel_id=1, source_target_pairs={{142,79},{143,78},{144,81},{145,80},{158,95},{159,94},{160,97},{16... | collective-permute-start | bytes 393224 | tf_op jit(solution)/shard_map/ppermute | solution.py:91
  40.7 4.9 %collective-permute-start.21 = (bf16[2,64,512]{2,1,0:T(8,128)(2,1)S(1)}, bf16[2,64,512]{2,1,0:T(8,128)(2,1)S(1)}, u32[]{:S(2)}, u32[]{:S(2)}) collective-permute-start(bf16[2,64,512]{2,1,0:T(8,128)(2,1)S(1)} %shard_map.58.after_ref), channel_id=1, source_target_pairs={{143,80},{144,79},{159,96},{160,95},{175,112},{176,111},{79,15},{8... | collective-permute-start | bytes 393224 | tf_op jit(solution)/shard_map/ppermute | solution.py:91
  40.8 5.5 %collective-permute-start.17 = (bf16[2,64,512]{2,1,0:T(8,128)(2,1)S(1)}, bf16[2,64,512]{2,1,0:T(8,128)(2,1)S(1)}, u32[]{:S(2)}, u32[]{:S(2)}) collective-permute-start(bf16[2,64,512]{2,1,0:T(8,128)(2,1)S(1)} %collective-permute-done.16.refs_2_), channel_id=1, source_target_pairs={{0,64},{1,66},{2,65},{3,68},{4,67},{5,70},{6,69},{7,72},{8,71},{9,... | collective-permute-start | bytes 393224 | tf_op jit(solution)/shard_map/ppermute | solution.py:91
  43.1 3.2 %collective-permute-start.18 = (bf16[2,64,512]{2,1,0:T(8,128)(2,1)S(1)}, bf16[2,64,512]{2,1,0:T(8,128)(2,1)S(1)}, u32[]{:S(2)}, u32[]{:S(2)}) collective-permute-start(bf16[2,64,512]{2,1,0:T(8,128)(2,1)S(1)} %collective-permute-done.16.refs_2_), channel_id=1, source_target_pairs={{0,65},{1,64},{2,67},{3,66},{4,69},{5,68},{6,71},{7,70},{8,73},{9,... | collective-permute-start | bytes 393224 | tf_op jit(solution)/shard_map/ppermute | solution.py:91
  43.1 3.2 %collective-permute-start.19 = (bf16[2,64,512]{2,1,0:T(8,128)(2,1)S(1)}, bf16[2,64,512]{2,1,0:T(8,128)(2,1)S(1)}, u32[]{:S(2)}, u32[]{:S(2)}) collective-permute-start(bf16[2,64,512]{2,1,0:T(8,128)(2,1)S(1)} %collective-permute-done.16.refs_2_), channel_id=1, source_target_pairs={{0,64},{1,65},{2,66},{3,67},{4,68},{5,69},{6,70},{7,71},{8,72},{9,... | collective-permute-start | bytes 393224 | tf_op jit(solution)/shard_map/ppermute | solution.py:91
  45.6 9.3 %collective-permute-start.25 = (bf16[2,64,512]{2,1,0:T(8,128)(2,1)S(1)}, bf16[2,64,512]{2,1,0:T(8,128)(2,1)S(1)}, u32[]{:S(2)}, u32[]{:S(2)}) collective-permute-start(bf16[2,64,512]{2,1,0:T(8,128)(2,1)S(1)} %shard_map.60.refs_4_), channel_id=1, source_target_pairs={{79,16},{80,15},{95,32},{96,31},{111,48},{112,47},{15,79},{16,80},... | collective-permute-start | bytes 393224 | tf_op jit(solution)/shard_map/ppermute | solution.py:91
  46.3 8.6 %collective-permute-start.22 = (bf16[2,64,512]{2,1,0:T(8,128)(2,1)S(1)}, bf16[2,64,512]{2,1,0:T(8,128)(2,1)S(1)}, u32[]{:S(2)}, u32[]{:S(2)}) collective-permute-start(bf16[2,64,512]{2,1,0:T(8,128)(2,1)S(1)} %shard_map.61), channel_id=1, source_target_pairs={{64,0},{65,2},{66,1},{67,4},{68,3},{69,6},{70,5},{71,8},{72,7},{73... | collective-permute-start | bytes 393224 | tf_op jit(solution)/shard_map/ppermute | solution.py:91
  49.5 5.5 %collective-permute-start.23 = (bf16[2,64,512]{2,1,0:T(8,128)(2,1)S(1)}, bf16[2,64,512]{2,1,0:T(8,128)(2,1)S(1)}, u32[]{:S(2)}, u32[]{:S(2)}) collective-permute-start(bf16[2,64,512]{2,1,0:T(8,128)(2,1)S(1)} %shard_map.61), channel_id=1, source_target_pairs={{64,1},{65,0},{66,3},{67,2},{68,5},{69,4},{70,7},{71,6},{72,9},{73... | collective-permute-start | bytes 393224 | tf_op jit(solution)/shard_map/ppermute | solution.py:91
  49.6 5.4 %collective-permute-start.24 = (bf16[2,64,512]{2,1,0:T(8,128)(2,1)S(1)}, bf16[2,64,512]{2,1,0:T(8,128)(2,1)S(1)}, u32[]{:S(2)}, u32[]{:S(2)}) collective-permute-start(bf16[2,64,512]{2,1,0:T(8,128)(2,1)S(1)} %shard_map.61), channel_id=1, source_target_pairs={{64,0},{65,1},{66,2},{67,3},{68,4},{69,5},{70,6},{71,7},{72,8},{73... | collective-permute-start | bytes 393224 | tf_op jit(solution)/shard_map/ppermute | solution.py:91

commit v5 on v4

--- a/solution.py
+++ b/solution.py
@@ -253,7 +253,7 @@
     up_2 = hop(down_3, 3, 2, up, ORDERS[3], addend=down_2)
     up_1, passed = crossing_hop(up_2, 2, 1, up, ORDERS[4], addend=down_1)
     rising = jnp.where(layer == 1, up_1, jnp.where(layer == 2, up_2, down_3))
-    rising = hop(up_1, 1, 0, up, ORDERS[5], down_3, passed, addend=source, kept=rising)
+    rising = hop(up_1, 1, 0, up, ORDERS[5], rising, passed, addend=source, kept=rising)
     return (falling[None], rising[None])
 
 

time: 56.3 us -> 55.2 us (0.980)
  waiting for transfers between devices: 16 us -> 15.2 us
    ppermute x26, waiting for transfers between devices: 16 us -> 15.2 us  [permute(): return lax.ppermute(values, AXES, pairs)]
  transfers between devices with their start and end apart: 26 -> 26, of which waited for: 12 -> 13; matrix products, arithmetic and copies ran while one was open for 1% -> 1% of each run, Pallas kernels for 4% -> 4%
where the time goes in v5:
time: 55.2 us; the launch traced here: 55.1 us
  starting transfers between devices  34 us (62%)
  waiting for transfers between devices  15.2 us (28%)
  Pallas kernels  3.47 us (6%)
  local copies, waits for them, and re-layouts  0.91 us (2%)
  between operations  0.76 us (1%)
  other arithmetic  0.69 us (1%)
    ppermute x26, starting transfers between devices, permute(): return lax.ppermute(values, AXES, pairs)  34 us
    ppermute x26, waiting for transfers between devices, permute(): return lax.ppermute(values, AXES, pairs)  15.2 us
    pallas_call x6, Pallas kernels, load(): pl.pallas_call(functools.partial(load_kernel, layers), out_shape=pltpu.VM...  2.15 us
    pallas_call x8, Pallas kernels, step(): pl.pallas_call(functools.partial(kernel, layer, tuple(operands)), out_sha...  1.32 us
  transfers between devices with their start and end apart: 26, of which 13 were waited for; matrix products, arithmetic and copies ran while one was open for 1% of the time, Pallas kernels for 4%

profile of v5, /device:TPU:6, one launch (start us, length us, event | category | flops | bytes accessed | tf_op | source)
XLA Modules:
  0.0 55.1 jit_solution(14333201439233062836)
XLA Ops:
  0.6 6.9 %collective-permute-start = (bf16[2,64,512]{2,1,0:T(8,128)(2,1)}, bf16[2,64,512]{2,1,0:T(8,128)(2,1)S(1)}, u32[]{:S(2)}, u32[]{:S(2)}) collective-permute-start(bf16[2,64,512]{2,1,0:T(8,128)(2,1)} %bitcast.7), channel_id=1, source_target_pairs={{0,64},{1,66},{2,65},{3,68},{4,67},{5,70},{6,69},{7,72},{8,71},{9,... | collective-permute-start | bytes 393224 | tf_op jit(solution)/shard_map/ppermute | solution.py:91
  7.5 0.5 collective-permute-start.2
  8.0 0.9 %copy-done = bf16[1,2,64,512]{3,2,1,0:T(8,128)(2,1)S(1)} copy-done((bf16[1,2,64,512]{3,2,1,0:T(8,128)(2,1)S(1)}, bf16[1,2,64,512]{3,2,1,0:T(8,128)(2,1)}, u32[]{:S(2)}) %copy-start) | copy-done | bytes 131096
  8.9 0.1 shard_map.50.refs_3_
  9.0 1.4 %collective-permute-done.refs_0_ = bf16[2,64,512]{2,1,0:T(8,128)(2,1)S(1)} collective-permute-done((bf16[2,64,512]{2,1,0:T(8,128)(2,1)}, bf16[2,64,512]{2,1,0:T(8,128)(2,1)S(1)}, u32[]{:S(2)}, u32[]{:S(2)}) %collective-permute-start) | collective-permute-done | bytes 131104 | tf_op jit(solution)/shard_map/ppermute | solution.py:91
  10.3 0.0 collective-permute-done.1.refs_1_
  10.4 1.4 %collective-permute-start.3 = (bf16[2,64,512]{2,1,0:T(8,128)(2,1)S(1)}, bf16[2,64,512]{2,1,0:T(8,128)(2,1)S(1)}, u32[]{:S(2)}, u32[]{:S(2)}) collective-permute-start(bf16[2,64,512]{2,1,0:T(8,128)(2,1)S(1)} %shard_map.51.after_ref.refs_4_.refs_6_), channel_id=1, source_target_pairs={{79,143},{80,144},{95,159},{96,160},{111,175},{112,176},{143,207},... | collective-permute-start | bytes 393224 | tf_op jit(solution)/shard_map/ppermute | solution.py:91
  11.7 0.1 collective-permute-start.7
  11.8 1.2 %collective-permute-start.8 = (bf16[2,64,512]{2,1,0:T(8,128)(2,1)S(1)}, bf16[2,64,512]{2,1,0:T(8,128)(2,1)S(1)}, u32[]{:S(2)}, u32[]{:S(2)}) collective-permute-start(bf16[2,64,512]{2,1,0:T(8,128)(2,1)S(1)} %shard_map.51.after_ref.refs_4_.refs_6_), channel_id=1, source_target_pairs={{79,144},{80,143},{95,160},{96,159},{111,176},{112,175},{143,207},... | collective-permute-start | bytes 393224 | tf_op jit(solution)/shard_map/ppermute | solution.py:91
  13.1 3.5 %collective-permute-done.3.refs_2_ = bf16[2,64,512]{2,1,0:T(8,128)(2,1)S(1)} collective-permute-done((bf16[2,64,512]{2,1,0:T(8,128)(2,1)S(1)}, bf16[2,64,512]{2,1,0:T(8,128)(2,1)S(1)}, u32[]{:S(2)}, u32[]{:S(2)}) %collective-permute-start.3) | collective-permute-done | bytes 131104 | tf_op jit(solution)/shard_map/ppermute | solution.py:91
  16.6 0.0 collective-permute-start.4
  16.6 0.5 collective-permute-start.5
  17.1 0.0 collective-permute-start.6
  17.1 0.1 shard_map.52.refs_3_.refs_5_
  17.2 3.2 %collective-permute-done.7.refs_1_.refs_3_ = bf16[2,64,512]{2,1,0:T(8,128)(2,1)S(1)} collective-permute-done((bf16[2,64,512]{2,1,0:T(8,128)(2,1)S(1)}, bf16[2,64,512]{2,1,0:T(8,128)(2,1)S(1)}, u32[]{:S(2)}, u32[]{:S(2)}) %collective-permute-start.7) | collective-permute-done | bytes 131104 | tf_op jit(solution)/shard_map/ppermute | solution.py:91
  20.3 1.4 %collective-permute-done.8.refs_0_ = bf16[2,64,512]{2,1,0:T(8,128)(2,1)S(1)} collective-permute-done((bf16[2,64,512]{2,1,0:T(8,128)(2,1)S(1)}, bf16[2,64,512]{2,1,0:T(8,128)(2,1)S(1)}, u32[]{:S(2)}, u32[]{:S(2)}) %collective-permute-start.8) | collective-permute-done | bytes 131104 | tf_op jit(solution)/shard_map/ppermute | solution.py:91
  21.8 0.6 %collective-permute-start.10 = (bf16[2,64,512]{2,1,0:T(8,128)(2,1)S(1)}, bf16[2,64,512]{2,1,0:T(8,128)(2,1)S(1)}, u32[]{:S(2)}, u32[]{:S(2)}) collective-permute-start(bf16[2,64,512]{2,1,0:T(8,128)(2,1)S(1)} %shard_map.54.after_ref.refs_4_), channel_id=1, source_target_pairs={{128,192},{129,194},{130,193},{131,196},{132,195},{133,198},{134,1... | collective-permute-start | bytes 393224 | tf_op jit(solution)/shard_map/ppermute | solution.py:91
  22.4 0.1 collective-permute-start.11
  22.5 0.4 collective-permute-start.9
  22.9 0.1 shard_map.55.refs_3_
  23.0 0.1 collective-permute-done.12.refs_4_
  23.1 0.3 collective-permute-done.10.refs_1_
  23.4 0.4 collective-permute-done.11.refs_2_
  23.7 0.2 collective-permute-done.9.refs_0_
  23.9 0.3 collective-permute-start.13
  24.3 0.2 collective-permute-start.14
  24.4 0.3 collective-permute-start.15
  24.8 0.1 shard_map.57.refs_3_
  24.8 0.5 collective-permute-done.13.refs_0_
  25.3 0.3 collective-permute-done.14.refs_1_
  25.6 0.2 collective-permute-done.15.refs_2_
  25.8 6.1 %collective-permute-start.16 = (bf16[2,64,512]{2,1,0:T(8,128)(2,1)S(1)}, bf16[2,64,512]{2,1,0:T(8,128)(2,1)S(1)}, u32[]{:S(2)}, u32[]{:S(2)}) collective-permute-start(bf16[2,64,512]{2,1,0:T(8,128)(2,1)S(1)} %shard_map.58.after_ref), channel_id=1, source_target_pairs={{143,79},{144,80},{159,95},{160,96},{175,111},{176,112},{79,15},{8... | collective-permute-start | bytes 393224 | tf_op jit(solution)/shard_map/ppermute | solution.py:91
  31.8 8.8 %collective-permute-start.20 = (bf16[2,64,512]{2,1,0:T(8,128)(2,1)S(1)}, bf16[2,64,512]{2,1,0:T(8,128)(2,1)S(1)}, u32[]{:S(2)}, u32[]{:S(2)}) collective-permute-start(bf16[2,64,512]{2,1,0:T(8,128)(2,1)S(1)} %shard_map.58.after_ref), channel_id=1, source_target_pairs={{142,79},{143,78},{144,81},{145,80},{158,95},{159,94},{160,97},{16... | collective-permute-start | bytes 393224 | tf_op jit(solution)/shard_map/ppermute | solution.py:91
  40.7 0.1 collective-permute-start.21
  40.8 0.0 collective-permute-done.16.refs_2_
  40.8 2.3 %collective-permute-start.17 = (bf16[2,64,512]{2,1,0:T(8,128)(2,1)S(1)}, bf16[2,64,512]{2,1,0:T(8,128)(2,1)S(1)}, u32[]{:S(2)}, u32[]{:S(2)}) collective-permute-start(bf16[2,64,512]{2,1,0:T(8,128)(2,1)S(1)} %collective-permute-done.16.refs_2_), channel_id=1, source_target_pairs={{0,64},{1,66},{2,65},{3,68},{4,67},{5,70},{6,69},{7,72},{8,71},{9,... | collective-permute-start | bytes 393224 | tf_op jit(solution)/shard_map/ppermute | solution.py:91
  43.1 0.0 collective-permute-start.18
  43.1 0.5 collective-permute-start.19
  43.6 0.1 shard_map.59.refs_3_.refs_5_
  43.7 0.9 %collective-permute-done.21.refs_0_ = bf16[2,64,512]{2,1,0:T(8,128)(2,1)S(1)} collective-permute-done((bf16[2,64,512]{2,1,0:T(8,128)(2,1)S(1)}, bf16[2,64,512]{2,1,0:T(8,128)(2,1)S(1)}, u32[]{:S(2)}, u32[]{:S(2)}) %collective-permute-start.21) | collective-permute-done | bytes 131104 | tf_op jit(solution)/shard_map/ppermute | solution.py:91
  44.6 1.6 %collective-permute-start.25 = (bf16[2,64,512]{2,1,0:T(8,128)(2,1)S(1)}, bf16[2,64,512]{2,1,0:T(8,128)(2,1)S(1)}, u32[]{:S(2)}, u32[]{:S(2)}) collective-permute-start(bf16[2,64,512]{2,1,0:T(8,128)(2,1)S(1)} %shard_map.60.refs_4_), channel_id=1, source_target_pairs={{79,16},{80,15},{95,32},{96,31},{111,48},{112,47},{15,79},{16,80},... | collective-permute-start | bytes 393224 | tf_op jit(solution)/shard_map/ppermute | solution.py:91
  46.3 1.9 %collective-permute-start.22 = (bf16[2,64,512]{2,1,0:T(8,128)(2,1)S(1)}, bf16[2,64,512]{2,1,0:T(8,128)(2,1)S(1)}, u32[]{:S(2)}, u32[]{:S(2)}) collective-permute-start(bf16[2,64,512]{2,1,0:T(8,128)(2,1)S(1)} %shard_map.61), channel_id=1, source_target_pairs={{64,0},{65,2},{66,1},{67,4},{68,3},{69,6},{70,5},{71,8},{72,7},{73... | collective-permute-start | bytes 393224 | tf_op jit(solution)/shard_map/ppermute | solution.py:91
  48.1 0.1 collective-permute-start.23
  48.2 0.1 collective-permute-start.24
  48.3 0.7 %select_select_fusion = (bf16[2,64,512]{2,1,0:T(8,128)(2,1)S(1)}, bf16[1,2,64,512]{3,2,1,0:T(8,128)(2,1)}) fusion(bf16[2,64,512]{2,1,0:T(8,128)(2,1)S(1)} %shard_map.61, bf16[2,64,512]{2,1,0:T(8,128)(2,1)S(1)} %shard_map.58.after_ref, bf16[2,64,512]{2,1,0:T(8,128)(2,1)S(1)} %shard_map.56.after_ref, pred[]{:T(512)S(6)} %eq.13, pred[]{:T(512)S(6)} %eq.12, ...), kind=kLoop, calls=%fused_computation | loop fusion | flops 327680 | bytes 1048579 | tf_op jit(solution)/shard_map/jit(_where)/select_n | solution.py:255
  49.0 1.9 %shard_map.62.refs_3_ = bf16[3,2,512,512]{3,2,1,0:T(8,128)(2,1)S(1)} custom-call(bf16[3,2,512,512]{3,2,1,0:T(8,128)(2,1)} %bitcast.21, bf16[2,64,512]{2,1,0:T(8,128)(2,1)S(1)} %get-tuple-element.2.after_ref.refs_6_), custom_call_target="tpu_custom_call" | custom-call | bytes 6291456 | tf_op jit(solution)/shard_map/pallas_call | solution.py:112
  50.9 2.9 %collective-permute-done.25.refs_4_ = bf16[2,64,512]{2,1,0:T(8,128)(2,1)S(1)} collective-permute-done((bf16[2,64,512]{2,1,0:T(8,128)(2,1)S(1)}, bf16[2,64,512]{2,1,0:T(8,128)(2,1)S(1)}, u32[]{:S(2)}, u32[]{:S(2)}) %collective-permute-start.25) | collective-permute-done | bytes 131104 | tf_op jit(solution)/shard_map/ppermute | solution.py:91
  53.8 1.3 %shard_map.63 = bf16[2,64,512]{2,1,0:T(8,128)(2,1)} custom-call(bf16[2,64,512]{2,1,0:T(8,128)(2,1)S(1)} %collective-permute-done.22.refs_0_, bf16[2,64,512]{2,1,0:T(8,128)(2,1)S(1)} %collective-permute-done.23.refs_1_, bf16[2,64,512]{2,1,0:T(8,128)(2,1)S(1)} %collective-permute-done.24.refs_2_, bf16[3,2,512,512]{3,2,1,0:T(8,128)(2,1)S(1)} %shard_map.62.refs_3_, ...), custom_call_target="tpu_custom_call" | custom-call | flops 402653184 | bytes 3801088 | tf_op jit(solution)/shard_map/pallas_call | solution.py:202
  (23 shorter events, 0.1 us)
Async XLA Ops:
  0.6 9.7 %collective-permute-start = (bf16[2,64,512]{2,1,0:T(8,128)(2,1)}, bf16[2,64,512]{2,1,0:T(8,128)(2,1)S(1)}, u32[]{:S(2)}, u32[]{:S(2)}) collective-permute-start(bf16[2,64,512]{2,1,0:T(8,128)(2,1)} %bitcast.7), channel_id=1, source_target_pairs={{0,64},{1,66},{2,65},{3,68},{4,67},{5,70},{6,69},{7,72},{8,71},{9,... | collective-permute-start | bytes 393224 | tf_op jit(solution)/shard_map/ppermute | solution.py:91
  7.5 2.9 %collective-permute-start.1 = (bf16[2,64,512]{2,1,0:T(8,128)(2,1)}, bf16[2,64,512]{2,1,0:T(8,128)(2,1)S(1)}, u32[]{:S(2)}, u32[]{:S(2)}) collective-permute-start(bf16[2,64,512]{2,1,0:T(8,128)(2,1)} %bitcast.8), channel_id=1, source_target_pairs={{0,65},{1,64},{2,67},{3,66},{4,69},{5,68},{6,71},{7,70},{8,73},{9,... | collective-permute-start | bytes 393224 | tf_op jit(solution)/shard_map/ppermute | solution.py:91
  7.5 2.9 %collective-permute-start.2 = (bf16[2,64,512]{2,1,0:T(8,128)(2,1)}, bf16[2,64,512]{2,1,0:T(8,128)(2,1)S(1)}, u32[]{:S(2)}, u32[]{:S(2)}) collective-permute-start(bf16[2,64,512]{2,1,0:T(8,128)(2,1)} %bitcast.9), channel_id=1, source_target_pairs={{0,64},{1,65},{2,66},{3,67},{4,68},{5,69},{6,70},{7,71},{8,72},{9,... | collective-permute-start | bytes 393224 | tf_op jit(solution)/shard_map/ppermute | solution.py:91
  8.0 0.9 %copy-start = (bf16[1,2,64,512]{3,2,1,0:T(8,128)(2,1)S(1)}, bf16[1,2,64,512]{3,2,1,0:T(8,128)(2,1)}, u32[]{:S(2)}) copy-start(bf16[1,2,64,512]{3,2,1,0:T(8,128)(2,1)} %param.3) | copy-start | bytes 393220
  10.4 11.4 %copy-start.1 = (bf16[1,2,64,512]{3,2,1,0:T(8,128)(2,1)S(1)}, bf16[1,2,64,512]{3,2,1,0:T(8,128)(2,1)}, u32[]{:S(2)}) copy-start(bf16[1,2,64,512]{3,2,1,0:T(8,128)(2,1)} %param.3) | copy-start | bytes 393220
  10.4 6.2 %collective-permute-start.3 = (bf16[2,64,512]{2,1,0:T(8,128)(2,1)S(1)}, bf16[2,64,512]{2,1,0:T(8,128)(2,1)S(1)}, u32[]{:S(2)}, u32[]{:S(2)}) collective-permute-start(bf16[2,64,512]{2,1,0:T(8,128)(2,1)S(1)} %shard_map.51.after_ref.refs_4_.refs_6_), channel_id=1, source_target_pairs={{79,143},{80,144},{95,159},{96,160},{111,175},{112,176},{143,207},... | collective-permute-start | bytes 393224 | tf_op jit(solution)/shard_map/ppermute | solution.py:91
  11.7 8.6 %collective-permute-start.7 = (bf16[2,64,512]{2,1,0:T(8,128)(2,1)S(1)}, bf16[2,64,512]{2,1,0:T(8,128)(2,1)S(1)}, u32[]{:S(2)}, u32[]{:S(2)}) collective-permute-start(bf16[2,64,512]{2,1,0:T(8,128)(2,1)S(1)} %shard_map.51.after_ref.refs_4_.refs_6_), channel_id=1, source_target_pairs={{78,143},{79,142},{80,145},{81,144},{94,159},{95,158},{96,161},{97... | collective-permute-start | bytes 393224 | tf_op jit(solution)/shard_map/ppermute | solution.py:91
  11.8 9.9 %collective-permute-start.8 = (bf16[2,64,512]{2,1,0:T(8,128)(2,1)S(1)}, bf16[2,64,512]{2,1,0:T(8,128)(2,1)S(1)}, u32[]{:S(2)}, u32[]{:S(2)}) collective-permute-start(bf16[2,64,512]{2,1,0:T(8,128)(2,1)S(1)} %shard_map.51.after_ref.refs_4_.refs_6_), channel_id=1, source_target_pairs={{79,144},{80,143},{95,160},{96,159},{111,176},{112,175},{143,207},... | collective-permute-start | bytes 393224 | tf_op jit(solution)/shard_map/ppermute | solution.py:91
  16.6 5.2 %collective-permute-start.4 = (bf16[2,64,512]{2,1,0:T(8,128)(2,1)S(1)}, bf16[2,64,512]{2,1,0:T(8,128)(2,1)S(1)}, u32[]{:S(2)}, u32[]{:S(2)}) collective-permute-start(bf16[2,64,512]{2,1,0:T(8,128)(2,1)S(1)} %collective-permute-done.3.refs_2_), channel_id=1, source_target_pairs={{192,128},{193,130},{194,129},{195,132},{196,131},{197,134},{198,1... | collective-permute-start | bytes 393224 | tf_op jit(solution)/shard_map/ppermute | solution.py:91
  16.6 5.2 %collective-permute-start.5 = (bf16[2,64,512]{2,1,0:T(8,128)(2,1)S(1)}, bf16[2,64,512]{2,1,0:T(8,128)(2,1)S(1)}, u32[]{:S(2)}, u32[]{:S(2)}) collective-permute-start(bf16[2,64,512]{2,1,0:T(8,128)(2,1)S(1)} %collective-permute-done.3.refs_2_), channel_id=1, source_target_pairs={{192,129},{193,128},{194,131},{195,130},{196,133},{197,132},{198,1... | collective-permute-start | bytes 393224 | tf_op jit(solution)/shard_map/ppermute | solution.py:91
  17.1 4.7 %collective-permute-start.6 = (bf16[2,64,512]{2,1,0:T(8,128)(2,1)S(1)}, bf16[2,64,512]{2,1,0:T(8,128)(2,1)S(1)}, u32[]{:S(2)}, u32[]{:S(2)}) collective-permute-start(bf16[2,64,512]{2,1,0:T(8,128)(2,1)S(1)} %collective-permute-done.3.refs_2_), channel_id=1, source_target_pairs={{192,128},{193,129},{194,130},{195,131},{196,132},{197,133},{198,1... | collective-permute-start | bytes 393224 | tf_op jit(solution)/shard_map/ppermute | solution.py:91
  21.7 1.3 %collective-permute-start.12 = (bf16[2,64,512]{2,1,0:T(8,128)(2,1)S(1)}, bf16[2,64,512]{2,1,0:T(8,128)(2,1)S(1)}, u32[]{:S(2)}, u32[]{:S(2)}) collective-permute-start(bf16[2,64,512]{2,1,0:T(8,128)(2,1)S(1)} %shard_map.53.refs_4_), channel_id=1, source_target_pairs={{143,208},{144,207},{159,224},{160,223},{175,240},{176,239},{207,1... | collective-permute-start | bytes 393224 | tf_op jit(solution)/shard_map/ppermute | solution.py:91
  21.8 1.6 %collective-permute-start.10 = (bf16[2,64,512]{2,1,0:T(8,128)(2,1)S(1)}, bf16[2,64,512]{2,1,0:T(8,128)(2,1)S(1)}, u32[]{:S(2)}, u32[]{:S(2)}) collective-permute-start(bf16[2,64,512]{2,1,0:T(8,128)(2,1)S(1)} %shard_map.54.after_ref.refs_4_), channel_id=1, source_target_pairs={{128,192},{129,194},{130,193},{131,196},{132,195},{133,198},{134,1... | collective-permute-start | bytes 393224 | tf_op jit(solution)/shard_map/ppermute | solution.py:91
  22.4 1.3 %collective-permute-start.11 = (bf16[2,64,512]{2,1,0:T(8,128)(2,1)S(1)}, bf16[2,64,512]{2,1,0:T(8,128)(2,1)S(1)}, u32[]{:S(2)}, u32[]{:S(2)}) collective-permute-start(bf16[2,64,512]{2,1,0:T(8,128)(2,1)S(1)} %shard_map.54.after_ref.refs_4_), channel_id=1, source_target_pairs={{128,193},{129,192},{130,195},{131,194},{132,197},{133,196},{134,1... | collective-permute-start | bytes 393224 | tf_op jit(solution)/shard_map/ppermute | solution.py:91
  22.5 1.4 %collective-permute-start.9 = (bf16[2,64,512]{2,1,0:T(8,128)(2,1)S(1)}, bf16[2,64,512]{2,1,0:T(8,128)(2,1)S(1)}, u32[]{:S(2)}, u32[]{:S(2)}) collective-permute-start(bf16[2,64,512]{2,1,0:T(8,128)(2,1)S(1)} %shard_map.54.after_ref.refs_4_), channel_id=1, source_target_pairs={{128,192},{129,193},{130,194},{131,195},{132,196},{133,197},{134,1... | collective-permute-start | bytes 393224 | tf_op jit(solution)/shard_map/ppermute | solution.py:91
  23.9 1.3 %collective-permute-start.13 = (bf16[2,64,512]{2,1,0:T(8,128)(2,1)S(1)}, bf16[2,64,512]{2,1,0:T(8,128)(2,1)S(1)}, u32[]{:S(2)}, u32[]{:S(2)}) collective-permute-start(bf16[2,64,512]{2,1,0:T(8,128)(2,1)S(1)} %shard_map.56.after_ref), channel_id=1, source_target_pairs={{192,128},{193,130},{194,129},{195,132},{196,131},{197,134},{198,1... | collective-permute-start | bytes 393224 | tf_op jit(solution)/shard_map/ppermute | solution.py:91
  24.3 1.3 %collective-permute-start.14 = (bf16[2,64,512]{2,1,0:T(8,128)(2,1)S(1)}, bf16[2,64,512]{2,1,0:T(8,128)(2,1)S(1)}, u32[]{:S(2)}, u32[]{:S(2)}) collective-permute-start(bf16[2,64,512]{2,1,0:T(8,128)(2,1)S(1)} %shard_map.56.after_ref), channel_id=1, source_target_pairs={{192,129},{193,128},{194,131},{195,130},{196,133},{197,132},{198,1... | collective-permute-start | bytes 393224 | tf_op jit(solution)/shard_map/ppermute | solution.py:91
  24.4 1.3 %collective-permute-start.15 = (bf16[2,64,512]{2,1,0:T(8,128)(2,1)S(1)}, bf16[2,64,512]{2,1,0:T(8,128)(2,1)S(1)}, u32[]{:S(2)}, u32[]{:S(2)}) collective-permute-start(bf16[2,64,512]{2,1,0:T(8,128)(2,1)S(1)} %shard_map.56.after_ref), channel_id=1, source_target_pairs={{192,128},{193,129},{194,130},{195,131},{196,132},{197,133},{198,1... | collective-permute-start | bytes 393224 | tf_op jit(solution)/shard_map/ppermute | solution.py:91
  25.8 15.0 %collective-permute-start.16 = (bf16[2,64,512]{2,1,0:T(8,128)(2,1)S(1)}, bf16[2,64,512]{2,1,0:T(8,128)(2,1)S(1)}, u32[]{:S(2)}, u32[]{:S(2)}) collective-permute-start(bf16[2,64,512]{2,1,0:T(8,128)(2,1)S(1)} %shard_map.58.after_ref), channel_id=1, source_target_pairs={{143,79},{144,80},{159,95},{160,96},{175,111},{176,112},{79,15},{8... | collective-permute-start | bytes 393224 | tf_op jit(solution)/shard_map/ppermute | solution.py:91
  31.8 11.8 %collective-permute-start.20 = (bf16[2,64,512]{2,1,0:T(8,128)(2,1)S(1)}, bf16[2,64,512]{2,1,0:T(8,128)(2,1)S(1)}, u32[]{:S(2)}, u32[]{:S(2)}) collective-permute-start(bf16[2,64,512]{2,1,0:T(8,128)(2,1)S(1)} %shard_map.58.after_ref), channel_id=1, source_target_pairs={{142,79},{143,78},{144,81},{145,80},{158,95},{159,94},{160,97},{16... | collective-permute-start | bytes 393224 | tf_op jit(solution)/shard_map/ppermute | solution.py:91
  40.7 3.9 %collective-permute-start.21 = (bf16[2,64,512]{2,1,0:T(8,128)(2,1)S(1)}, bf16[2,64,512]{2,1,0:T(8,128)(2,1)S(1)}, u32[]{:S(2)}, u32[]{:S(2)}) collective-permute-start(bf16[2,64,512]{2,1,0:T(8,128)(2,1)S(1)} %shard_map.58.after_ref), channel_id=1, source_target_pairs={{143,80},{144,79},{159,96},{160,95},{175,112},{176,111},{79,15},{8... | collective-permute-start | bytes 393224 | tf_op jit(solution)/shard_map/ppermute | solution.py:91
  40.8 5.4 %collective-permute-start.17 = (bf16[2,64,512]{2,1,0:T(8,128)(2,1)S(1)}, bf16[2,64,512]{2,1,0:T(8,128)(2,1)S(1)}, u32[]{:S(2)}, u32[]{:S(2)}) collective-permute-start(bf16[2,64,512]{2,1,0:T(8,128)(2,1)S(1)} %collective-permute-done.16.refs_2_), channel_id=1, source_target_pairs={{0,64},{1,66},{2,65},{3,68},{4,67},{5,70},{6,69},{7,72},{8,71},{9,... | collective-permute-start | bytes 393224 | tf_op jit(solution)/shard_map/ppermute | solution.py:91
  43.1 3.1 %collective-permute-start.18 = (bf16[2,64,512]{2,1,0:T(8,128)(2,1)S(1)}, bf16[2,64,512]{2,1,0:T(8,128)(2,1)S(1)}, u32[]{:S(2)}, u32[]{:S(2)}) collective-permute-start(bf16[2,64,512]{2,1,0:T(8,128)(2,1)S(1)} %collective-permute-done.16.refs_2_), channel_id=1, source_target_pairs={{0,65},{1,64},{2,67},{3,66},{4,69},{5,68},{6,71},{7,70},{8,73},{9,... | collective-permute-start | bytes 393224 | tf_op jit(solution)/shard_map/ppermute | solution.py:91
  43.1 3.1 %collective-permute-start.19 = (bf16[2,64,512]{2,1,0:T(8,128)(2,1)S(1)}, bf16[2,64,512]{2,1,0:T(8,128)(2,1)S(1)}, u32[]{:S(2)}, u32[]{:S(2)}) collective-permute-start(bf16[2,64,512]{2,1,0:T(8,128)(2,1)S(1)} %collective-permute-done.16.refs_2_), channel_id=1, source_target_pairs={{0,64},{1,65},{2,66},{3,67},{4,68},{5,69},{6,70},{7,71},{8,72},{9,... | collective-permute-start | bytes 393224 | tf_op jit(solution)/shard_map/ppermute | solution.py:91
  44.6 9.2 %collective-permute-start.25 = (bf16[2,64,512]{2,1,0:T(8,128)(2,1)S(1)}, bf16[2,64,512]{2,1,0:T(8,128)(2,1)S(1)}, u32[]{:S(2)}, u32[]{:S(2)}) collective-permute-start(bf16[2,64,512]{2,1,0:T(8,128)(2,1)S(1)} %shard_map.60.refs_4_), channel_id=1, source_target_pairs={{79,16},{80,15},{95,32},{96,31},{111,48},{112,47},{15,79},{16,80},... | collective-permute-start | bytes 393224 | tf_op jit(solution)/shard_map/ppermute | solution.py:91
  46.3 7.5 %collective-permute-start.22 = (bf16[2,64,512]{2,1,0:T(8,128)(2,1)S(1)}, bf16[2,64,512]{2,1,0:T(8,128)(2,1)S(1)}, u32[]{:S(2)}, u32[]{:S(2)}) collective-permute-start(bf16[2,64,512]{2,1,0:T(8,128)(2,1)S(1)} %shard_map.61), channel_id=1, source_target_pairs={{64,0},{65,2},{66,1},{67,4},{68,3},{69,6},{70,5},{71,8},{72,7},{73... | collective-permute-start | bytes 393224 | tf_op jit(solution)/shard_map/ppermute | solution.py:91
  48.1 5.6 %collective-permute-start.23 = (bf16[2,64,512]{2,1,0:T(8,128)(2,1)S(1)}, bf16[2,64,512]{2,1,0:T(8,128)(2,1)S(1)}, u32[]{:S(2)}, u32[]{:S(2)}) collective-permute-start(bf16[2,64,512]{2,1,0:T(8,128)(2,1)S(1)} %shard_map.61), channel_id=1, source_target_pairs={{64,1},{65,0},{66,3},{67,2},{68,5},{69,4},{70,7},{71,6},{72,9},{73... | collective-permute-start | bytes 393224 | tf_op jit(solution)/shard_map/ppermute | solution.py:91
  48.2 5.6 %collective-permute-start.24 = (bf16[2,64,512]{2,1,0:T(8,128)(2,1)S(1)}, bf16[2,64,512]{2,1,0:T(8,128)(2,1)S(1)}, u32[]{:S(2)}, u32[]{:S(2)}) collective-permute-start(bf16[2,64,512]{2,1,0:T(8,128)(2,1)S(1)} %shard_map.61), channel_id=1, source_target_pairs={{64,0},{65,1},{66,2},{67,3},{68,4},{69,5},{70,6},{71,7},{72,8},{73... | collective-permute-start | bytes 393224 | tf_op jit(solution)/shard_map/ppermute | solution.py:91

commit v6 on v5

--- a/solution.py
+++ b/solution.py
@@ -234,7 +234,7 @@
     relay = target ^ 1
     held = load(blocks, values, target)
     crossed = permute(values, across(source, target, tiles))
-    seam = permute(values, else_on_chip(around(source, target, far_mate, far_mate), tiles, at_seam))
+    seam = permute(values, else_on_chip(around(source, target, far_mate, same), tiles, at_seam))
     direct = permute(values, else_on_chip(around(source, target, near_mate, over), tiles, by_seam))
     early = step(target, seam_kernel, far=seam, near=direct, own=crossed, blocks=held, addend=addend)
     passed = permute(early, else_on_chip(within_chip(target, relay, far_mate), tiles, at_seam))

time: 55.2 us -> 54.4 us (0.986)
  starting transfers between devices: 34 us -> 32.2 us
  waiting for transfers between devices: 15.2 us -> 16.3 us
    ppermute x26, starting transfers between devices: 34 us -> 32.2 us  [permute(): return lax.ppermute(values, AXES, pairs)]
    ppermute x26, waiting for transfers between devices: 15.2 us -> 16.3 us  [permute(): return lax.ppermute(values, AXES, pairs)]
  transfers between devices with their start and end apart: 26 -> 26, of which waited for: 13 -> 12; matrix products, arithmetic and copies ran while one was open for 1% -> 1% of each run, Pallas kernels for 4% -> 4%
where the time goes in v6:
time: 54.4 us; the launch traced here: 54.3 us
  starting transfers between devices  32.2 us (59%)
  waiting for transfers between devices  16.3 us (30%)
  Pallas kernels  3.48 us (6%)
  local copies, waits for them, and re-layouts  0.91 us (2%)
  between operations  0.77 us (1%)
  other arithmetic  0.69 us (1%)
    ppermute x26, starting transfers between devices, permute(): return lax.ppermute(values, AXES, pairs)  32.2 us
    ppermute x26, waiting for transfers between devices, permute(): return lax.ppermute(values, AXES, pairs)  16.3 us
    pallas_call x6, Pallas kernels, load(): pl.pallas_call(functools.partial(load_kernel, layers), out_shape=pltpu.VM...  2.15 us
    pallas_call x8, Pallas kernels, step(): pl.pallas_call(functools.partial(kernel, layer, tuple(operands)), out_sha...  1.34 us
  transfers between devices with their start and end apart: 26, of which 12 were waited for; matrix products, arithmetic and copies ran while one was open for 1% of the time, Pallas kernels for 4%

profile of v6, /device:TPU:6, one launch (start us, length us, event | category | flops | bytes accessed | tf_op | source)
XLA Modules:
  0.0 54.3 jit_solution(793923763202689634)
XLA Ops:
  0.6 6.9 %collective-permute-start = (bf16[2,64,512]{2,1,0:T(8,128)(2,1)}, bf16[2,64,512]{2,1,0:T(8,128)(2,1)S(1)}, u32[]{:S(2)}, u32[]{:S(2)}) collective-permute-start(bf16[2,64,512]{2,1,0:T(8,128)(2,1)} %bitcast.7), channel_id=1, source_target_pairs={{0,64},{1,66},{2,65},{3,68},{4,67},{5,70},{6,69},{7,72},{8,71},{9,... | collective-permute-start | bytes 393224 | tf_op jit(solution)/shard_map/ppermute | solution.py:91
  7.5 0.5 collective-permute-start.2
  8.0 0.9 %copy-done = bf16[1,2,64,512]{3,2,1,0:T(8,128)(2,1)S(1)} copy-done((bf16[1,2,64,512]{3,2,1,0:T(8,128)(2,1)S(1)}, bf16[1,2,64,512]{3,2,1,0:T(8,128)(2,1)}, u32[]{:S(2)}) %copy-start) | copy-done | bytes 131096
  8.9 0.1 shard_map.50.refs_3_
  9.0 1.4 %collective-permute-done.refs_0_ = bf16[2,64,512]{2,1,0:T(8,128)(2,1)S(1)} collective-permute-done((bf16[2,64,512]{2,1,0:T(8,128)(2,1)}, bf16[2,64,512]{2,1,0:T(8,128)(2,1)S(1)}, u32[]{:S(2)}, u32[]{:S(2)}) %collective-permute-start) | collective-permute-done | bytes 131104 | tf_op jit(solution)/shard_map/ppermute | solution.py:91
  10.3 0.0 collective-permute-done.1.refs_1_
  10.4 1.4 %collective-permute-start.3 = (bf16[2,64,512]{2,1,0:T(8,128)(2,1)S(1)}, bf16[2,64,512]{2,1,0:T(8,128)(2,1)S(1)}, u32[]{:S(2)}, u32[]{:S(2)}) collective-permute-start(bf16[2,64,512]{2,1,0:T(8,128)(2,1)S(1)} %shard_map.51.after_ref.refs_4_.refs_6_), channel_id=1, source_target_pairs={{79,143},{80,144},{95,159},{96,160},{111,175},{112,176},{143,207},... | collective-permute-start | bytes 393224 | tf_op jit(solution)/shard_map/ppermute | solution.py:91
  11.7 0.1 collective-permute-start.7
  11.8 1.2 %collective-permute-start.8 = (bf16[2,64,512]{2,1,0:T(8,128)(2,1)S(1)}, bf16[2,64,512]{2,1,0:T(8,128)(2,1)S(1)}, u32[]{:S(2)}, u32[]{:S(2)}) collective-permute-start(bf16[2,64,512]{2,1,0:T(8,128)(2,1)S(1)} %shard_map.51.after_ref.refs_4_.refs_6_), channel_id=1, source_target_pairs={{79,144},{80,143},{95,160},{96,159},{111,176},{112,175},{143,207},... | collective-permute-start | bytes 393224 | tf_op jit(solution)/shard_map/ppermute | solution.py:91
  13.1 3.5 %collective-permute-done.3.refs_2_ = bf16[2,64,512]{2,1,0:T(8,128)(2,1)S(1)} collective-permute-done((bf16[2,64,512]{2,1,0:T(8,128)(2,1)S(1)}, bf16[2,64,512]{2,1,0:T(8,128)(2,1)S(1)}, u32[]{:S(2)}, u32[]{:S(2)}) %collective-permute-start.3) | collective-permute-done | bytes 131104 | tf_op jit(solution)/shard_map/ppermute | solution.py:91
  16.6 0.0 collective-permute-start.4
  16.6 0.5 collective-permute-start.5
  17.1 0.0 collective-permute-start.6
  17.1 0.1 shard_map.52.refs_3_.refs_5_
  17.2 3.2 %collective-permute-done.7.refs_1_.refs_3_ = bf16[2,64,512]{2,1,0:T(8,128)(2,1)S(1)} collective-permute-done((bf16[2,64,512]{2,1,0:T(8,128)(2,1)S(1)}, bf16[2,64,512]{2,1,0:T(8,128)(2,1)S(1)}, u32[]{:S(2)}, u32[]{:S(2)}) %collective-permute-start.7) | collective-permute-done | bytes 131104 | tf_op jit(solution)/shard_map/ppermute | solution.py:91
  20.3 2.8 %collective-permute-done.8.refs_0_ = bf16[2,64,512]{2,1,0:T(8,128)(2,1)S(1)} collective-permute-done((bf16[2,64,512]{2,1,0:T(8,128)(2,1)S(1)}, bf16[2,64,512]{2,1,0:T(8,128)(2,1)S(1)}, u32[]{:S(2)}, u32[]{:S(2)}) %collective-permute-start.8) | collective-permute-done | bytes 131104 | tf_op jit(solution)/shard_map/ppermute | solution.py:91
  23.1 0.0 collective-permute-start.12
  23.1 0.0 collective-permute-done.6.refs_2_
  23.2 0.6 %collective-permute-start.10 = (bf16[2,64,512]{2,1,0:T(8,128)(2,1)S(1)}, bf16[2,64,512]{2,1,0:T(8,128)(2,1)S(1)}, u32[]{:S(2)}, u32[]{:S(2)}) collective-permute-start(bf16[2,64,512]{2,1,0:T(8,128)(2,1)S(1)} %shard_map.54.after_ref.refs_4_), channel_id=1, source_target_pairs={{128,192},{129,194},{130,193},{131,196},{132,195},{133,198},{134,1... | collective-permute-start | bytes 393224 | tf_op jit(solution)/shard_map/ppermute | solution.py:91
  23.8 0.1 collective-permute-start.11
  23.9 0.4 collective-permute-start.9
  24.3 0.1 shard_map.55.refs_3_
  24.3 0.1 collective-permute-done.12.refs_4_
  24.5 0.3 collective-permute-done.10.refs_1_
  24.7 0.4 collective-permute-done.11.refs_2_
  25.1 0.2 collective-permute-done.9.refs_0_
  25.3 0.3 collective-permute-start.13
  25.6 0.2 collective-permute-start.14
  25.8 0.3 collective-permute-start.15
  26.1 0.1 shard_map.57.refs_3_
  26.2 0.5 collective-permute-done.13.refs_0_
  26.6 0.3 collective-permute-done.14.refs_1_
  27.0 0.2 collective-permute-done.15.refs_2_
  27.2 4.7 %collective-permute-start.16 = (bf16[2,64,512]{2,1,0:T(8,128)(2,1)S(1)}, bf16[2,64,512]{2,1,0:T(8,128)(2,1)S(1)}, u32[]{:S(2)}, u32[]{:S(2)}) collective-permute-start(bf16[2,64,512]{2,1,0:T(8,128)(2,1)S(1)} %shard_map.58.after_ref), channel_id=1, source_target_pairs={{143,79},{144,80},{159,95},{160,96},{175,111},{176,112},{79,15},{8... | collective-permute-start | bytes 393224 | tf_op jit(solution)/shard_map/ppermute | solution.py:91
  31.8 7.6 %collective-permute-start.20 = (bf16[2,64,512]{2,1,0:T(8,128)(2,1)S(1)}, bf16[2,64,512]{2,1,0:T(8,128)(2,1)S(1)}, u32[]{:S(2)}, u32[]{:S(2)}) collective-permute-start(bf16[2,64,512]{2,1,0:T(8,128)(2,1)S(1)} %shard_map.58.after_ref), channel_id=1, source_target_pairs={{142,79},{143,78},{144,81},{145,80},{158,95},{159,94},{160,97},{16... | collective-permute-start | bytes 393224 | tf_op jit(solution)/shard_map/ppermute | solution.py:91
  39.5 1.1 %collective-permute-start.21 = (bf16[2,64,512]{2,1,0:T(8,128)(2,1)S(1)}, bf16[2,64,512]{2,1,0:T(8,128)(2,1)S(1)}, u32[]{:S(2)}, u32[]{:S(2)}) collective-permute-start(bf16[2,64,512]{2,1,0:T(8,128)(2,1)S(1)} %shard_map.58.after_ref), channel_id=1, source_target_pairs={{143,80},{144,79},{159,96},{160,95},{175,112},{176,111},{79,15},{8... | collective-permute-start | bytes 393224 | tf_op jit(solution)/shard_map/ppermute | solution.py:91
  40.6 2.5 %collective-permute-start.17 = (bf16[2,64,512]{2,1,0:T(8,128)(2,1)S(1)}, bf16[2,64,512]{2,1,0:T(8,128)(2,1)S(1)}, u32[]{:S(2)}, u32[]{:S(2)}) collective-permute-start(bf16[2,64,512]{2,1,0:T(8,128)(2,1)S(1)} %collective-permute-done.16.refs_2_), channel_id=1, source_target_pairs={{0,64},{1,66},{2,65},{3,68},{4,67},{5,70},{6,69},{7,72},{8,71},{9,... | collective-permute-start | bytes 393224 | tf_op jit(solution)/shard_map/ppermute | solution.py:91
  43.1 0.0 collective-permute-start.18
  43.1 0.5 collective-permute-start.19
  43.6 0.1 shard_map.59.refs_3_.refs_5_
  43.7 2.5 %collective-permute-start.25 = (bf16[2,64,512]{2,1,0:T(8,128)(2,1)S(1)}, bf16[2,64,512]{2,1,0:T(8,128)(2,1)S(1)}, u32[]{:S(2)}, u32[]{:S(2)}) collective-permute-start(bf16[2,64,512]{2,1,0:T(8,128)(2,1)S(1)} %shard_map.60.refs_4_), channel_id=1, source_target_pairs={{79,16},{80,15},{95,32},{96,31},{111,48},{112,47},{15,79},{16,80},... | collective-permute-start | bytes 393224 | tf_op jit(solution)/shard_map/ppermute | solution.py:91
  46.3 0.5 collective-permute-start.22
  46.8 0.1 collective-permute-start.23
  46.9 0.1 collective-permute-start.24
  47.0 0.7 %select_select_fusion = (bf16[2,64,512]{2,1,0:T(8,128)(2,1)S(1)}, bf16[1,2,64,512]{3,2,1,0:T(8,128)(2,1)}) fusion(bf16[2,64,512]{2,1,0:T(8,128)(2,1)S(1)} %shard_map.61, bf16[2,64,512]{2,1,0:T(8,128)(2,1)S(1)} %shard_map.58.after_ref, bf16[2,64,512]{2,1,0:T(8,128)(2,1)S(1)} %shard_map.56.after_ref, pred[]{:T(512)S(6)} %eq.13, pred[]{:T(512)S(6)} %eq.12, ...), kind=kLoop, calls=%fused_computation | loop fusion | flops 327680 | bytes 1048579 | tf_op jit(solution)/shard_map/jit(_where)/select_n | solution.py:255
  47.7 1.9 %shard_map.62.refs_3_ = bf16[3,2,512,512]{3,2,1,0:T(8,128)(2,1)S(1)} custom-call(bf16[3,2,512,512]{3,2,1,0:T(8,128)(2,1)} %bitcast.21, bf16[2,64,512]{2,1,0:T(8,128)(2,1)S(1)} %get-tuple-element.2.after_ref.refs_6_), custom_call_target="tpu_custom_call" | custom-call | bytes 6291456 | tf_op jit(solution)/shard_map/pallas_call | solution.py:112
  49.6 3.5 %collective-permute-done.25.refs_4_ = bf16[2,64,512]{2,1,0:T(8,128)(2,1)S(1)} collective-permute-done((bf16[2,64,512]{2,1,0:T(8,128)(2,1)S(1)}, bf16[2,64,512]{2,1,0:T(8,128)(2,1)S(1)}, u32[]{:S(2)}, u32[]{:S(2)}) %collective-permute-start.25) | collective-permute-done | bytes 131104 | tf_op jit(solution)/shard_map/ppermute | solution.py:91
  53.0 1.3 %shard_map.63 = bf16[2,64,512]{2,1,0:T(8,128)(2,1)} custom-call(bf16[2,64,512]{2,1,0:T(8,128)(2,1)S(1)} %collective-permute-done.22.refs_0_, bf16[2,64,512]{2,1,0:T(8,128)(2,1)S(1)} %collective-permute-done.23.refs_1_, bf16[2,64,512]{2,1,0:T(8,128)(2,1)S(1)} %collective-permute-done.24.refs_2_, bf16[3,2,512,512]{3,2,1,0:T(8,128)(2,1)S(1)} %shard_map.62.refs_3_, ...), custom_call_target="tpu_custom_call" | custom-call | flops 402653184 | bytes 3801088 | tf_op jit(solution)/shard_map/pallas_call | solution.py:202
  (23 shorter events, 0.1 us)
Async XLA Ops:
  0.6 9.7 %collective-permute-start = (bf16[2,64,512]{2,1,0:T(8,128)(2,1)}, bf16[2,64,512]{2,1,0:T(8,128)(2,1)S(1)}, u32[]{:S(2)}, u32[]{:S(2)}) collective-permute-start(bf16[2,64,512]{2,1,0:T(8,128)(2,1)} %bitcast.7), channel_id=1, source_target_pairs={{0,64},{1,66},{2,65},{3,68},{4,67},{5,70},{6,69},{7,72},{8,71},{9,... | collective-permute-start | bytes 393224 | tf_op jit(solution)/shard_map/ppermute | solution.py:91
  7.5 2.9 %collective-permute-start.1 = (bf16[2,64,512]{2,1,0:T(8,128)(2,1)}, bf16[2,64,512]{2,1,0:T(8,128)(2,1)S(1)}, u32[]{:S(2)}, u32[]{:S(2)}) collective-permute-start(bf16[2,64,512]{2,1,0:T(8,128)(2,1)} %bitcast.8), channel_id=1, source_target_pairs={{0,65},{1,64},{2,67},{3,66},{4,69},{5,68},{6,71},{7,70},{8,73},{9,... | collective-permute-start | bytes 393224 | tf_op jit(solution)/shard_map/ppermute | solution.py:91
  7.5 2.9 %collective-permute-start.2 = (bf16[2,64,512]{2,1,0:T(8,128)(2,1)}, bf16[2,64,512]{2,1,0:T(8,128)(2,1)S(1)}, u32[]{:S(2)}, u32[]{:S(2)}) collective-permute-start(bf16[2,64,512]{2,1,0:T(8,128)(2,1)} %bitcast.9), channel_id=1, source_target_pairs={{0,64},{1,65},{2,66},{3,67},{4,68},{5,69},{6,70},{7,71},{8,72},{9,... | collective-permute-start | bytes 393224 | tf_op jit(solution)/shard_map/ppermute | solution.py:91
  8.0 0.9 %copy-start = (bf16[1,2,64,512]{3,2,1,0:T(8,128)(2,1)S(1)}, bf16[1,2,64,512]{3,2,1,0:T(8,128)(2,1)}, u32[]{:S(2)}) copy-start(bf16[1,2,64,512]{3,2,1,0:T(8,128)(2,1)} %param.3) | copy-start | bytes 393220
  10.4 12.7 %copy-start.1 = (bf16[1,2,64,512]{3,2,1,0:T(8,128)(2,1)S(1)}, bf16[1,2,64,512]{3,2,1,0:T(8,128)(2,1)}, u32[]{:S(2)}) copy-start(bf16[1,2,64,512]{3,2,1,0:T(8,128)(2,1)} %param.3) | copy-start | bytes 393220
  10.4 6.2 %collective-permute-start.3 = (bf16[2,64,512]{2,1,0:T(8,128)(2,1)S(1)}, bf16[2,64,512]{2,1,0:T(8,128)(2,1)S(1)}, u32[]{:S(2)}, u32[]{:S(2)}) collective-permute-start(bf16[2,64,512]{2,1,0:T(8,128)(2,1)S(1)} %shard_map.51.after_ref.refs_4_.refs_6_), channel_id=1, source_target_pairs={{79,143},{80,144},{95,159},{96,160},{111,175},{112,176},{143,207},... | collective-permute-start | bytes 393224 | tf_op jit(solution)/shard_map/ppermute | solution.py:91
  11.7 8.6 %collective-permute-start.7 = (bf16[2,64,512]{2,1,0:T(8,128)(2,1)S(1)}, bf16[2,64,512]{2,1,0:T(8,128)(2,1)S(1)}, u32[]{:S(2)}, u32[]{:S(2)}) collective-permute-start(bf16[2,64,512]{2,1,0:T(8,128)(2,1)S(1)} %shard_map.51.after_ref.refs_4_.refs_6_), channel_id=1, source_target_pairs={{78,143},{79,142},{80,145},{81,144},{94,159},{95,158},{96,161},{97... | collective-permute-start | bytes 393224 | tf_op jit(solution)/shard_map/ppermute | solution.py:91
  11.8 11.3 %collective-permute-start.8 = (bf16[2,64,512]{2,1,0:T(8,128)(2,1)S(1)}, bf16[2,64,512]{2,1,0:T(8,128)(2,1)S(1)}, u32[]{:S(2)}, u32[]{:S(2)}) collective-permute-start(bf16[2,64,512]{2,1,0:T(8,128)(2,1)S(1)} %shard_map.51.after_ref.refs_4_.refs_6_), channel_id=1, source_target_pairs={{79,144},{80,143},{95,160},{96,159},{111,176},{112,175},{143,207},... | collective-permute-start | bytes 393224 | tf_op jit(solution)/shard_map/ppermute | solution.py:91
  16.6 6.5 %collective-permute-start.4 = (bf16[2,64,512]{2,1,0:T(8,128)(2,1)S(1)}, bf16[2,64,512]{2,1,0:T(8,128)(2,1)S(1)}, u32[]{:S(2)}, u32[]{:S(2)}) collective-permute-start(bf16[2,64,512]{2,1,0:T(8,128)(2,1)S(1)} %collective-permute-done.3.refs_2_), channel_id=1, source_target_pairs={{192,128},{193,130},{194,129},{195,132},{196,131},{197,134},{198,1... | collective-permute-start | bytes 393224 | tf_op jit(solution)/shard_map/ppermute | solution.py:91
  16.6 6.5 %collective-permute-start.5 = (bf16[2,64,512]{2,1,0:T(8,128)(2,1)S(1)}, bf16[2,64,512]{2,1,0:T(8,128)(2,1)S(1)}, u32[]{:S(2)}, u32[]{:S(2)}) collective-permute-start(bf16[2,64,512]{2,1,0:T(8,128)(2,1)S(1)} %collective-permute-done.3.refs_2_), channel_id=1, source_target_pairs={{192,129},{193,128},{194,131},{195,130},{196,133},{197,132},{198,1... | collective-permute-start | bytes 393224 | tf_op jit(solution)/shard_map/ppermute | solution.py:91
  17.1 6.0 %collective-permute-start.6 = (bf16[2,64,512]{2,1,0:T(8,128)(2,1)S(1)}, bf16[2,64,512]{2,1,0:T(8,128)(2,1)S(1)}, u32[]{:S(2)}, u32[]{:S(2)}) collective-permute-start(bf16[2,64,512]{2,1,0:T(8,128)(2,1)S(1)} %collective-permute-done.3.refs_2_), channel_id=1, source_target_pairs={{192,128},{193,129},{194,130},{195,131},{196,132},{197,133},{198,1... | collective-permute-start | bytes 393224 | tf_op jit(solution)/shard_map/ppermute | solution.py:91
  23.1 1.3 %collective-permute-start.12 = (bf16[2,64,512]{2,1,0:T(8,128)(2,1)S(1)}, bf16[2,64,512]{2,1,0:T(8,128)(2,1)S(1)}, u32[]{:S(2)}, u32[]{:S(2)}) collective-permute-start(bf16[2,64,512]{2,1,0:T(8,128)(2,1)S(1)} %shard_map.53.refs_4_), channel_id=1, source_target_pairs={{143,208},{144,207},{159,224},{160,223},{175,240},{176,239},{207,1... | collective-permute-start | bytes 393224 | tf_op jit(solution)/shard_map/ppermute | solution.py:91
  23.2 1.6 %collective-permute-start.10 = (bf16[2,64,512]{2,1,0:T(8,128)(2,1)S(1)}, bf16[2,64,512]{2,1,0:T(8,128)(2,1)S(1)}, u32[]{:S(2)}, u32[]{:S(2)}) collective-permute-start(bf16[2,64,512]{2,1,0:T(8,128)(2,1)S(1)} %shard_map.54.after_ref.refs_4_), channel_id=1, source_target_pairs={{128,192},{129,194},{130,193},{131,196},{132,195},{133,198},{134,1... | collective-permute-start | bytes 393224 | tf_op jit(solution)/shard_map/ppermute | solution.py:91
  23.8 1.3 %collective-permute-start.11 = (bf16[2,64,512]{2,1,0:T(8,128)(2,1)S(1)}, bf16[2,64,512]{2,1,0:T(8,128)(2,1)S(1)}, u32[]{:S(2)}, u32[]{:S(2)}) collective-permute-start(bf16[2,64,512]{2,1,0:T(8,128)(2,1)S(1)} %shard_map.54.after_ref.refs_4_), channel_id=1, source_target_pairs={{128,193},{129,192},{130,195},{131,194},{132,197},{133,196},{134,1... | collective-permute-start | bytes 393224 | tf_op jit(solution)/shard_map/ppermute | solution.py:91
  23.9 1.4 %collective-permute-start.9 = (bf16[2,64,512]{2,1,0:T(8,128)(2,1)S(1)}, bf16[2,64,512]{2,1,0:T(8,128)(2,1)S(1)}, u32[]{:S(2)}, u32[]{:S(2)}) collective-permute-start(bf16[2,64,512]{2,1,0:T(8,128)(2,1)S(1)} %shard_map.54.after_ref.refs_4_), channel_id=1, source_target_pairs={{128,192},{129,193},{130,194},{131,195},{132,196},{133,197},{134,1... | collective-permute-start | bytes 393224 | tf_op jit(solution)/shard_map/ppermute | solution.py:91
  25.3 1.3 %collective-permute-start.13 = (bf16[2,64,512]{2,1,0:T(8,128)(2,1)S(1)}, bf16[2,64,512]{2,1,0:T(8,128)(2,1)S(1)}, u32[]{:S(2)}, u32[]{:S(2)}) collective-permute-start(bf16[2,64,512]{2,1,0:T(8,128)(2,1)S(1)} %shard_map.56.after_ref), channel_id=1, source_target_pairs={{192,128},{193,130},{194,129},{195,132},{196,131},{197,134},{198,1... | collective-permute-start | bytes 393224 | tf_op jit(solution)/shard_map/ppermute | solution.py:91
  25.6 1.3 %collective-permute-start.14 = (bf16[2,64,512]{2,1,0:T(8,128)(2,1)S(1)}, bf16[2,64,512]{2,1,0:T(8,128)(2,1)S(1)}, u32[]{:S(2)}, u32[]{:S(2)}) collective-permute-start(bf16[2,64,512]{2,1,0:T(8,128)(2,1)S(1)} %shard_map.56.after_ref), channel_id=1, source_target_pairs={{192,129},{193,128},{194,131},{195,130},{196,133},{197,132},{198,1... | collective-permute-start | bytes 393224 | tf_op jit(solution)/shard_map/ppermute | solution.py:91
  25.8 1.3 %collective-permute-start.15 = (bf16[2,64,512]{2,1,0:T(8,128)(2,1)S(1)}, bf16[2,64,512]{2,1,0:T(8,128)(2,1)S(1)}, u32[]{:S(2)}, u32[]{:S(2)}) collective-permute-start(bf16[2,64,512]{2,1,0:T(8,128)(2,1)S(1)} %shard_map.56.after_ref), channel_id=1, source_target_pairs={{192,128},{193,129},{194,130},{195,131},{196,132},{197,133},{198,1... | collective-permute-start | bytes 393224 | tf_op jit(solution)/shard_map/ppermute | solution.py:91
  27.2 13.4 %collective-permute-start.16 = (bf16[2,64,512]{2,1,0:T(8,128)(2,1)S(1)}, bf16[2,64,512]{2,1,0:T(8,128)(2,1)S(1)}, u32[]{:S(2)}, u32[]{:S(2)}) collective-permute-start(bf16[2,64,512]{2,1,0:T(8,128)(2,1)S(1)} %shard_map.58.after_ref), channel_id=1, source_target_pairs={{143,79},{144,80},{159,95},{160,96},{175,111},{176,112},{79,15},{8... | collective-permute-start | bytes 393224 | tf_op jit(solution)/shard_map/ppermute | solution.py:91
  31.8 11.8 %collective-permute-start.20 = (bf16[2,64,512]{2,1,0:T(8,128)(2,1)S(1)}, bf16[2,64,512]{2,1,0:T(8,128)(2,1)S(1)}, u32[]{:S(2)}, u32[]{:S(2)}) collective-permute-start(bf16[2,64,512]{2,1,0:T(8,128)(2,1)S(1)} %shard_map.58.after_ref), channel_id=1, source_target_pairs={{142,79},{143,78},{144,81},{145,80},{158,95},{159,94},{160,97},{16... | collective-permute-start | bytes 393224 | tf_op jit(solution)/shard_map/ppermute | solution.py:91
  39.5 4.2 %collective-permute-start.21 = (bf16[2,64,512]{2,1,0:T(8,128)(2,1)S(1)}, bf16[2,64,512]{2,1,0:T(8,128)(2,1)S(1)}, u32[]{:S(2)}, u32[]{:S(2)}) collective-permute-start(bf16[2,64,512]{2,1,0:T(8,128)(2,1)S(1)} %shard_map.58.after_ref), channel_id=1, source_target_pairs={{143,80},{144,79},{159,96},{160,95},{175,112},{176,111},{79,15},{8... | collective-permute-start | bytes 393224 | tf_op jit(solution)/shard_map/ppermute | solution.py:91
  40.6 5.7 %collective-permute-start.17 = (bf16[2,64,512]{2,1,0:T(8,128)(2,1)S(1)}, bf16[2,64,512]{2,1,0:T(8,128)(2,1)S(1)}, u32[]{:S(2)}, u32[]{:S(2)}) collective-permute-start(bf16[2,64,512]{2,1,0:T(8,128)(2,1)S(1)} %collective-permute-done.16.refs_2_), channel_id=1, source_target_pairs={{0,64},{1,66},{2,65},{3,68},{4,67},{5,70},{6,69},{7,72},{8,71},{9,... | collective-permute-start | bytes 393224 | tf_op jit(solution)/shard_map/ppermute | solution.py:91
  43.1 3.1 %collective-permute-start.18 = (bf16[2,64,512]{2,1,0:T(8,128)(2,1)S(1)}, bf16[2,64,512]{2,1,0:T(8,128)(2,1)S(1)}, u32[]{:S(2)}, u32[]{:S(2)}) collective-permute-start(bf16[2,64,512]{2,1,0:T(8,128)(2,1)S(1)} %collective-permute-done.16.refs_2_), channel_id=1, source_target_pairs={{0,65},{1,64},{2,67},{3,66},{4,69},{5,68},{6,71},{7,70},{8,73},{9,... | collective-permute-start | bytes 393224 | tf_op jit(solution)/shard_map/ppermute | solution.py:91
  43.1 3.1 %collective-permute-start.19 = (bf16[2,64,512]{2,1,0:T(8,128)(2,1)S(1)}, bf16[2,64,512]{2,1,0:T(8,128)(2,1)S(1)}, u32[]{:S(2)}, u32[]{:S(2)}) collective-permute-start(bf16[2,64,512]{2,1,0:T(8,128)(2,1)S(1)} %collective-permute-done.16.refs_2_), channel_id=1, source_target_pairs={{0,64},{1,65},{2,66},{3,67},{4,68},{5,69},{6,70},{7,71},{8,72},{9,... | collective-permute-start | bytes 393224 | tf_op jit(solution)/shard_map/ppermute | solution.py:91
  43.7 9.3 %collective-permute-start.25 = (bf16[2,64,512]{2,1,0:T(8,128)(2,1)S(1)}, bf16[2,64,512]{2,1,0:T(8,128)(2,1)S(1)}, u32[]{:S(2)}, u32[]{:S(2)}) collective-permute-start(bf16[2,64,512]{2,1,0:T(8,128)(2,1)S(1)} %shard_map.60.refs_4_), channel_id=1, source_target_pairs={{79,16},{80,15},{95,32},{96,31},{111,48},{112,47},{15,79},{16,80},... | collective-permute-start | bytes 393224 | tf_op jit(solution)/shard_map/ppermute | solution.py:91
  46.3 6.8 %collective-permute-start.22 = (bf16[2,64,512]{2,1,0:T(8,128)(2,1)S(1)}, bf16[2,64,512]{2,1,0:T(8,128)(2,1)S(1)}, u32[]{:S(2)}, u32[]{:S(2)}) collective-permute-start(bf16[2,64,512]{2,1,0:T(8,128)(2,1)S(1)} %shard_map.61), channel_id=1, source_target_pairs={{64,0},{65,2},{66,1},{67,4},{68,3},{69,6},{70,5},{71,8},{72,7},{73... | collective-permute-start | bytes 393224 | tf_op jit(solution)/shard_map/ppermute | solution.py:91
  46.8 6.2 %collective-permute-start.23 = (bf16[2,64,512]{2,1,0:T(8,128)(2,1)S(1)}, bf16[2,64,512]{2,1,0:T(8,128)(2,1)S(1)}, u32[]{:S(2)}, u32[]{:S(2)}) collective-permute-start(bf16[2,64,512]{2,1,0:T(8,128)(2,1)S(1)} %shard_map.61), channel_id=1, source_target_pairs={{64,1},{65,0},{66,3},{67,2},{68,5},{69,4},{70,7},{71,6},{72,9},{73... | collective-permute-start | bytes 393224 | tf_op jit(solution)/shard_map/ppermute | solution.py:91
  46.9 6.2 %collective-permute-start.24 = (bf16[2,64,512]{2,1,0:T(8,128)(2,1)S(1)}, bf16[2,64,512]{2,1,0:T(8,128)(2,1)S(1)}, u32[]{:S(2)}, u32[]{:S(2)}) collective-permute-start(bf16[2,64,512]{2,1,0:T(8,128)(2,1)S(1)} %shard_map.61), channel_id=1, source_target_pairs={{64,0},{65,1},{66,2},{67,3},{68,4},{69,5},{70,6},{71,7},{72,8},{73... | collective-permute-start | bytes 393224 | tf_op jit(solution)/shard_map/ppermute | solution.py:91

commit v7 on v6

--- a/solution.py
+++ b/solution.py
@@ -196,6 +196,68 @@
     out_ref[1] = imag
 
 
+def first_kernel(layer, names, *refs):
+    *refs, sum_ref = refs
+    refs = dict(zip(names, refs))
+
+    @pl.when(lax.axis_index("layer") == layer)
+    def _():
+        rows = refs["own"].shape[1]
+        near_number = 2 - lax.rem(lax.axis_index("tile"), 2)
+        by_real = jnp.zeros(sum_ref.shape[1:], jnp.float32)
+        by_imag = by_real
+        for name, number in (("own", 0), ("near", near_number)):
+            values = refs[name][...].reshape(2 * rows, -1)
+            by_real += jnp.dot(values, refs["blocks"][number, 0], preferred_element_type=jnp.float32)
+            by_imag += jnp.dot(values, refs["blocks"][number, 1], preferred_element_type=jnp.float32)
+        sum_ref[0] = by_real
+        sum_ref[1] = by_imag
+
+
+def last_kernel(layer, names, *refs):
+    *refs, out_ref = refs
+    refs = dict(zip(names, refs))
+    here = lax.axis_index("layer") == layer
+
+    @pl.when(jnp.logical_not(here))
+    def _():
+        out_ref[...] = refs["kept"][...]
+
+    @pl.when(here)
+    def _():
+        tile = lax.axis_index("tile")
+        rows, cells = refs["far"].shape[1:]
+        edge = jnp.logical_or(tile == 0, tile == lax.axis_size("tile") - 1)
+        far = jnp.where(seam_here(0), refs["passed"][...], refs["far"][...]).reshape(2 * rows, cells)
+        far = jnp.where(edge, jnp.zeros_like(far), far)
+        number = 1 + lax.rem(tile, 2)
+        by_real = refs["sums"][0] + jnp.dot(far, refs["blocks"][number, 0], preferred_element_type=jnp.float32)
+        by_imag = refs["sums"][1] + jnp.dot(far, refs["blocks"][number, 1], preferred_element_type=jnp.float32)
+        addend_ref = refs["addend"]
+        out_ref[0] = (by_real[:rows] - by_imag[rows:] + addend_ref[0].astype(jnp.float32)).astype(out_ref.dtype)
+        out_ref[1] = (by_imag[:rows] + by_real[rows:] + addend_ref[1].astype(jnp.float32)).astype(out_ref.dtype)
+
+
+def call(kernel, layer, shape, dtype, flops, **operands):
+    vmem = pl.BlockSpec(memory_space=pltpu.VMEM)
+    return pl.pallas_call(
+        functools.partial(kernel, layer, tuple(operands)),
+        out_shape=jax.ShapeDtypeStruct(shape, dtype),
+        in_specs=[vmem] * len(operands),
+        out_specs=vmem,
+        compiler_params=pltpu.CompilerParams(vmem_limit_bytes=VMEM_LIMIT),
+        cost_estimate=pl.CostEstimate(flops=flops, bytes_accessed=operands["blocks"].size, transcendentals=0),
+    )(*operands.values())
+
+
+def last_hop(values, source, target, held, order, passed, addend, kept):
+    arrived = spread(values, source, target, order, far=inner_mate)
+    parts, rows, cells = addend.shape
+    flops = 8 * rows * cells * cells
+    sums = call(first_kernel, target, (2, parts * rows, cells), jnp.float32, 2 * flops, near=arrived["near"], own=arrived["own"], blocks=held)
+    return call(last_kernel, target, addend.shape, addend.dtype, flops, far=arrived["far"], passed=passed, sums=sums, blocks=held, addend=addend, kept=kept)
+
+
 def step(layer, kernel=step_kernel, **operands):
     vmem = pl.BlockSpec(memory_space=pltpu.VMEM)
     addend = operands["addend"]
@@ -253,7 +315,7 @@
     up_2 = hop(down_3, 3, 2, up, ORDERS[3], addend=down_2)
     up_1, passed = crossing_hop(up_2, 2, 1, up, ORDERS[4], addend=down_1)
     rising = jnp.where(layer == 1, up_1, jnp.where(layer == 2, up_2, down_3))
-    rising = hop(up_1, 1, 0, up, ORDERS[5], rising, passed, addend=source, kept=rising)
+    rising = last_hop(up_1, 1, 0, load(up, rising, 0), ORDERS[5], passed, source, rising)
     return (falling[None], rising[None])
 
 

time: 54.4 us -> 54.1 us (level)
  waiting for transfers between devices: 16.3 us -> 15.5 us
    pallas_call x0 -> x2, Pallas kernels: none -> 1.42 us  [call(): pl.pallas_call(functools.partial(kernel, layer, tuple(operands)), out_sha...]
    pallas_call x8 -> x7, Pallas kernels: 1.34 us -> 0.08 us  [step(): pl.pallas_call(functools.partial(kernel, layer, tuple(operands)), out_sha...]
    ppermute x26, waiting for transfers between devices: 16.3 us -> 15.5 us  [permute(): return lax.ppermute(values, AXES, pairs)]
  transfers between devices with their start and end apart: 26 -> 26, of which waited for: 12 -> 13; matrix products, arithmetic and copies ran while one was open for 1% -> 1% of each run, Pallas kernels for 4% -> 5%
where the time goes in v7:
time: 54.1 us; the launch traced here: 54 us
  starting transfers between devices  32.5 us (60%)
  waiting for transfers between devices  15.5 us (29%)
  Pallas kernels  3.65 us (7%)
  local copies, waits for them, and re-layouts  0.91 us (2%)
  between operations  0.78 us (1%)
  other arithmetic  0.69 us (1%)
    ppermute x26, starting transfers between devices, permute(): return lax.ppermute(values, AXES, pairs)  32.5 us
    ppermute x26, waiting for transfers between devices, permute(): return lax.ppermute(values, AXES, pairs)  15.5 us
    pallas_call x6, Pallas kernels, load(): pl.pallas_call(functools.partial(load_kernel, layers), out_shape=pltpu.VM...  2.15 us
    pallas_call x2, Pallas kernels, call(): pl.pallas_call(functools.partial(kernel, layer, tuple(operands)), out_sha...  1.42 us
  transfers between devices with their start and end apart: 26, of which 13 were waited for; matrix products, arithmetic and copies ran while one was open for 1% of the time, Pallas kernels for 5%

profile of v7, /device:TPU:6, one launch (start us, length us, event | category | flops | bytes accessed | tf_op | source)
XLA Modules:
  0.0 54.0 jit_solution(2275211076479782987)
XLA Ops:
  0.6 6.9 %collective-permute-start = (bf16[2,64,512]{2,1,0:T(8,128)(2,1)}, bf16[2,64,512]{2,1,0:T(8,128)(2,1)S(1)}, u32[]{:S(2)}, u32[]{:S(2)}) collective-permute-start(bf16[2,64,512]{2,1,0:T(8,128)(2,1)} %bitcast.7), channel_id=1, source_target_pairs={{0,64},{1,66},{2,65},{3,68},{4,67},{5,70},{6,69},{7,72},{8,71},{9,... | collective-permute-start | bytes 393224 | tf_op jit(solution)/shard_map/ppermute | solution.py:91
  7.5 0.5 collective-permute-start.2
  8.0 0.9 %copy-done = bf16[1,2,64,512]{3,2,1,0:T(8,128)(2,1)S(1)} copy-done((bf16[1,2,64,512]{3,2,1,0:T(8,128)(2,1)S(1)}, bf16[1,2,64,512]{3,2,1,0:T(8,128)(2,1)}, u32[]{:S(2)}) %copy-start) | copy-done | bytes 131096
  8.9 0.1 shard_map.50.refs_3_
  9.0 1.4 %collective-permute-done.refs_0_ = bf16[2,64,512]{2,1,0:T(8,128)(2,1)S(1)} collective-permute-done((bf16[2,64,512]{2,1,0:T(8,128)(2,1)}, bf16[2,64,512]{2,1,0:T(8,128)(2,1)S(1)}, u32[]{:S(2)}, u32[]{:S(2)}) %collective-permute-start) | collective-permute-done | bytes 131104 | tf_op jit(solution)/shard_map/ppermute | solution.py:91
  10.3 0.0 collective-permute-done.1.refs_1_
  10.4 1.4 %collective-permute-start.3 = (bf16[2,64,512]{2,1,0:T(8,128)(2,1)S(1)}, bf16[2,64,512]{2,1,0:T(8,128)(2,1)S(1)}, u32[]{:S(2)}, u32[]{:S(2)}) collective-permute-start(bf16[2,64,512]{2,1,0:T(8,128)(2,1)S(1)} %shard_map.51.after_ref.refs_4_.refs_6_), channel_id=1, source_target_pairs={{79,143},{80,144},{95,159},{96,160},{111,175},{112,176},{143,207},... | collective-permute-start | bytes 393224 | tf_op jit(solution)/shard_map/ppermute | solution.py:91
  11.7 0.1 collective-permute-start.7
  11.8 1.2 %collective-permute-start.8 = (bf16[2,64,512]{2,1,0:T(8,128)(2,1)S(1)}, bf16[2,64,512]{2,1,0:T(8,128)(2,1)S(1)}, u32[]{:S(2)}, u32[]{:S(2)}) collective-permute-start(bf16[2,64,512]{2,1,0:T(8,128)(2,1)S(1)} %shard_map.51.after_ref.refs_4_.refs_6_), channel_id=1, source_target_pairs={{79,144},{80,143},{95,160},{96,159},{111,176},{112,175},{143,207},... | collective-permute-start | bytes 393224 | tf_op jit(solution)/shard_map/ppermute | solution.py:91
  13.1 3.5 %collective-permute-done.3.refs_2_ = bf16[2,64,512]{2,1,0:T(8,128)(2,1)S(1)} collective-permute-done((bf16[2,64,512]{2,1,0:T(8,128)(2,1)S(1)}, bf16[2,64,512]{2,1,0:T(8,128)(2,1)S(1)}, u32[]{:S(2)}, u32[]{:S(2)}) %collective-permute-start.3) | collective-permute-done | bytes 131104 | tf_op jit(solution)/shard_map/ppermute | solution.py:91
  16.6 0.0 collective-permute-start.4
  16.6 0.5 collective-permute-start.5
  17.1 0.0 collective-permute-start.6
  17.1 0.1 shard_map.52.refs_3_.refs_5_
  17.2 3.2 %collective-permute-done.7.refs_1_.refs_3_ = bf16[2,64,512]{2,1,0:T(8,128)(2,1)S(1)} collective-permute-done((bf16[2,64,512]{2,1,0:T(8,128)(2,1)S(1)}, bf16[2,64,512]{2,1,0:T(8,128)(2,1)S(1)}, u32[]{:S(2)}, u32[]{:S(2)}) %collective-permute-start.7) | collective-permute-done | bytes 131104 | tf_op jit(solution)/shard_map/ppermute | solution.py:91
  20.3 2.8 %collective-permute-done.8.refs_0_ = bf16[2,64,512]{2,1,0:T(8,128)(2,1)S(1)} collective-permute-done((bf16[2,64,512]{2,1,0:T(8,128)(2,1)S(1)}, bf16[2,64,512]{2,1,0:T(8,128)(2,1)S(1)}, u32[]{:S(2)}, u32[]{:S(2)}) %collective-permute-start.8) | collective-permute-done | bytes 131104 | tf_op jit(solution)/shard_map/ppermute | solution.py:91
  23.2 0.6 %collective-permute-start.10 = (bf16[2,64,512]{2,1,0:T(8,128)(2,1)S(1)}, bf16[2,64,512]{2,1,0:T(8,128)(2,1)S(1)}, u32[]{:S(2)}, u32[]{:S(2)}) collective-permute-start(bf16[2,64,512]{2,1,0:T(8,128)(2,1)S(1)} %shard_map.54.after_ref.refs_4_), channel_id=1, source_target_pairs={{128,192},{129,194},{130,193},{131,196},{132,195},{133,198},{134,1... | collective-permute-start | bytes 393224 | tf_op jit(solution)/shard_map/ppermute | solution.py:91
  23.8 0.1 collective-permute-start.11
  23.9 0.4 collective-permute-start.9
  24.3 0.1 shard_map.55.refs_3_
  24.3 0.1 collective-permute-done.12.refs_4_
  24.5 0.3 collective-permute-done.10.refs_1_
  24.7 0.4 collective-permute-done.11.refs_2_
  25.1 0.2 collective-permute-done.9.refs_0_
  25.3 0.3 collective-permute-start.13
  25.6 0.2 collective-permute-start.14
  25.8 0.3 collective-permute-start.15
  26.1 0.1 shard_map.57.refs_3_
  26.2 0.5 collective-permute-done.13.refs_0_
  26.6 0.3 collective-permute-done.14.refs_1_
  27.0 0.2 collective-permute-done.15.refs_2_
  27.2 4.7 %collective-permute-start.16 = (bf16[2,64,512]{2,1,0:T(8,128)(2,1)S(1)}, bf16[2,64,512]{2,1,0:T(8,128)(2,1)S(1)}, u32[]{:S(2)}, u32[]{:S(2)}) collective-permute-start(bf16[2,64,512]{2,1,0:T(8,128)(2,1)S(1)} %shard_map.58.after_ref), channel_id=1, source_target_pairs={{143,79},{144,80},{159,95},{160,96},{175,111},{176,112},{79,15},{8... | collective-permute-start | bytes 393224 | tf_op jit(solution)/shard_map/ppermute | solution.py:91
  31.8 7.6 %collective-permute-start.20 = (bf16[2,64,512]{2,1,0:T(8,128)(2,1)S(1)}, bf16[2,64,512]{2,1,0:T(8,128)(2,1)S(1)}, u32[]{:S(2)}, u32[]{:S(2)}) collective-permute-start(bf16[2,64,512]{2,1,0:T(8,128)(2,1)S(1)} %shard_map.58.after_ref), channel_id=1, source_target_pairs={{142,79},{143,78},{144,81},{145,80},{158,95},{159,94},{160,97},{16... | collective-permute-start | bytes 393224 | tf_op jit(solution)/shard_map/ppermute | solution.py:91
  39.5 1.1 %collective-permute-start.21 = (bf16[2,64,512]{2,1,0:T(8,128)(2,1)S(1)}, bf16[2,64,512]{2,1,0:T(8,128)(2,1)S(1)}, u32[]{:S(2)}, u32[]{:S(2)}) collective-permute-start(bf16[2,64,512]{2,1,0:T(8,128)(2,1)S(1)} %shard_map.58.after_ref), channel_id=1, source_target_pairs={{143,80},{144,79},{159,96},{160,95},{175,112},{176,111},{79,15},{8... | collective-permute-start | bytes 393224 | tf_op jit(solution)/shard_map/ppermute | solution.py:91
  40.6 2.5 %collective-permute-start.17 = (bf16[2,64,512]{2,1,0:T(8,128)(2,1)S(1)}, bf16[2,64,512]{2,1,0:T(8,128)(2,1)S(1)}, u32[]{:S(2)}, u32[]{:S(2)}) collective-permute-start(bf16[2,64,512]{2,1,0:T(8,128)(2,1)S(1)} %collective-permute-done.16.refs_2_), channel_id=1, source_target_pairs={{0,64},{1,66},{2,65},{3,68},{4,67},{5,70},{6,69},{7,72},{8,71},{9,... | collective-permute-start | bytes 393224 | tf_op jit(solution)/shard_map/ppermute | solution.py:91
  43.1 0.0 collective-permute-start.18
  43.1 0.5 collective-permute-start.19
  43.6 0.1 shard_map.59.refs_3_.refs_5_
  43.7 2.5 %collective-permute-start.23 = (bf16[2,64,512]{2,1,0:T(8,128)(2,1)S(1)}, bf16[2,64,512]{2,1,0:T(8,128)(2,1)S(1)}, u32[]{:S(2)}, u32[]{:S(2)}) collective-permute-start(bf16[2,64,512]{2,1,0:T(8,128)(2,1)S(1)} %shard_map.60.refs_4_), channel_id=1, source_target_pairs={{79,16},{80,15},{95,32},{96,31},{111,48},{112,47},{15,79},{16,80},... | collective-permute-start | bytes 393224 | tf_op jit(solution)/shard_map/ppermute | solution.py:91
  46.3 0.5 collective-permute-start.24
  46.8 0.1 collective-permute-start.25
  46.9 0.4 collective-permute-start.22
  47.3 0.7 %select_select_fusion = (bf16[2,64,512]{2,1,0:T(8,128)(2,1)S(1)}, bf16[1,2,64,512]{3,2,1,0:T(8,128)(2,1)}) fusion(bf16[2,64,512]{2,1,0:T(8,128)(2,1)S(1)} %shard_map.61, bf16[2,64,512]{2,1,0:T(8,128)(2,1)S(1)} %shard_map.58.after_ref, bf16[2,64,512]{2,1,0:T(8,128)(2,1)S(1)} %shard_map.56.after_ref, pred[]{:T(512)S(6)} %eq.13, pred[]{:T(512)S(6)} %eq.12, ...), kind=kLoop, calls=%fused_computation | loop fusion | flops 327680 | bytes 1048579 | tf_op jit(solution)/shard_map/jit(_where)/select_n | solution.py:317
  48.0 1.9 %shard_map.62.refs_2_.refs_3_ = bf16[3,2,512,512]{3,2,1,0:T(8,128)(2,1)S(1)} custom-call(bf16[3,2,512,512]{3,2,1,0:T(8,128)(2,1)} %bitcast.21, bf16[2,64,512]{2,1,0:T(8,128)(2,1)S(1)} %get-tuple-element.2.after_ref.refs_5_), custom_call_target="tpu_custom_call" | custom-call | bytes 6291456 | tf_op jit(solution)/shard_map/pallas_call | solution.py:112
  49.9 0.9 %collective-permute-done.24.refs_0_ = bf16[2,64,512]{2,1,0:T(8,128)(2,1)S(1)} collective-permute-done((bf16[2,64,512]{2,1,0:T(8,128)(2,1)S(1)}, bf16[2,64,512]{2,1,0:T(8,128)(2,1)S(1)}, u32[]{:S(2)}, u32[]{:S(2)}) %collective-permute-start.24) | collective-permute-done | bytes 131104 | tf_op jit(solution)/shard_map/ppermute | solution.py:91
  50.7 0.4 shard_map.63.refs_2_
  51.2 1.8 %collective-permute-done.23.refs_1_ = bf16[2,64,512]{2,1,0:T(8,128)(2,1)S(1)} collective-permute-done((bf16[2,64,512]{2,1,0:T(8,128)(2,1)S(1)}, bf16[2,64,512]{2,1,0:T(8,128)(2,1)S(1)}, u32[]{:S(2)}, u32[]{:S(2)}) %collective-permute-start.23) | collective-permute-done | bytes 131104 | tf_op jit(solution)/shard_map/ppermute | solution.py:91
  53.0 1.0 %shard_map.64 = bf16[2,64,512]{2,1,0:T(8,128)(2,1)} custom-call(bf16[2,64,512]{2,1,0:T(8,128)(2,1)S(1)} %collective-permute-done.22.refs_0_, bf16[2,64,512]{2,1,0:T(8,128)(2,1)S(1)} %collective-permute-done.23.refs_1_, f32[2,128,512]{2,1,0:T(8,128)S(1)} %shard_map.63.refs_2_, bf16[3,2,512,512]{3,2,1,0:T(8,128)(2,1)S(1)} %shard_map.62.refs_2_.refs_3_, ...), custom_call_target="tpu_custom_call" | custom-call | flops 134217728 | bytes 1572864 | tf_op jit(solution)/shard_map/pallas_call | solution.py:243
  (24 shorter events, 0.1 us)
Async XLA Ops:
  0.6 9.7 %collective-permute-start = (bf16[2,64,512]{2,1,0:T(8,128)(2,1)}, bf16[2,64,512]{2,1,0:T(8,128)(2,1)S(1)}, u32[]{:S(2)}, u32[]{:S(2)}) collective-permute-start(bf16[2,64,512]{2,1,0:T(8,128)(2,1)} %bitcast.7), channel_id=1, source_target_pairs={{0,64},{1,66},{2,65},{3,68},{4,67},{5,70},{6,69},{7,72},{8,71},{9,... | collective-permute-start | bytes 393224 | tf_op jit(solution)/shard_map/ppermute | solution.py:91
  7.5 2.9 %collective-permute-start.1 = (bf16[2,64,512]{2,1,0:T(8,128)(2,1)}, bf16[2,64,512]{2,1,0:T(8,128)(2,1)S(1)}, u32[]{:S(2)}, u32[]{:S(2)}) collective-permute-start(bf16[2,64,512]{2,1,0:T(8,128)(2,1)} %bitcast.8), channel_id=1, source_target_pairs={{0,65},{1,64},{2,67},{3,66},{4,69},{5,68},{6,71},{7,70},{8,73},{9,... | collective-permute-start | bytes 393224 | tf_op jit(solution)/shard_map/ppermute | solution.py:91
  7.5 2.9 %collective-permute-start.2 = (bf16[2,64,512]{2,1,0:T(8,128)(2,1)}, bf16[2,64,512]{2,1,0:T(8,128)(2,1)S(1)}, u32[]{:S(2)}, u32[]{:S(2)}) collective-permute-start(bf16[2,64,512]{2,1,0:T(8,128)(2,1)} %bitcast.9), channel_id=1, source_target_pairs={{0,64},{1,65},{2,66},{3,67},{4,68},{5,69},{6,70},{7,71},{8,72},{9,... | collective-permute-start | bytes 393224 | tf_op jit(solution)/shard_map/ppermute | solution.py:91
  8.0 0.9 %copy-start = (bf16[1,2,64,512]{3,2,1,0:T(8,128)(2,1)S(1)}, bf16[1,2,64,512]{3,2,1,0:T(8,128)(2,1)}, u32[]{:S(2)}) copy-start(bf16[1,2,64,512]{3,2,1,0:T(8,128)(2,1)} %param.3) | copy-start | bytes 393220
  10.4 12.7 %copy-start.1 = (bf16[1,2,64,512]{3,2,1,0:T(8,128)(2,1)S(1)}, bf16[1,2,64,512]{3,2,1,0:T(8,128)(2,1)}, u32[]{:S(2)}) copy-start(bf16[1,2,64,512]{3,2,1,0:T(8,128)(2,1)} %param.3) | copy-start | bytes 393220
  10.4 6.2 %collective-permute-start.3 = (bf16[2,64,512]{2,1,0:T(8,128)(2,1)S(1)}, bf16[2,64,512]{2,1,0:T(8,128)(2,1)S(1)}, u32[]{:S(2)}, u32[]{:S(2)}) collective-permute-start(bf16[2,64,512]{2,1,0:T(8,128)(2,1)S(1)} %shard_map.51.after_ref.refs_4_.refs_6_), channel_id=1, source_target_pairs={{79,143},{80,144},{95,159},{96,160},{111,175},{112,176},{143,207},... | collective-permute-start | bytes 393224 | tf_op jit(solution)/shard_map/ppermute | solution.py:91
  11.7 8.6 %collective-permute-start.7 = (bf16[2,64,512]{2,1,0:T(8,128)(2,1)S(1)}, bf16[2,64,512]{2,1,0:T(8,128)(2,1)S(1)}, u32[]{:S(2)}, u32[]{:S(2)}) collective-permute-start(bf16[2,64,512]{2,1,0:T(8,128)(2,1)S(1)} %shard_map.51.after_ref.refs_4_.refs_6_), channel_id=1, source_target_pairs={{78,143},{79,142},{80,145},{81,144},{94,159},{95,158},{96,161},{97... | collective-permute-start | bytes 393224 | tf_op jit(solution)/shard_map/ppermute | solution.py:91
  11.8 11.3 %collective-permute-start.8 = (bf16[2,64,512]{2,1,0:T(8,128)(2,1)S(1)}, bf16[2,64,512]{2,1,0:T(8,128)(2,1)S(1)}, u32[]{:S(2)}, u32[]{:S(2)}) collective-permute-start(bf16[2,64,512]{2,1,0:T(8,128)(2,1)S(1)} %shard_map.51.after_ref.refs_4_.refs_6_), channel_id=1, source_target_pairs={{79,144},{80,143},{95,160},{96,159},{111,176},{112,175},{143,207},... | collective-permute-start | bytes 393224 | tf_op jit(solution)/shard_map/ppermute | solution.py:91
  16.6 6.5 %collective-permute-start.4 = (bf16[2,64,512]{2,1,0:T(8,128)(2,1)S(1)}, bf16[2,64,512]{2,1,0:T(8,128)(2,1)S(1)}, u32[]{:S(2)}, u32[]{:S(2)}) collective-permute-start(bf16[2,64,512]{2,1,0:T(8,128)(2,1)S(1)} %collective-permute-done.3.refs_2_), channel_id=1, source_target_pairs={{192,128},{193,130},{194,129},{195,132},{196,131},{197,134},{198,1... | collective-permute-start | bytes 393224 | tf_op jit(solution)/shard_map/ppermute | solution.py:91
  16.6 6.5 %collective-permute-start.5 = (bf16[2,64,512]{2,1,0:T(8,128)(2,1)S(1)}, bf16[2,64,512]{2,1,0:T(8,128)(2,1)S(1)}, u32[]{:S(2)}, u32[]{:S(2)}) collective-permute-start(bf16[2,64,512]{2,1,0:T(8,128)(2,1)S(1)} %collective-permute-done.3.refs_2_), channel_id=1, source_target_pairs={{192,129},{193,128},{194,131},{195,130},{196,133},{197,132},{198,1... | collective-permute-start | bytes 393224 | tf_op jit(solution)/shard_map/ppermute | solution.py:91
  17.1 6.0 %collective-permute-start.6 = (bf16[2,64,512]{2,1,0:T(8,128)(2,1)S(1)}, bf16[2,64,512]{2,1,0:T(8,128)(2,1)S(1)}, u32[]{:S(2)}, u32[]{:S(2)}) collective-permute-start(bf16[2,64,512]{2,1,0:T(8,128)(2,1)S(1)} %collective-permute-done.3.refs_2_), channel_id=1, source_target_pairs={{192,128},{193,129},{194,130},{195,131},{196,132},{197,133},{198,1... | collective-permute-start | bytes 393224 | tf_op jit(solution)/shard_map/ppermute | solution.py:91
  23.1 1.3 %collective-permute-start.12 = (bf16[2,64,512]{2,1,0:T(8,128)(2,1)S(1)}, bf16[2,64,512]{2,1,0:T(8,128)(2,1)S(1)}, u32[]{:S(2)}, u32[]{:S(2)}) collective-permute-start(bf16[2,64,512]{2,1,0:T(8,128)(2,1)S(1)} %shard_map.53.refs_4_), channel_id=1, source_target_pairs={{143,208},{144,207},{159,224},{160,223},{175,240},{176,239},{207,1... | collective-permute-start | bytes 393224 | tf_op jit(solution)/shard_map/ppermute | solution.py:91
  23.2 1.6 %collective-permute-start.10 = (bf16[2,64,512]{2,1,0:T(8,128)(2,1)S(1)}, bf16[2,64,512]{2,1,0:T(8,128)(2,1)S(1)}, u32[]{:S(2)}, u32[]{:S(2)}) collective-permute-start(bf16[2,64,512]{2,1,0:T(8,128)(2,1)S(1)} %shard_map.54.after_ref.refs_4_), channel_id=1, source_target_pairs={{128,192},{129,194},{130,193},{131,196},{132,195},{133,198},{134,1... | collective-permute-start | bytes 393224 | tf_op jit(solution)/shard_map/ppermute | solution.py:91
  23.8 1.3 %collective-permute-start.11 = (bf16[2,64,512]{2,1,0:T(8,128)(2,1)S(1)}, bf16[2,64,512]{2,1,0:T(8,128)(2,1)S(1)}, u32[]{:S(2)}, u32[]{:S(2)}) collective-permute-start(bf16[2,64,512]{2,1,0:T(8,128)(2,1)S(1)} %shard_map.54.after_ref.refs_4_), channel_id=1, source_target_pairs={{128,193},{129,192},{130,195},{131,194},{132,197},{133,196},{134,1... | collective-permute-start | bytes 393224 | tf_op jit(solution)/shard_map/ppermute | solution.py:91
  23.9 1.4 %collective-permute-start.9 = (bf16[2,64,512]{2,1,0:T(8,128)(2,1)S(1)}, bf16[2,64,512]{2,1,0:T(8,128)(2,1)S(1)}, u32[]{:S(2)}, u32[]{:S(2)}) collective-permute-start(bf16[2,64,512]{2,1,0:T(8,128)(2,1)S(1)} %shard_map.54.after_ref.refs_4_), channel_id=1, source_target_pairs={{128,192},{129,193},{130,194},{131,195},{132,196},{133,197},{134,1... | collective-permute-start | bytes 393224 | tf_op jit(solution)/shard_map/ppermute | solution.py:91
  25.3 1.3 %collective-permute-start.13 = (bf16[2,64,512]{2,1,0:T(8,128)(2,1)S(1)}, bf16[2,64,512]{2,1,0:T(8,128)(2,1)S(1)}, u32[]{:S(2)}, u32[]{:S(2)}) collective-permute-start(bf16[2,64,512]{2,1,0:T(8,128)(2,1)S(1)} %shard_map.56.after_ref), channel_id=1, source_target_pairs={{192,128},{193,130},{194,129},{195,132},{196,131},{197,134},{198,1... | collective-permute-start | bytes 393224 | tf_op jit(solution)/shard_map/ppermute | solution.py:91
  25.6 1.3 %collective-permute-start.14 = (bf16[2,64,512]{2,1,0:T(8,128)(2,1)S(1)}, bf16[2,64,512]{2,1,0:T(8,128)(2,1)S(1)}, u32[]{:S(2)}, u32[]{:S(2)}) collective-permute-start(bf16[2,64,512]{2,1,0:T(8,128)(2,1)S(1)} %shard_map.56.after_ref), channel_id=1, source_target_pairs={{192,129},{193,128},{194,131},{195,130},{196,133},{197,132},{198,1... | collective-permute-start | bytes 393224 | tf_op jit(solution)/shard_map/ppermute | solution.py:91
  25.8 1.3 %collective-permute-start.15 = (bf16[2,64,512]{2,1,0:T(8,128)(2,1)S(1)}, bf16[2,64,512]{2,1,0:T(8,128)(2,1)S(1)}, u32[]{:S(2)}, u32[]{:S(2)}) collective-permute-start(bf16[2,64,512]{2,1,0:T(8,128)(2,1)S(1)} %shard_map.56.after_ref), channel_id=1, source_target_pairs={{192,128},{193,129},{194,130},{195,131},{196,132},{197,133},{198,1... | collective-permute-start | bytes 393224 | tf_op jit(solution)/shard_map/ppermute | solution.py:91
  27.2 13.4 %collective-permute-start.16 = (bf16[2,64,512]{2,1,0:T(8,128)(2,1)S(1)}, bf16[2,64,512]{2,1,0:T(8,128)(2,1)S(1)}, u32[]{:S(2)}, u32[]{:S(2)}) collective-permute-start(bf16[2,64,512]{2,1,0:T(8,128)(2,1)S(1)} %shard_map.58.after_ref), channel_id=1, source_target_pairs={{143,79},{144,80},{159,95},{160,96},{175,111},{176,112},{79,15},{8... | collective-permute-start | bytes 393224 | tf_op jit(solution)/shard_map/ppermute | solution.py:91
  31.8 11.8 %collective-permute-start.20 = (bf16[2,64,512]{2,1,0:T(8,128)(2,1)S(1)}, bf16[2,64,512]{2,1,0:T(8,128)(2,1)S(1)}, u32[]{:S(2)}, u32[]{:S(2)}) collective-permute-start(bf16[2,64,512]{2,1,0:T(8,128)(2,1)S(1)} %shard_map.58.after_ref), channel_id=1, source_target_pairs={{142,79},{143,78},{144,81},{145,80},{158,95},{159,94},{160,97},{16... | collective-permute-start | bytes 393224 | tf_op jit(solution)/shard_map/ppermute | solution.py:91
  39.5 4.2 %collective-permute-start.21 = (bf16[2,64,512]{2,1,0:T(8,128)(2,1)S(1)}, bf16[2,64,512]{2,1,0:T(8,128)(2,1)S(1)}, u32[]{:S(2)}, u32[]{:S(2)}) collective-permute-start(bf16[2,64,512]{2,1,0:T(8,128)(2,1)S(1)} %shard_map.58.after_ref), channel_id=1, source_target_pairs={{143,80},{144,79},{159,96},{160,95},{175,112},{176,111},{79,15},{8... | collective-permute-start | bytes 393224 | tf_op jit(solution)/shard_map/ppermute | solution.py:91
  40.6 5.7 %collective-permute-start.17 = (bf16[2,64,512]{2,1,0:T(8,128)(2,1)S(1)}, bf16[2,64,512]{2,1,0:T(8,128)(2,1)S(1)}, u32[]{:S(2)}, u32[]{:S(2)}) collective-permute-start(bf16[2,64,512]{2,1,0:T(8,128)(2,1)S(1)} %collective-permute-done.16.refs_2_), channel_id=1, source_target_pairs={{0,64},{1,66},{2,65},{3,68},{4,67},{5,70},{6,69},{7,72},{8,71},{9,... | collective-permute-start | bytes 393224 | tf_op jit(solution)/shard_map/ppermute | solution.py:91
  43.1 3.1 %collective-permute-start.18 = (bf16[2,64,512]{2,1,0:T(8,128)(2,1)S(1)}, bf16[2,64,512]{2,1,0:T(8,128)(2,1)S(1)}, u32[]{:S(2)}, u32[]{:S(2)}) collective-permute-start(bf16[2,64,512]{2,1,0:T(8,128)(2,1)S(1)} %collective-permute-done.16.refs_2_), channel_id=1, source_target_pairs={{0,65},{1,64},{2,67},{3,66},{4,69},{5,68},{6,71},{7,70},{8,73},{9,... | collective-permute-start | bytes 393224 | tf_op jit(solution)/shard_map/ppermute | solution.py:91
  43.1 3.1 %collective-permute-start.19 = (bf16[2,64,512]{2,1,0:T(8,128)(2,1)S(1)}, bf16[2,64,512]{2,1,0:T(8,128)(2,1)S(1)}, u32[]{:S(2)}, u32[]{:S(2)}) collective-permute-start(bf16[2,64,512]{2,1,0:T(8,128)(2,1)S(1)} %collective-permute-done.16.refs_2_), channel_id=1, source_target_pairs={{0,64},{1,65},{2,66},{3,67},{4,68},{5,69},{6,70},{7,71},{8,72},{9,... | collective-permute-start | bytes 393224 | tf_op jit(solution)/shard_map/ppermute | solution.py:91
  43.7 9.3 %collective-permute-start.23 = (bf16[2,64,512]{2,1,0:T(8,128)(2,1)S(1)}, bf16[2,64,512]{2,1,0:T(8,128)(2,1)S(1)}, u32[]{:S(2)}, u32[]{:S(2)}) collective-permute-start(bf16[2,64,512]{2,1,0:T(8,128)(2,1)S(1)} %shard_map.60.refs_4_), channel_id=1, source_target_pairs={{79,16},{80,15},{95,32},{96,31},{111,48},{112,47},{15,79},{16,80},... | collective-permute-start | bytes 393224 | tf_op jit(solution)/shard_map/ppermute | solution.py:91
  46.3 4.5 %collective-permute-start.24 = (bf16[2,64,512]{2,1,0:T(8,128)(2,1)S(1)}, bf16[2,64,512]{2,1,0:T(8,128)(2,1)S(1)}, u32[]{:S(2)}, u32[]{:S(2)}) collective-permute-start(bf16[2,64,512]{2,1,0:T(8,128)(2,1)S(1)} %shard_map.61), channel_id=1, source_target_pairs={{64,1},{65,0},{66,3},{67,2},{68,5},{69,4},{70,7},{71,6},{72,9},{73... | collective-permute-start | bytes 393224 | tf_op jit(solution)/shard_map/ppermute | solution.py:91
  46.8 4.0 %collective-permute-start.25 = (bf16[2,64,512]{2,1,0:T(8,128)(2,1)S(1)}, bf16[2,64,512]{2,1,0:T(8,128)(2,1)S(1)}, u32[]{:S(2)}, u32[]{:S(2)}) collective-permute-start(bf16[2,64,512]{2,1,0:T(8,128)(2,1)S(1)} %shard_map.61), channel_id=1, source_target_pairs={{64,0},{65,1},{66,2},{67,3},{68,4},{69,5},{70,6},{71,7},{72,8},{73... | collective-permute-start | bytes 393224 | tf_op jit(solution)/shard_map/ppermute | solution.py:91
  46.9 6.1 %collective-permute-start.22 = (bf16[2,64,512]{2,1,0:T(8,128)(2,1)S(1)}, bf16[2,64,512]{2,1,0:T(8,128)(2,1)S(1)}, u32[]{:S(2)}, u32[]{:S(2)}) collective-permute-start(bf16[2,64,512]{2,1,0:T(8,128)(2,1)S(1)} %shard_map.61), channel_id=1, source_target_pairs={{64,0},{65,2},{66,1},{67,4},{68,3},{69,6},{70,5},{71,8},{72,7},{73... | collective-permute-start | bytes 393224 | tf_op jit(solution)/shard_map/ppermute | solution.py:91
